TPU v7x, 1024 devices: a whole 8x8x8 slice. The times are simulated.
1024 devices in a mesh: row: 32 (over y, z_hi), col: 32 (over z_lo, x, core).
Axes of the slice: x: 8, y: 8, z: 8 (z_hi: 4, z_lo: 2; z = z_hi * 2 + z_lo), core: 2. Of those that a mesh axis runs over, the one named last changes fastest.
Arguments:
- tile_values: bfloat16 [32, 32, 96, 128, 128], P('row', 'col'), may hold values from -0.09375 to 0.09375
- tile_rows: int32 [32, 32, 96], P('row', 'col'), may hold values from 0 to 63
- tile_cols: int32 [32, 32, 96], P('row', 'col'), may hold values from 0 to 63
- tile_count: int32 [32, 32], P('row', 'col'), may hold values from 12 to 96, as said below
- vectors: bfloat16 [16, 262144], P(None, ('row', 'col')), may hold values from -6 to 6
Outputs:
- first_image: bfloat16 [16, 262144], P(None, ('row', 'col'))
- second_image: float32 [16, 262144], P(None, ('row', 'col'))
Inputs may be any that keep to these rules, and one draw needn't show every extreme that they name: Each device's live slots are its first tile_count slots; the rest of its slots hold arbitrary data. Some device has all 96 slots live in every draw.
All inputs are finite; a program needn't handle non-finite values.
Results may differ from a plain program's by a relative error of at most 0.011.
Values may be sent and summed in bfloat16 or wider, within the bound.
No kernel may reach another device: no remote copies, remote signals or barrier semaphores. Data moves between devices by JAX's collectives and lax.ppermute only.
A program may use at most 32 MiB of HBM per device.

v0:
```python
import jax
import jax.numpy as jnp
from jax import lax
from jax.sharding import PartitionSpec as P


def scatter_tiles(products, slot_index, is_live, group_count):
    marks = ((slot_index[:, None] == jnp.arange(group_count)[None, :]) & is_live[:, None]).astype(
        jnp.float32
    )
    return jnp.einsum("kni,ns->ksi", products, marks)


def per_device(tile_values, tile_rows, tile_cols, tile_count, vectors):
    tiles = tile_values[0, 0]
    row_index = tile_rows[0, 0]
    col_index = tile_cols[0, 0]
    slot_count = tiles.shape[0]
    tile_width = tiles.shape[-1]
    is_live = jnp.arange(slot_count) < tile_count[0, 0]

    def hamiltonian(vector_slice):
        vec_count, slice_len = vector_slice.shape
        row_segment = lax.all_gather(vector_slice, "col", axis=1, tiled=True)
        row_tiles = row_segment.shape[1] // tile_width
        col_tiles = lax.axis_size("row") * slice_len // tile_width
        picked_rows = row_segment.reshape(vec_count, row_tiles, tile_width)[:, row_index]
        col_segment = lax.all_gather(vector_slice, "row", axis=1, tiled=True)
        picked_cols = col_segment.reshape(vec_count, col_tiles, tile_width)[:, col_index]
        direct = jnp.einsum("nij,knj->kni", tiles, picked_cols, preferred_element_type=jnp.float32)
        mirror = jnp.einsum("nij,kni->knj", tiles, picked_rows, preferred_element_type=jnp.float32)
        direct_terms = scatter_tiles(direct, row_index, is_live, row_tiles).reshape(
            vec_count, row_tiles * tile_width
        )
        mirror_terms = scatter_tiles(mirror, col_index, is_live, col_tiles).reshape(
            vec_count, col_tiles * tile_width
        )
        row_part = lax.psum_scatter(direct_terms, "col", scatter_dimension=1, tiled=True)
        col_part = lax.psum_scatter(mirror_terms, "row", scatter_dimension=1, tiled=True)
        return row_part + col_part

    first_image = hamiltonian(vectors).astype(jnp.bfloat16)
    second_image = hamiltonian(first_image)
    return (first_image, second_image)


def solution(mesh):
    return jax.shard_map(
        per_device,
        mesh=mesh,
        in_specs=(
            P("row", "col", None, None, None),
            P("row", "col", None),
            P("row", "col", None),
            P("row", "col"),
            P(None, ("row", "col")),
        ),
        out_specs=(P(None, ("row", "col")), P(None, ("row", "col"))),
        check_vma=False,
    )
```

profile of v0, /device:TPU:16, one launch (start us, length us, event | category | flops | bytes accessed | tf_op | source)
XLA Modules:
  0.0 806.4 jit_solution(9863492504651411521)
XLA Ops:
  8.0 0.8 fusion.49
  8.8 36.9 %all_gather.13 = bf16[16,8192]{1,0:T(8,128)(2,1)S(1)} all-gather(bf16[16,256]{1,0:T(8,128)(2,1)} %param.9), channel_id=1, replica_groups=mesh['row'=32,'col'=32] {'col'}, dimensions={1}, use_global_device_ids=true | all-gather | bytes 270336 | tf_op jit(solution)/shard_map/all_gather | solution.py:24
  45.7 1.4 gather_fusion.1
  47.1 1.9 fusion.11
  49.3 1.1 copy.41
  50.5 88.4 %all_gather.12 = bf16[16,8192]{1,0:T(8,128)(2,1)S(1)} all-gather(bf16[16,256]{1,0:T(8,128)(2,1)S(1)} %copy-done.2), channel_id=1, replica_groups=mesh['row'=32,'col'=32] {'row'}, dimensions={1}, use_global_device_ids=true | all-gather | bytes 270336 | tf_op jit(solution)/shard_map/all_gather | solution.py:28
  139.0 1.4 gather_fusion
  140.4 2.7 fusion.8
  143.4 1.1 copy.42
  144.6 143.5 %reduce-scatter.7.cloned.1.call-done = f32[16,256]{1,0:T(8,128)} async-done(((f32[16,8192]{1,0:T(8,128)}), f32[16,256]{1,0:T(8,128)}) %reduce-scatter.7.cloned.1.call-update) | async-done | bytes 16400 | tf_op jit(solution)/shard_map/reduce_scatter | solution.py:39
  288.1 122.0 %reduce-scatter.5.cloned.1.call-done = f32[16,256]{1,0:T(8,128)} async-done(((f32[16,8192]{1,0:T(8,128)}), f32[16,256]{1,0:T(8,128)}) %reduce-scatter.5.cloned.1.call-update) | async-done | bytes 16400 | tf_op jit(solution)/shard_map/reduce_scatter | solution.py:38
  410.1 0.7 add_convert_fusion
  410.9 31.1 %all_gather.15 = bf16[16,8192]{1,0:T(8,128)(2,1)S(1)} all-gather(bf16[16,256]{1,0:T(8,128)(2,1)S(1)} %add_convert_fusion), channel_id=1, replica_groups=mesh['row'=32,'col'=32] {'col'}, dimensions={1}, use_global_device_ids=true | all-gather | bytes 270336 | tf_op jit(solution)/shard_map/all_gather | solution.py:24
  442.0 1.4 gather_fusion.3
  443.4 1.9 fusion.17
  445.6 1.1 copy.39
  446.8 78.5 %all_gather.14 = bf16[16,8192]{1,0:T(8,128)(2,1)S(1)} all-gather(bf16[16,256]{1,0:T(8,128)(2,1)S(1)} %add_convert_fusion), channel_id=1, replica_groups=mesh['row'=32,'col'=32] {'row'}, dimensions={1}, use_global_device_ids=true | all-gather | bytes 270336 | tf_op jit(solution)/shard_map/all_gather | solution.py:28
  525.3 1.4 gather_fusion.2
  526.7 2.7 fusion.14
  529.5 0.3 fusion.22
  529.7 1.1 copy.40
  530.8 146.2 %reduce-scatter.11.cloned.1.call-done = f32[16,256]{1,0:T(8,128)} async-done(((f32[16,8192]{1,0:T(8,128)}), f32[16,256]{1,0:T(8,128)}) %reduce-scatter.11.cloned.1.call-update) | async-done | bytes 16400 | tf_op jit(solution)/shard_map/reduce_scatter | solution.py:39
  677.1 121.5 %reduce-scatter.9.cloned.1.call-done = f32[16,256]{1,0:T(8,128)} async-done(((f32[16,8192]{1,0:T(8,128)}), f32[16,256]{1,0:T(8,128)}) %reduce-scatter.9.cloned.1.call-update) | async-done | bytes 16400 | tf_op jit(solution)/shard_map/reduce_scatter | solution.py:38
  798.6 1.3 add.39
  (29 shorter events, 1.2 us)
Async XLA Ops:
  7.2 40.0 %copy-start = (bf16[1,1,96,128,128]{4,3,2,1,0:T(8,128)(2,1)S(1)}, bf16[1,1,96,128,128]{4,3,2,1,0:T(8,128)(2,1)}, u32[]{:S(2)}) copy-start(bf16[1,1,96,128,128]{4,3,2,1,0:T(8,128)(2,1)} %param.5) | copy-start | bytes 9437188
  7.2 41.9 %copy-start.3 = (s32[1,1,96]{2,1,0:T(1,128)S(1)}, s32[1,1,96]{2,1,0:T(1,128)}, u32[]{:S(2)}) copy-start(s32[1,1,96]{2,1,0:T(1,128)} %param.7) | copy-start | bytes 1156
  7.2 280.9 %reduce-scatter.7.cloned.1.call-start = ((), (), s32[]{:S(2)}) async-start(), calls=%async_computation.5 | async-start | bytes 540672 | tf_op jit(solution)/shard_map/reduce_scatter | solution.py:39
  47.1 3.4 copy-start.2
  50.4 92.7 %copy-start.4 = (s32[1,1,96]{2,1,0:T(1,128)S(1)}, s32[1,1,96]{2,1,0:T(1,128)}, u32[]{:S(2)}) copy-start(s32[1,1,96]{2,1,0:T(1,128)} %param.6) | copy-start | bytes 1156
  50.4 359.7 %reduce-scatter.5.cloned.1.call-start = ((), (), s32[]{:S(2)}) async-start(), calls=%async_computation.4 | async-start | bytes 540672 | tf_op jit(solution)/shard_map/reduce_scatter | solution.py:38
  144.5 532.6 %reduce-scatter.11.cloned.1.call-start = ((), (), s32[]{:S(2)}) async-start(), calls=%async_computation.7 | async-start | bytes 540672 | tf_op jit(solution)/shard_map/reduce_scatter | solution.py:39
  410.9 35.9 %copy-start.1 = (bf16[16,256]{1,0:T(8,128)(2,1)}, bf16[16,256]{1,0:T(8,128)(2,1)S(1)}, u32[]{:S(2)}) copy-start(bf16[16,256]{1,0:T(8,128)(2,1)S(1)} %add_convert_fusion) | copy-start | bytes 24580
  446.7 351.9 %reduce-scatter.9.cloned.1.call-start = ((), (), s32[]{:S(2)}) async-start(), calls=%async_computation.6 | async-start | bytes 540672 | tf_op jit(solution)/shard_map/reduce_scatter | solution.py:38
Sparse Core Ops, SparseCore 0:
  50.5 237.4 reduce-scatter.6
  291.8 118.2 reduce-scatter.4
  446.8 230.2 reduce-scatter.10
  680.7 117.8 reduce-scatter.8
where the time goes:
time: 807 us; the launch traced here: 806 us
  waiting for transfers between devices  533 us (66%)
  blocking collectives  235 us (29%)
  between operations  14.6 us (2%)
  matrix products  10.3 us (1%)
  local copies, waits for them, and re-layouts  10.2 us (1%)
    reduce_scatter x2, waiting for transfers between devices, hamiltonian(): lax.psum_scatter(mirror_terms, 'row', scatter_dimension=1, tiled=True)  290 us
    reduce_scatter x2, waiting for transfers between devices, hamiltonian(): lax.psum_scatter(direct_terms, 'col', scatter_dimension=1, tiled=True)  244 us
    all_gather x2, blocking collectives, hamiltonian(): col_segment = lax.all_gather(vector_slice, 'row', axis=1, tiled=True)  167 us
    all_gather x2, blocking collectives, hamiltonian(): row_segment = lax.all_gather(vector_slice, 'col', axis=1, tiled=True)  68 us
  transfers between devices with their start and end apart: 4, of which 4 were waited for; matrix products, arithmetic and copies ran while one was open for 1% of the time, Pallas kernels for 0%

commit v1 on v0

v1 whole, which is shorter than its diff:
```python
import jax
import jax.numpy as jnp
from jax import lax
from jax.experimental import pallas as pl
from jax.experimental.pallas import tpu as pltpu
from jax.sharding import PartitionSpec as P

UNROLL = 16
F32 = jnp.float32
BF16 = jnp.bfloat16


def products_kernel(rows_ref, cols_ref, count_ref, tiles_ref, row_seg_ref, col_seg_ref, direct_ref, mirror_ref, direct_acc, mirror_acc):
    slots = tiles_ref.shape[0]
    row_tiles = row_seg_ref.shape[0]
    col_tiles = col_seg_ref.shape[0]
    direct_acc[...] = jnp.zeros_like(direct_acc)
    mirror_acc[...] = jnp.zeros_like(mirror_acc)
    count = count_ref[0]

    def block(step, _):
        base = step * UNROLL
        results = []
        for u in range(UNROLL):
            n = base + u
            r, c = rows_ref[n], cols_ref[n]
            tile = tiles_ref[n]
            direct = lax.dot_general(col_seg_ref[c], tile, (((1,), (1,)), ((), ())), preferred_element_type=F32)
            mirror = lax.dot_general(row_seg_ref[r], tile, (((1,), (0,)), ((), ())), preferred_element_type=F32)
            live = n < count
            results.append((jnp.where(live, r, row_tiles), jnp.where(live, c, col_tiles), direct, mirror))
        for r, c, direct, mirror in results:
            direct_acc[r] += direct
            mirror_acc[c] += mirror
        return 0

    lax.fori_loop(0, slots // UNROLL, block, 0)
    direct_ref[...] = direct_acc[:row_tiles].astype(BF16)
    mirror_ref[...] = mirror_acc[:col_tiles].astype(BF16)


def products(rows, cols, count, tiles, row_seg, col_seg):
    vmem = pl.BlockSpec(memory_space=pltpu.VMEM)
    smem = pl.BlockSpec(memory_space=pltpu.SMEM)
    spare = lambda seg: pltpu.VMEM((seg.shape[0] + 1,) + seg.shape[1:], F32)
    return pl.pallas_call(
        products_kernel,
        out_shape=(jax.ShapeDtypeStruct(row_seg.shape, BF16), jax.ShapeDtypeStruct(col_seg.shape, BF16)),
        in_specs=[smem, smem, smem, vmem, vmem, vmem],
        out_specs=(vmem, vmem),
        scratch_shapes=[spare(row_seg), spare(col_seg)],
        compiler_params=pltpu.CompilerParams(vmem_limit_bytes=24 * 1024 * 1024),
        name="tile_products",
    )(rows, cols, count, tiles, row_seg, col_seg)


def sum_kernel(row_recv_ref, col_recv_ref, image_ref, *copies_ref):
    parts = row_recv_ref.shape[1]
    width = row_recv_ref.shape[-1]
    for h in range(parts):
        total = jnp.sum(row_recv_ref[:, h].astype(F32), axis=0) + jnp.sum(col_recv_ref[:, h].astype(F32), axis=0)
        value = total.astype(image_ref.dtype)
        image_ref[:, h * width:(h + 1) * width] = value
        if copies_ref:
            copies_ref[0][:, h] = jnp.broadcast_to(value[None], (copies_ref[0].shape[0],) + value.shape)


def sum_parts(row_recv, col_recv, dtype, copies):
    vmem = pl.BlockSpec(memory_space=pltpu.VMEM)
    parts, vec_count, width = row_recv.shape[1:]
    shapes = [jax.ShapeDtypeStruct((vec_count, parts * width), dtype)]
    if copies:
        shapes.append(jax.ShapeDtypeStruct(row_recv.shape, dtype))
    return pl.pallas_call(
        sum_kernel,
        out_shape=tuple(shapes),
        in_specs=[vmem, vmem],
        out_specs=(vmem,) * len(shapes),
        compiler_params=pltpu.CompilerParams(vmem_limit_bytes=16 * 1024 * 1024),
        name="sum_parts",
    )(row_recv, col_recv)


def exchange(parts, axis):
    return lax.all_to_all(parts, axis, 0, 0)


def per_device(tile_values, tile_rows, tile_cols, tile_count, vectors):
    tiles = tile_values[0, 0]
    rows, cols, count = tile_rows[0, 0], tile_cols[0, 0], tile_count[0]
    tile = tiles.shape[-1]
    vec_count, slice_len = vectors.shape
    parts = slice_len // tile
    peers = lax.axis_size("row")

    def image(copies, dtype, again):
        row_seg = exchange(copies, "col").reshape(-1, vec_count, tile)
        col_seg = exchange(copies, "row").reshape(-1, vec_count, tile)
        direct, mirror = products(rows, cols, count, tiles, row_seg, col_seg)
        row_recv = exchange(direct.reshape(copies.shape), "col")
        col_recv = exchange(mirror.reshape(copies.shape), "row")
        return sum_parts(row_recv, col_recv, dtype, again)

    own = vectors.reshape(vec_count, parts, tile).swapaxes(0, 1)
    copies = jnp.broadcast_to(own[None], (peers,) + own.shape)
    first_image, copies = image(copies, BF16, True)
    (second_image,) = image(copies, F32, False)
    return (first_image, second_image)


def solution(mesh):
    return jax.shard_map(
        per_device,
        mesh=mesh,
        in_specs=(
            P("row", "col", None, None, None),
            P("row", "col", None),
            P("row", "col", None),
            P("row", "col"),
            P(None, ("row", "col")),
        ),
        out_specs=(P(None, ("row", "col")), P(None, ("row", "col"))),
        check_vma=False,
    )
```

time: 807 us -> 176 us (0.22)
  waiting for transfers between devices: 533 us -> 12.5 us
  blocking collectives: 235 us -> 139 us
  between operations: 14.6 us -> 1.31 us
  matrix products: 10.3 us -> 0 us
  Pallas kernels: 0 us -> 9.56 us
  starting transfers between devices: 0.16 us -> 8.98 us
    reduce_scatter x4 -> x0, waiting for transfers between devices: 533 us -> none  [the longest x2 290 us: hamiltonian(): lax.psum_scatter(mirror_terms, 'row', scatter_dimension=1, tiled=True)]
    all_gather x4 -> x0, blocking collectives: 235 us -> none  [the longest x2 167 us: hamiltonian(): col_segment = lax.all_gather(vector_slice, 'row', axis=1, tiled=True)]
    all_to_all x0 -> x7, blocking collectives: none -> 139 us  [exchange(): return lax.all_to_all(parts, axis, 0, 0)]
    all_to_all x0 -> x1, waiting for transfers between devices: none -> 12.5 us  [exchange(): return lax.all_to_all(parts, axis, 0, 0)]
    dot_general x8 -> x0, matrix products: 10.3 us -> none  [the longest x2 5.43 us: hamiltonian(): jnp.einsum('nij,knj->kni', tiles, picked_cols, preferred_element_type=jnp...]
    pallas_call x0 -> x4, Pallas kernels: none -> 9.56 us  [the longest x2 8.16 us: products(): pl.pallas_call(products_kernel, out_shape=(jax.ShapeDtypeStruct(row_seg.s...]
    all_to_all x0 -> x1, starting transfers between devices: none -> 8.98 us  [exchange(): return lax.all_to_all(parts, axis, 0, 0)]
  transfers between devices with their start and end apart: 4 -> 1, of which waited for: 4 -> 1; matrix products, arithmetic and copies ran while one was open for 1% -> 0% of each run, Pallas kernels for 0% -> 0%
where the time goes in v1:
time: 176 us
  blocking collectives  139 us (79%)
  waiting for transfers between devices  12.5 us (7%)
  Pallas kernels  9.56 us (5%)
  starting transfers between devices  8.98 us (5%)
  local copies, waits for them, and re-layouts  4.65 us (3%)
    all_to_all x7, blocking collectives, exchange(): return lax.all_to_all(parts, axis, 0, 0)  139 us
    all_to_all x1, waiting for transfers between devices, exchange(): return lax.all_to_all(parts, axis, 0, 0)  12.5 us
    all_to_all x1, starting transfers between devices, exchange(): return lax.all_to_all(parts, axis, 0, 0)  8.98 us
    pallas_call x2, Pallas kernels, products(): pl.pallas_call(products_kernel, out_shape=(jax.ShapeDtypeStruct(row_seg.s...  8.16 us
  transfers between devices with their start and end apart: 1, of which 1 were waited for; matrix products, arithmetic and copies ran while one was open for 0% of the time, Pallas kernels for 0%

profile of v1, /device:TPU:16, one launch (start us, length us, event | category | flops | bytes accessed | tf_op | source)
XLA Modules:
  0.0 175.6 jit_solution(431303359397551981)
XLA Ops:
  0.6 0.7 reshape.32
  1.3 0.7 broadcast_in_dim.2
  2.1 36.5 %all_to_all.40 = bf16[32,2,16,128]{3,2,1,0:T(8,128)(2,1)S(1)} all-to-all(bf16[32,2,16,128]{3,2,1,0:T(8,128)(2,1)} %broadcast_in_dim.2), channel_id=1, replica_groups=mesh['row'=32,'col'=32] {'row'}, dimensions={0} | all-to-all | bytes 524288 | tf_op jit(solution)/shard_map/all_to_all | solution.py:85
  38.6 9.0 %all-to-all-start = ((bf16[32,2,16,128]{3,2,1,0:T(8,128)(2,1)}), bf16[32,2,16,128]{3,2,1,0:T(8,128)(2,1)S(1)}, u32[]{:S(2)}, u32[]{:S(2)}) async-start(bf16[32,2,16,128]{3,2,1,0:T(8,128)(2,1)} %broadcast_in_dim.2), calls=%async_computation | async-start | bytes 524288 | tf_op jit(solution)/shard_map/all_to_all | solution.py:85
  48.2 12.5 %all-to-all-done = bf16[32,2,16,128]{3,2,1,0:T(8,128)(2,1)S(1)} async-done(((bf16[32,2,16,128]{3,2,1,0:T(8,128)(2,1)}), bf16[32,2,16,128]{3,2,1,0:T(8,128)(2,1)S(1)}, u32[]{:S(2)}, u32[]{:S(2)}) %all-to-all-start) | async-done | bytes 262176 | tf_op jit(solution)/shard_map/all_to_all | solution.py:85
  60.7 0.0 copy-start
  60.7 1.9 %copy-done = bf16[1,1,96,128,128]{4,3,2,1,0:T(8,128)(2,1)S(1)} copy-done((bf16[1,1,96,128,128]{4,3,2,1,0:T(8,128)(2,1)S(1)}, bf16[1,1,96,128,128]{4,3,2,1,0:T(8,128)(2,1)}, u32[]{:S(2)}) %copy-start) | copy-done | bytes 3145752
  62.6 0.0 copy-start.1
  62.6 0.7 copy-done.1
  63.3 0.0 copy-start.2
  63.3 0.7 copy-done.2
  63.9 4.1 %tile_products.2 = (bf16[64,16,128]{2,1,0:T(8,128)(2,1)S(1)}, bf16[64,16,128]{2,1,0:T(8,128)(2,1)S(1)}) custom-call(s32[96]{0:T(128)S(1)} %bitcast.25, s32[96]{0:T(128)S(1)} %bitcast.27, s32[1]{0:T(128)} %bitcast.13.count_ref, bf16[96,128,128]{2,1,0:T(8,128)(2,1)S(1)} %bitcast.15, bf16[64,16,128]{2,1,0:T(8,128)(2,1)S(1)} %bitcast.18, ...), custom_call_target="tpu_custom_call" | custom-call | tf_op jit(solution)/shard_map/tile_products/pallas_call | solution.py:46
  68.0 17.6 %all_to_all.41.col_recv_ref = bf16[32,2,16,128]{3,2,1,0:T(8,128)(2,1)S(1)} all-to-all(bf16[32,2,16,128]{3,2,1,0:T(8,128)(2,1)S(1)} %bitcast.24), channel_id=1, replica_groups=mesh['row'=32,'col'=32] {'row'}, dimensions={0} | all-to-all | bytes 524288 | tf_op jit(solution)/shard_map/all_to_all | solution.py:85
  85.6 16.5 %all_to_all.42.row_recv_ref = bf16[32,2,16,128]{3,2,1,0:T(8,128)(2,1)S(1)} all-to-all(bf16[32,2,16,128]{3,2,1,0:T(8,128)(2,1)S(1)} %bitcast.22), channel_id=1, replica_groups=mesh['row'=32,'col'=32] {'col'}, dimensions={0} | all-to-all | bytes 524288 | tf_op jit(solution)/shard_map/all_to_all | solution.py:85
  102.0 0.7 sum_parts.2
  102.7 17.6 %all_to_all.43 = bf16[32,2,16,128]{3,2,1,0:T(8,128)(2,1)S(1)} all-to-all(bf16[32,2,16,128]{3,2,1,0:T(8,128)(2,1)S(1)} %get-tuple-element.11), channel_id=1, replica_groups=mesh['row'=32,'col'=32] {'row'}, dimensions={0} | all-to-all | bytes 524288 | tf_op jit(solution)/shard_map/all_to_all | solution.py:85
  120.3 16.4 %all_to_all.44 = bf16[32,2,16,128]{3,2,1,0:T(8,128)(2,1)S(1)} all-to-all(bf16[32,2,16,128]{3,2,1,0:T(8,128)(2,1)S(1)} %get-tuple-element.11), channel_id=1, replica_groups=mesh['row'=32,'col'=32] {'col'}, dimensions={0} | all-to-all | bytes 524288 | tf_op jit(solution)/shard_map/all_to_all | solution.py:85
  136.8 4.1 %tile_products.3 = (bf16[64,16,128]{2,1,0:T(8,128)(2,1)S(1)}, bf16[64,16,128]{2,1,0:T(8,128)(2,1)S(1)}) custom-call(s32[96]{0:T(128)S(1)} %bitcast.26, s32[96]{0:T(128)S(1)} %bitcast.28, s32[1]{0:T(128)} %bitcast.14.count_ref, bf16[96,128,128]{2,1,0:T(8,128)(2,1)S(1)} %bitcast.16, bf16[64,16,128]{2,1,0:T(8,128)(2,1)S(1)} %bitcast.20, ...), custom_call_target="tpu_custom_call" | custom-call | tf_op jit(solution)/shard_map/tile_products/pallas_call | solution.py:46
  140.9 17.6 %all_to_all.45.col_recv_ref = bf16[32,2,16,128]{3,2,1,0:T(8,128)(2,1)S(1)} all-to-all(bf16[32,2,16,128]{3,2,1,0:T(8,128)(2,1)S(1)} %bitcast.23), channel_id=1, replica_groups=mesh['row'=32,'col'=32] {'row'}, dimensions={0} | all-to-all | bytes 524288 | tf_op jit(solution)/shard_map/all_to_all | solution.py:85
  158.5 16.4 %all_to_all.46.row_recv_ref = bf16[32,2,16,128]{3,2,1,0:T(8,128)(2,1)S(1)} all-to-all(bf16[32,2,16,128]{3,2,1,0:T(8,128)(2,1)S(1)} %bitcast.21), channel_id=1, replica_groups=mesh['row'=32,'col'=32] {'col'}, dimensions={0} | all-to-all | bytes 524288 | tf_op jit(solution)/shard_map/all_to_all | solution.py:85
  174.9 0.7 sum_parts.3
  (1 shorter events, 0.0 us)
Async XLA Ops:
  38.6 22.2 %all-to-all-start = ((bf16[32,2,16,128]{3,2,1,0:T(8,128)(2,1)}), bf16[32,2,16,128]{3,2,1,0:T(8,128)(2,1)S(1)}, u32[]{:S(2)}, u32[]{:S(2)}) async-start(bf16[32,2,16,128]{3,2,1,0:T(8,128)(2,1)} %broadcast_in_dim.2), calls=%async_computation | async-start | bytes 524288 | tf_op jit(solution)/shard_map/all_to_all | solution.py:85
  60.7 1.9 %copy-start = (bf16[1,1,96,128,128]{4,3,2,1,0:T(8,128)(2,1)S(1)}, bf16[1,1,96,128,128]{4,3,2,1,0:T(8,128)(2,1)}, u32[]{:S(2)}) copy-start(bf16[1,1,96,128,128]{4,3,2,1,0:T(8,128)(2,1)} %param.5) | copy-start | bytes 9437188
  62.6 0.7 copy-start.1
  63.3 0.7 copy-start.2

commit v2 on v0

v2 whole, which is shorter than its diff:
```python
import functools

import jax
import jax.numpy as jnp
from jax import lax
from jax.experimental import pallas as pl
from jax.experimental.pallas import tpu as pltpu
from jax.sharding import Mesh
from jax.sharding import PartitionSpec as P

UNROLL = 16
F32 = jnp.float32
BF16 = jnp.bfloat16
ROW = "row"
NEAR = "near"
CORE = "core"
CORES = 2
VMEM = pl.BlockSpec(memory_space=pltpu.VMEM)
SMEM = pl.BlockSpec(memory_space=pltpu.SMEM)


def by_core(tile_row, parts, near):
    part, owner = tile_row % parts, tile_row // parts
    return owner // CORES * parts + part, owner % CORES, near * parts


def mirror_kernel(parts, near, rows_ref, cols_ref, count_ref, tiles_ref, row_seg_ref, out_ref, acc):
    slots, col_tiles = tiles_ref.shape[0], out_ref.shape[0]
    acc[...] = jnp.zeros_like(acc)
    count = count_ref[0]

    def block(step, _):
        results = []
        for u in range(UNROLL):
            n = step * UNROLL + u
            place, core, half = by_core(rows_ref[n], parts, near)
            picked = row_seg_ref[core * half + place]
            product = lax.dot_general(picked, tiles_ref[n], (((1,), (0,)), ((), ())), preferred_element_type=F32)
            results.append((jnp.where(n < count, cols_ref[n], col_tiles), product))
        for c, product in results:
            acc[c] += product
        return 0

    lax.fori_loop(0, slots // UNROLL, block, 0)
    out_ref[...] = acc[:col_tiles].astype(BF16)


def direct_kernel(parts, near, rows_ref, cols_ref, count_ref, core_ref, tiles_ref, col_seg_ref, keep_ref, send_ref, acc):
    slots, half = tiles_ref.shape[0], keep_ref.shape[0]
    acc[...] = jnp.zeros_like(acc)
    count, mine = count_ref[0], core_ref[0]

    def block(step, _):
        results = []
        for u in range(UNROLL):
            n = step * UNROLL + u
            picked = col_seg_ref[cols_ref[n]]
            product = lax.dot_general(picked, tiles_ref[n], (((1,), (1,)), ((), ())), preferred_element_type=F32)
            place, core, _ = by_core(rows_ref[n], parts, near)
            where = jnp.where(core == mine, 0, half) + place
            results.append((jnp.where(n < count, where, 2 * half), product))
        for r, product in results:
            acc[r] += product
        return 0

    lax.fori_loop(0, slots // UNROLL, block, 0)
    keep_ref[...] = acc[:half]
    send_ref[...] = acc[half:2 * half].astype(BF16)


def half_kernel(keep_ref, recv_ref, out_ref):
    out_ref[...] = (keep_ref[...] + recv_ref[...].astype(F32)).astype(BF16)


def sum_kernel(row_recv_ref, near_recv_ref, image_ref, *copies_ref):
    parts, width = row_recv_ref.shape[1], row_recv_ref.shape[-1]
    for h in range(parts):
        total = jnp.sum(row_recv_ref[:, h].astype(F32), axis=0) + jnp.sum(near_recv_ref[:, h].astype(F32), axis=0)
        value = total.astype(image_ref.dtype)
        image_ref[:, h * width:(h + 1) * width] = value
        for ref in copies_ref:
            ref[:, h] = jnp.broadcast_to(value[None], (ref.shape[0],) + value.shape)


def call(kernel, name, in_specs, shapes, scratch, flops, moved, *args):
    return pl.pallas_call(
        kernel,
        out_shape=tuple(jax.ShapeDtypeStruct(s, d) for s, d in shapes),
        in_specs=in_specs,
        out_specs=(VMEM,) * len(shapes),
        scratch_shapes=scratch,
        compiler_params=pltpu.CompilerParams(vmem_limit_bytes=20 * 1024 * 1024),
        cost_estimate=pl.CostEstimate(flops=flops, bytes_accessed=moved, transcendentals=0),
        name=name,
    )(*args)


def per_device(tile_values, tile_rows, tile_cols, tile_count, vectors):
    tiles = tile_values[0, 0]
    rows, cols, count = tile_rows[0, 0], tile_cols[0, 0], tile_count[0]
    slots, tile = tiles.shape[0], tiles.shape[-1]
    vec_count, slice_len = vectors.shape
    parts = slice_len // tile
    peers, near = lax.axis_size(ROW), lax.axis_size(NEAR)
    own_core = lax.axis_index(CORE).astype(jnp.int32).reshape(1)
    piece = (parts, vec_count, tile)
    half = (near * parts, vec_count, tile)
    seg = (peers * parts, vec_count, tile)
    flops, moved = 2 * slots * vec_count * tile * tile, 2 * tiles.size
    acc = lambda n: [pltpu.VMEM((n + 1, vec_count, tile), F32)]

    def image(near_copies, row_copies, dtype, again):
        near_recv = lax.all_to_all(near_copies, NEAR, 0, 0)
        col_seg = lax.all_to_all(row_copies, ROW, 0, 0).reshape(seg)
        row_seg = lax.all_gather(near_recv.reshape(half), CORE, axis=0, tiled=True)
        (mirror,) = call(
            functools.partial(mirror_kernel, parts, near), "mirror_products", [SMEM] * 3 + [VMEM] * 2,
            [(seg, BF16)], acc(seg[0]), flops, moved, rows, cols, count, tiles, row_seg)
        row_recv = lax.all_to_all(mirror.reshape((peers,) + piece), ROW, 0, 0)
        keep, send = call(
            functools.partial(direct_kernel, parts, near), "direct_products", [SMEM] * 4 + [VMEM] * 2,
            [(half, F32), (half, BF16)], acc(CORES * half[0]), flops, moved, rows, cols, count, own_core, tiles, col_seg)
        recv = lax.ppermute(send, CORE, [(0, 1), (1, 0)])
        (chip,) = call(half_kernel, "chip_sum", [VMEM] * 2, [(half, BF16)], [], keep.size, 8 * keep.size, keep, recv)
        near_recv = lax.all_to_all(chip.reshape((near,) + piece), NEAR, 0, 0)
        shapes = [((vec_count, slice_len), dtype)]
        if again:
            shapes += [((near,) + piece, dtype), ((peers,) + piece, dtype)]
        return call(sum_kernel, "sum_parts", [VMEM] * 2, shapes, [], 2 * row_recv.size, 4 * row_recv.size, row_recv, near_recv)

    own = vectors.reshape(vec_count, parts, tile).swapaxes(0, 1)
    spread = lambda n: jnp.broadcast_to(own[None], (n,) + own.shape)
    first_image, near_copies, row_copies = image(spread(near), spread(peers), BF16, True)
    (second_image,) = image(near_copies, row_copies, F32, False)
    return (first_image, second_image)


def solution(mesh):
    rows, cols = mesh.devices.shape
    split = Mesh(mesh.devices.reshape(rows, cols // CORES, CORES), (ROW, NEAR, CORE))
    both = (NEAR, CORE)
    whole = (ROW, NEAR, CORE)
    return jax.shard_map(
        per_device,
        mesh=split,
        in_specs=(P(ROW, both, None, None, None), P(ROW, both, None), P(ROW, both, None), P(ROW, both), P(None, whole)),
        out_specs=(P(None, whole), P(None, whole)),
        check_vma=False,
    )
```

time: 807 us -> 153 us (0.19)
  waiting for transfers between devices: 533 us -> 31.8 us
  blocking collectives: 235 us -> 56.7 us
  starting transfers between devices: 0.16 us -> 41.6 us
  Pallas kernels: 0 us -> 15.8 us
  between operations: 14.6 us -> 1.4 us
  matrix products: 10.3 us -> 0 us
    reduce_scatter x4 -> x0, waiting for transfers between devices: 533 us -> none  [the longest x2 290 us: hamiltonian(): lax.psum_scatter(mirror_terms, 'row', scatter_dimension=1, tiled=True)]
    all_gather x4 -> x2, blocking collectives: 235 us -> 3.99 us  [image(): row_seg = lax.all_gather(near_recv.reshape(half), CORE, axis=0, tiled=True)]
    all_to_all x0 -> x4, blocking collectives: none -> 52.7 us  [the longest x2 29.6 us: image(): near_recv = lax.all_to_all(near_copies, NEAR, 0, 0)]
    all_to_all x0 -> x4, starting transfers between devices: none -> 37.8 us  [the longest x2 25.3 us: image(): col_seg = lax.all_to_all(row_copies, ROW, 0, 0).reshape(seg)]
    all_to_all x0 -> x4, waiting for transfers between devices: none -> 29.1 us  [the longest x2 17 us: image(): row_recv = lax.all_to_all(mirror.reshape((peers,) + piece), ROW, 0, 0)]
    pallas_call x0 -> x8, Pallas kernels: none -> 15.8 us  [call(): pl.pallas_call(kernel, out_shape=tuple((jax.ShapeDtypeStruct(s, d) for s,...]
    dot_general x8 -> x0, matrix products: 10.3 us -> none  [the longest x2 5.43 us: hamiltonian(): jnp.einsum('nij,knj->kni', tiles, picked_cols, preferred_element_type=jnp...]
  transfers between devices with their start and end apart: 4 -> 6, of which waited for: 4 -> 6; matrix products, arithmetic and copies ran while one was open for 1% -> 0% of each run, Pallas kernels for 0% -> 8%
where the time goes in v2:
time: 153 us; the launch traced here: 152 us
  blocking collectives  56.7 us (37%)
  starting transfers between devices  41.6 us (27%)
  waiting for transfers between devices  31.8 us (21%)
  Pallas kernels  15.8 us (10%)
  local copies, waits for them, and re-layouts  4.69 us (3%)
    all_to_all x2, blocking collectives, image(): near_recv = lax.all_to_all(near_copies, NEAR, 0, 0)  29.6 us
    all_to_all x2, starting transfers between devices, image(): col_seg = lax.all_to_all(row_copies, ROW, 0, 0).reshape(seg)  25.3 us
    all_to_all x2, blocking collectives, image(): near_recv = lax.all_to_all(chip.reshape((near,) + piece), NEAR, 0, 0)  23.1 us
    all_to_all x2, waiting for transfers between devices, image(): row_recv = lax.all_to_all(mirror.reshape((peers,) + piece), ROW, 0, 0)  17 us
    pallas_call x8, Pallas kernels, call(): pl.pallas_call(kernel, out_shape=tuple((jax.ShapeDtypeStruct(s, d) for s,...  15.8 us
    all_to_all x2, starting transfers between devices, image(): row_recv = lax.all_to_all(mirror.reshape((peers,) + piece), ROW, 0, 0)  12.5 us
    all_to_all x2, waiting for transfers between devices, image(): col_seg = lax.all_to_all(row_copies, ROW, 0, 0).reshape(seg)  12.1 us
    all_gather x2, blocking collectives, image(): row_seg = lax.all_gather(near_recv.reshape(half), CORE, axis=0, tiled=True)  3.99 us
  transfers between devices with their start and end apart: 6, of which 6 were waited for; matrix products, arithmetic and copies ran while one was open for 0% of the time, Pallas kernels for 8%

profile of v2, /device:TPU:16, one launch (start us, length us, event | category | flops | bytes accessed | tf_op | source)
XLA Modules:
  0.0 152.0 jit_solution(651888336444040394)
XLA Ops:
  1.4 18.0 %all_to_all.40 = bf16[16,2,16,128]{3,2,1,0:T(8,128)(2,1)S(1)} all-to-all(bf16[16,2,16,128]{3,2,1,0:T(8,128)(2,1)S(1)} %broadcast_in_dim.4), channel_id=1, replica_groups=mesh['row'=32,'near'=16,'core'=2] {'near'}, dimensions={0} | all-to-all | bytes 262144 | tf_op jit(solution)/shard_map/all_to_all | solution.py:113
  20.1 21.1 %all-to-all-start.2 = ((bf16[32,2,16,128]{3,2,1,0:T(8,128)(2,1)}), bf16[32,2,16,128]{3,2,1,0:T(8,128)(2,1)S(1)}, u32[]{:S(2)}, u32[]{:S(2)}) async-start(bf16[32,2,16,128]{3,2,1,0:T(8,128)(2,1)} %broadcast_in_dim.5), calls=%async_computation.2 | async-start | bytes 524288 | tf_op jit(solution)/shard_map/all_to_all | solution.py:114
  41.8 2.0 %all_gather.6.row_seg_ref = bf16[64,16,128]{2,1,0:T(8,128)(2,1)S(1)} all-gather(bf16[32,16,128]{2,1,0:T(8,128)(2,1)S(1)} %bitcast.34), channel_id=1, replica_groups=mesh['row'=32,'near'=16,'core'=2] {'core'}, dimensions={0}, use_global_device_ids=true | all-gather | bytes 393216 | tf_op jit(solution)/shard_map/all_gather | solution.py:115
  43.8 1.9 %copy-done = bf16[1,1,96,128,128]{4,3,2,1,0:T(8,128)(2,1)S(1)} copy-done((bf16[1,1,96,128,128]{4,3,2,1,0:T(8,128)(2,1)S(1)}, bf16[1,1,96,128,128]{4,3,2,1,0:T(8,128)(2,1)}, u32[]{:S(2)}) %copy-start) | copy-done | bytes 3145752
  47.0 3.2 %mirror_products.2 = bf16[64,16,128]{2,1,0:T(8,128)(2,1)} custom-call(s32[96]{0:T(128)S(1)} %bitcast.26, s32[96]{0:T(128)S(1)} %bitcast.30, s32[1]{0:T(128)} %bitcast.14.count_ref, bf16[96,128,128]{2,1,0:T(8,128)(2,1)S(1)} %bitcast.18, bf16[64,16,128]{2,1,0:T(8,128)(2,1)S(1)} %all_gather.6.row_seg_ref), custom_call_target="tpu_custom_call" | custom-call | flops 50331648 | bytes 3145728 | tf_op jit(solution)/shard_map/mirror_products/pallas_call | solution.py:86
  50.2 4.1 %all-to-all-done.2 = bf16[32,2,16,128]{3,2,1,0:T(8,128)(2,1)S(1)} async-done(((bf16[32,2,16,128]{3,2,1,0:T(8,128)(2,1)}), bf16[32,2,16,128]{3,2,1,0:T(8,128)(2,1)S(1)}, u32[]{:S(2)}, u32[]{:S(2)}) %all-to-all-start.2) | async-done | bytes 262176 | tf_op jit(solution)/shard_map/all_to_all | solution.py:114
  54.4 8.1 %all-to-all-start.1 = ((bf16[32,2,16,128]{3,2,1,0:T(8,128)(2,1)}), bf16[32,2,16,128]{3,2,1,0:T(8,128)(2,1)}, u32[]{:S(2)}, u32[]{:S(2)}) async-start(bf16[32,2,16,128]{3,2,1,0:T(8,128)(2,1)} %bitcast.6), calls=%async_computation.1 | async-start | bytes 524288 | tf_op jit(solution)/shard_map/all_to_all | solution.py:119
  62.5 3.0 %direct_products.2 = (f32[32,16,128]{2,1,0:T(8,128)S(1)}, bf16[32,16,128]{2,1,0:T(8,128)(2,1)S(1)}) custom-call(s32[96]{0:T(128)S(1)} %bitcast.27, s32[96]{0:T(128)S(1)} %bitcast.31, s32[1]{0:T(128)} %bitcast.15.count_ref, s32[1]{0:T(128)} %bitcast.7.core_ref, bf16[96,128,128]{2,1,0:T(8,128)(2,1)S(1)} %bitcast.19, bf16[64,16,128]{2,1,0:T(8,128)(2,1)S(1)} %bitcast.22), custom_call_target="tpu_custom_call" | custom-call | flops 50331648 | bytes 3145728 | tf_op jit(solution)/shard_map/direct_products/pallas_call | solution.py:86
  65.5 1.9 %collective-permute-start = (bf16[32,16,128]{2,1,0:T(8,128)(2,1)S(1)}, bf16[32,16,128]{2,1,0:T(8,128)(2,1)S(1)}, u32[]{:S(2)}, u32[]{:S(2)}) collective-permute-start(bf16[32,16,128]{2,1,0:T(8,128)(2,1)S(1)} %get-tuple-element.10), channel_id=1, source_target_pairs={{0,1},{1,0},{2,3},{3,2},{4,5},{5,4},{6,7},{7,6},{8,9},{9,8},{10,11... | collective-permute-start | bytes 393224 | tf_op jit(solution)/shard_map/ppermute | solution.py:123
  67.5 1.3 collective-permute-done.recv_ref
  68.8 8.6 %all-to-all-done.1.row_recv_ref = bf16[32,2,16,128]{3,2,1,0:T(8,128)(2,1)} async-done(((bf16[32,2,16,128]{3,2,1,0:T(8,128)(2,1)}), bf16[32,2,16,128]{3,2,1,0:T(8,128)(2,1)}, u32[]{:S(2)}, u32[]{:S(2)}) %all-to-all-start.1) | async-done | bytes 262176 | tf_op jit(solution)/shard_map/all_to_all | solution.py:119
  77.4 11.6 %all_to_all.41.near_recv_ref = bf16[16,2,16,128]{3,2,1,0:T(8,128)(2,1)S(1)} all-to-all(bf16[16,2,16,128]{3,2,1,0:T(8,128)(2,1)S(1)} %bitcast.24), channel_id=1, replica_groups=mesh['row'=32,'near'=16,'core'=2] {'near'}, dimensions={0} | all-to-all | bytes 262144 | tf_op jit(solution)/shard_map/all_to_all | solution.py:125
  89.0 1.6 %sum_parts.2 = (bf16[16,256]{1,0:T(8,128)(2,1)}, bf16[16,2,16,128]{3,2,1,0:T(8,128)(2,1)S(1)}, bf16[32,2,16,128]{3,2,1,0:T(8,128)(2,1)S(1)}) custom-call(bf16[32,2,16,128]{3,2,1,0:T(8,128)(2,1)} %all-to-all-done.1.row_recv_ref, bf16[16,2,16,128]{3,2,1,0:T(8,128)(2,1)S(1)} %all_to_all.41.near_recv_ref), custom_call_target="tpu_custom_call" | custom-call | flops 262144 | bytes 524288 | tf_op jit(solution)/shard_map/sum_parts/pallas_call | solution.py:86
  90.6 11.6 %all_to_all.42 = bf16[16,2,16,128]{3,2,1,0:T(8,128)(2,1)S(1)} all-to-all(bf16[16,2,16,128]{3,2,1,0:T(8,128)(2,1)S(1)} %get-tuple-element.12), channel_id=1, replica_groups=mesh['row'=32,'near'=16,'core'=2] {'near'}, dimensions={0} | all-to-all | bytes 262144 | tf_op jit(solution)/shard_map/all_to_all | solution.py:113
  102.3 4.2 %all-to-all-start.6 = ((bf16[32,2,16,128]{3,2,1,0:T(8,128)(2,1)}), bf16[32,2,16,128]{3,2,1,0:T(8,128)(2,1)S(1)}, u32[]{:S(2)}, u32[]{:S(2)}) async-start(bf16[32,2,16,128]{3,2,1,0:T(8,128)(2,1)} %copy-done.2), calls=%async_computation.6 | async-start | bytes 524288 | tf_op jit(solution)/shard_map/all_to_all | solution.py:114
  106.5 2.0 %all_gather.7.row_seg_ref = bf16[64,16,128]{2,1,0:T(8,128)(2,1)S(1)} all-gather(bf16[32,16,128]{2,1,0:T(8,128)(2,1)S(1)} %bitcast.35), channel_id=1, replica_groups=mesh['row'=32,'near'=16,'core'=2] {'core'}, dimensions={0}, use_global_device_ids=true | all-gather | bytes 393216 | tf_op jit(solution)/shard_map/all_gather | solution.py:115
  108.5 3.2 %mirror_products.3 = bf16[64,16,128]{2,1,0:T(8,128)(2,1)} custom-call(s32[96]{0:T(128)S(1)} %bitcast.28, s32[96]{0:T(128)S(1)} %bitcast.32, s32[1]{0:T(128)} %bitcast.16.count_ref, bf16[96,128,128]{2,1,0:T(8,128)(2,1)S(1)} %bitcast.20, bf16[64,16,128]{2,1,0:T(8,128)(2,1)S(1)} %all_gather.7.row_seg_ref), custom_call_target="tpu_custom_call" | custom-call | flops 50331648 | bytes 3145728 | tf_op jit(solution)/shard_map/mirror_products/pallas_call | solution.py:86
  111.7 8.0 %all-to-all-done.6 = bf16[32,2,16,128]{3,2,1,0:T(8,128)(2,1)S(1)} async-done(((bf16[32,2,16,128]{3,2,1,0:T(8,128)(2,1)}), bf16[32,2,16,128]{3,2,1,0:T(8,128)(2,1)S(1)}, u32[]{:S(2)}, u32[]{:S(2)}) %all-to-all-start.6) | async-done | bytes 262176 | tf_op jit(solution)/shard_map/all_to_all | solution.py:114
  119.7 4.4 %all-to-all-start.5 = ((bf16[32,2,16,128]{3,2,1,0:T(8,128)(2,1)}), bf16[32,2,16,128]{3,2,1,0:T(8,128)(2,1)}, u32[]{:S(2)}, u32[]{:S(2)}) async-start(bf16[32,2,16,128]{3,2,1,0:T(8,128)(2,1)} %bitcast.11), calls=%async_computation.5 | async-start | bytes 524288 | tf_op jit(solution)/shard_map/all_to_all | solution.py:119
  124.1 3.0 %direct_products.3 = (f32[32,16,128]{2,1,0:T(8,128)S(1)}, bf16[32,16,128]{2,1,0:T(8,128)(2,1)S(1)}) custom-call(s32[96]{0:T(128)S(1)} %bitcast.29, s32[96]{0:T(128)S(1)} %bitcast.33, s32[1]{0:T(128)} %bitcast.17.count_ref, s32[1]{0:T(128)} %bitcast.7.core_ref, bf16[96,128,128]{2,1,0:T(8,128)(2,1)S(1)} %bitcast.21, bf16[64,16,128]{2,1,0:T(8,128)(2,1)S(1)} %bitcast.23), custom_call_target="tpu_custom_call" | custom-call | flops 50331648 | bytes 3145728 | tf_op jit(solution)/shard_map/direct_products/pallas_call | solution.py:86
  127.1 1.9 %collective-permute-start.1 = (bf16[32,16,128]{2,1,0:T(8,128)(2,1)S(1)}, bf16[32,16,128]{2,1,0:T(8,128)(2,1)S(1)}, u32[]{:S(2)}, u32[]{:S(2)}) collective-permute-start(bf16[32,16,128]{2,1,0:T(8,128)(2,1)S(1)} %get-tuple-element.15), channel_id=1, source_target_pairs={{0,1},{1,0},{2,3},{3,2},{4,5},{5,4},{6,7},{7,6},{8,9},{9,8},{10,11... | collective-permute-start | bytes 393224 | tf_op jit(solution)/shard_map/ppermute | solution.py:123
  130.3 8.5 %all-to-all-done.5.row_recv_ref = bf16[32,2,16,128]{3,2,1,0:T(8,128)(2,1)} async-done(((bf16[32,2,16,128]{3,2,1,0:T(8,128)(2,1)}), bf16[32,2,16,128]{3,2,1,0:T(8,128)(2,1)}, u32[]{:S(2)}, u32[]{:S(2)}) %all-to-all-start.5) | async-done | bytes 262176 | tf_op jit(solution)/shard_map/all_to_all | solution.py:119
  138.8 11.5 %all_to_all.43.near_recv_ref = bf16[16,2,16,128]{3,2,1,0:T(8,128)(2,1)S(1)} all-to-all(bf16[16,2,16,128]{3,2,1,0:T(8,128)(2,1)S(1)} %bitcast.25), channel_id=1, replica_groups=mesh['row'=32,'near'=16,'core'=2] {'near'}, dimensions={0} | all-to-all | bytes 262144 | tf_op jit(solution)/shard_map/all_to_all | solution.py:125
  150.3 1.6 %sum_parts.3 = f32[16,256]{1,0:T(8,128)} custom-call(bf16[32,2,16,128]{3,2,1,0:T(8,128)(2,1)} %all-to-all-done.5.row_recv_ref, bf16[16,2,16,128]{3,2,1,0:T(8,128)(2,1)S(1)} %all_to_all.43.near_recv_ref), custom_call_target="tpu_custom_call" | custom-call | flops 262144 | bytes 524288 | tf_op jit(solution)/shard_map/sum_parts/pallas_call | solution.py:86
  (20 shorter events, 4.2 us)
Async XLA Ops:
  0.6 61.9 %copy-start.4 = (s32[1,1,96]{2,1,0:T(1,128)S(1)}, s32[1,1,96]{2,1,0:T(1,128)}, u32[]{:S(2)}) copy-start(s32[1,1,96]{2,1,0:T(1,128)} %param.6) | copy-start | bytes 1156
  0.6 61.9 %copy-start.6 = (s32[1,1,96]{2,1,0:T(1,128)S(1)}, s32[1,1,96]{2,1,0:T(1,128)}, u32[]{:S(2)}) copy-start(s32[1,1,96]{2,1,0:T(1,128)} %param.7) | copy-start | bytes 1156
  20.1 34.3 %all-to-all-start.2 = ((bf16[32,2,16,128]{3,2,1,0:T(8,128)(2,1)}), bf16[32,2,16,128]{3,2,1,0:T(8,128)(2,1)S(1)}, u32[]{:S(2)}, u32[]{:S(2)}) async-start(bf16[32,2,16,128]{3,2,1,0:T(8,128)(2,1)} %broadcast_in_dim.5), calls=%async_computation.2 | async-start | bytes 524288 | tf_op jit(solution)/shard_map/all_to_all | solution.py:114
  43.8 1.9 %copy-start = (bf16[1,1,96,128,128]{4,3,2,1,0:T(8,128)(2,1)S(1)}, bf16[1,1,96,128,128]{4,3,2,1,0:T(8,128)(2,1)}, u32[]{:S(2)}) copy-start(bf16[1,1,96,128,128]{4,3,2,1,0:T(8,128)(2,1)} %param.5) | copy-start | bytes 9437188
  45.7 0.7 copy-start.3
  46.4 0.7 copy-start.5
  47.0 15.5 %copy-start.1 = (bf16[1,1,96,128,128]{4,3,2,1,0:T(8,128)(2,1)S(1)}, bf16[1,1,96,128,128]{4,3,2,1,0:T(8,128)(2,1)}, u32[]{:S(2)}) copy-start(bf16[1,1,96,128,128]{4,3,2,1,0:T(8,128)(2,1)} %param.5) | copy-start | bytes 9437188
  54.4 23.0 %all-to-all-start.1 = ((bf16[32,2,16,128]{3,2,1,0:T(8,128)(2,1)}), bf16[32,2,16,128]{3,2,1,0:T(8,128)(2,1)}, u32[]{:S(2)}, u32[]{:S(2)}) async-start(bf16[32,2,16,128]{3,2,1,0:T(8,128)(2,1)} %bitcast.6), calls=%async_computation.1 | async-start | bytes 524288 | tf_op jit(solution)/shard_map/all_to_all | solution.py:119
  65.5 3.2 %collective-permute-start = (bf16[32,16,128]{2,1,0:T(8,128)(2,1)S(1)}, bf16[32,16,128]{2,1,0:T(8,128)(2,1)S(1)}, u32[]{:S(2)}, u32[]{:S(2)}) collective-permute-start(bf16[32,16,128]{2,1,0:T(8,128)(2,1)S(1)} %get-tuple-element.10), channel_id=1, source_target_pairs={{0,1},{1,0},{2,3},{3,2},{4,5},{5,4},{6,7},{7,6},{8,9},{9,8},{10,11... | collective-permute-start | bytes 393224 | tf_op jit(solution)/shard_map/ppermute | solution.py:123
  90.6 11.6 %copy-start.2 = (bf16[32,2,16,128]{3,2,1,0:T(8,128)(2,1)}, bf16[32,2,16,128]{3,2,1,0:T(8,128)(2,1)S(1)}, u32[]{:S(2)}) copy-start(bf16[32,2,16,128]{3,2,1,0:T(8,128)(2,1)S(1)} %get-tuple-element.13) | copy-start | bytes 786436
  102.3 17.4 %all-to-all-start.6 = ((bf16[32,2,16,128]{3,2,1,0:T(8,128)(2,1)}), bf16[32,2,16,128]{3,2,1,0:T(8,128)(2,1)S(1)}, u32[]{:S(2)}, u32[]{:S(2)}) async-start(bf16[32,2,16,128]{3,2,1,0:T(8,128)(2,1)} %copy-done.2), calls=%async_computation.6 | async-start | bytes 524288 | tf_op jit(solution)/shard_map/all_to_all | solution.py:114
  119.7 19.2 %all-to-all-start.5 = ((bf16[32,2,16,128]{3,2,1,0:T(8,128)(2,1)}), bf16[32,2,16,128]{3,2,1,0:T(8,128)(2,1)}, u32[]{:S(2)}, u32[]{:S(2)}) async-start(bf16[32,2,16,128]{3,2,1,0:T(8,128)(2,1)} %bitcast.11), calls=%async_computation.5 | async-start | bytes 524288 | tf_op jit(solution)/shard_map/all_to_all | solution.py:119
  127.1 3.2 %collective-permute-start.1 = (bf16[32,16,128]{2,1,0:T(8,128)(2,1)S(1)}, bf16[32,16,128]{2,1,0:T(8,128)(2,1)S(1)}, u32[]{:S(2)}, u32[]{:S(2)}) collective-permute-start(bf16[32,16,128]{2,1,0:T(8,128)(2,1)S(1)} %get-tuple-element.15), channel_id=1, source_target_pairs={{0,1},{1,0},{2,3},{3,2},{4,5},{5,4},{6,7},{7,6},{8,9},{9,8},{10,11... | collective-permute-start | bytes 393224 | tf_op jit(solution)/shard_map/ppermute | solution.py:123

commit v3 on v2

v3 whole, which is shorter than its diff:
```python
import functools

import jax
import jax.numpy as jnp
from jax import lax
from jax.experimental import pallas as pl
from jax.experimental.pallas import tpu as pltpu
from jax.sharding import Mesh
from jax.sharding import PartitionSpec as P

UNROLL = 16
F32 = jnp.float32
BF16 = jnp.bfloat16
ROW = "row"
ZLO = "z_lo"
LINE = "x"
CORE = "core"
ZLOS, LINES, CORES = 2, 8, 2
QUADS = ZLOS * CORES
VMEM = pl.BlockSpec(memory_space=pltpu.VMEM)
SMEM = pl.BlockSpec(memory_space=pltpu.SMEM)


def position(tile_row, parts):
    part, owner = tile_row & (parts - 1), tile_row >> (parts.bit_length() - 1)
    core, line = owner & (CORES - 1), (owner >> 1) & (LINES - 1)
    return owner >> (CORES * LINES).bit_length() - 1, core, line * parts + part


def mirror_kernel(parts, rows_ref, cols_ref, count_ref, tiles_ref, row_seg_ref, out_ref, acc):
    slots, col_tiles = tiles_ref.shape[0], out_ref.shape[0]
    quad = row_seg_ref.shape[0] // QUADS
    acc[...] = jnp.zeros_like(acc)
    count = count_ref[0]

    def block(step, _):
        results = []
        for u in range(UNROLL):
            n = step * UNROLL + u
            z_lo, core, place = position(rows_ref[n], parts)
            picked = row_seg_ref[(core * ZLOS + z_lo) * quad + place]
            product = lax.dot_general(picked, tiles_ref[n], (((1,), (0,)), ((), ())), preferred_element_type=F32)
            results.append((jnp.where(n < count, cols_ref[n], col_tiles), product))
        for c, product in results:
            acc[c] += product
        return 0

    lax.fori_loop(0, slots // UNROLL, block, 0)
    out_ref[...] = acc[:col_tiles].astype(BF16)


def direct_kernel(parts, rows_ref, cols_ref, count_ref, place_ref, tiles_ref, col_seg_ref, keep_ref, core_ref, z_lo_ref, both_ref, acc):
    slots, quad = tiles_ref.shape[0], keep_ref.shape[0]
    acc[...] = jnp.zeros_like(acc)
    count, my_z_lo, my_core = count_ref[0], place_ref[0], place_ref[1]

    def block(step, _):
        results = []
        for u in range(UNROLL):
            n = step * UNROLL + u
            picked = col_seg_ref[cols_ref[n]]
            product = lax.dot_general(picked, tiles_ref[n], (((1,), (1,)), ((), ())), preferred_element_type=F32)
            z_lo, core, place = position(rows_ref[n], parts)
            where = ((z_lo ^ my_z_lo) * CORES + (core ^ my_core)) * quad + place
            results.append((jnp.where(n < count, where, QUADS * quad), product))
        for r, product in results:
            acc[r] += product
        return 0

    lax.fori_loop(0, slots // UNROLL, block, 0)
    keep_ref[...] = acc[:quad]
    for q, ref in enumerate((core_ref, z_lo_ref, both_ref), 1):
        ref[...] = acc[q * quad:(q + 1) * quad].astype(BF16)


def quad_kernel(keep_ref, core_ref, z_lo_ref, both_ref, out_ref):
    out_ref[...] = (keep_ref[...] + core_ref[...].astype(F32) + (z_lo_ref[...].astype(F32) + both_ref[...].astype(F32))).astype(BF16)


def row_sum_kernel(recv_ref, out_ref):
    for h in range(recv_ref.shape[1]):
        out_ref[h] = jnp.sum(recv_ref[:, h].astype(F32), axis=0)


def image_kernel(row_sum_ref, line_recv_ref, image_ref, *copies_ref):
    parts, width = row_sum_ref.shape[0], row_sum_ref.shape[-1]
    for h in range(parts):
        value = (row_sum_ref[h] + jnp.sum(line_recv_ref[:, h].astype(F32), axis=0)).astype(image_ref.dtype)
        image_ref[:, h * width:(h + 1) * width] = value
        for ref in copies_ref:
            ref[:, h] = jnp.broadcast_to(value[None], (ref.shape[0],) + value.shape)


def call(kernel, name, in_specs, shapes, scratch, flops, moved, *args):
    return pl.pallas_call(
        kernel,
        out_shape=tuple(jax.ShapeDtypeStruct(s, d) for s, d in shapes),
        in_specs=in_specs,
        out_specs=(VMEM,) * len(shapes),
        scratch_shapes=scratch,
        compiler_params=pltpu.CompilerParams(vmem_limit_bytes=12 * 1024 * 1024),
        cost_estimate=pl.CostEstimate(flops=flops, bytes_accessed=moved, transcendentals=0),
        name=name,
    )(*args)


def per_device(tile_values, tile_rows, tile_cols, tile_count, vectors):
    tiles = tile_values[0, 0]
    rows, cols, count = tile_rows[0, 0], tile_cols[0, 0], tile_count[0]
    slots, tile = tiles.shape[0], tiles.shape[-1]
    vec_count, slice_len = vectors.shape
    parts = slice_len // tile
    peers = lax.axis_size(ROW)
    place = jnp.stack([lax.axis_index(ZLO), lax.axis_index(CORE)]).astype(jnp.int32)
    piece = (parts, vec_count, tile)
    quad = (LINES * parts, vec_count, tile)
    seg = (peers * parts, vec_count, tile)
    flops, moved = 2 * slots * vec_count * tile * tile, 2 * tiles.size
    acc = lambda n: [pltpu.VMEM((n + 1, vec_count, tile), F32)]

    def image(line_copies, row_copies, dtype, again):
        line_recv = lax.all_to_all(line_copies, LINE, 0, 0)
        col_seg = lax.all_to_all(row_copies, ROW, 0, 0).reshape(seg)
        two_lines = lax.all_gather(line_recv.reshape(quad), ZLO, axis=0, tiled=True)
        row_seg = lax.all_gather(two_lines, CORE, axis=0, tiled=True)
        (mirror,) = call(
            functools.partial(mirror_kernel, parts), "mirror_products", [SMEM] * 3 + [VMEM] * 2,
            [(seg, BF16)], acc(seg[0]), flops, moved, rows, cols, count, tiles, row_seg)
        row_recv = lax.all_to_all(mirror.reshape((peers,) + piece), ROW, 0, 0)
        keep, to_core, to_z_lo, to_both = call(
            functools.partial(direct_kernel, parts), "direct_products", [SMEM] * 4 + [VMEM] * 2,
            [(quad, F32)] + [(quad, BF16)] * 3, acc(QUADS * quad[0]), flops, moved, rows, cols, count, place, tiles, col_seg)
        recv = [
            lax.ppermute(to_both, (ZLO, CORE), [(i, QUADS - 1 - i) for i in range(QUADS)]),
            lax.ppermute(to_z_lo, ZLO, [(0, 1), (1, 0)]),
            lax.ppermute(to_core, CORE, [(0, 1), (1, 0)]),
        ]
        (line,) = call(quad_kernel, "quad_sum", [VMEM] * 4, [(quad, BF16)], [], 4 * keep.size, 12 * keep.size, keep, *recv)
        line_recv = lax.all_to_all(line.reshape((LINES,) + piece), LINE, 0, 0)
        (row_sum,) = call(row_sum_kernel, "row_sum", [VMEM], [(piece, F32)], [], row_recv.size, 2 * row_recv.size, row_recv)
        shapes = [((vec_count, slice_len), dtype)]
        if again:
            shapes += [((LINES,) + piece, dtype), ((peers,) + piece, dtype)]
        return call(image_kernel, "image", [VMEM] * 2, shapes, [], line_recv.size, 4 * line_recv.size, row_sum, line_recv)

    own = vectors.reshape(vec_count, parts, tile).swapaxes(0, 1)
    spread = lambda n: jnp.broadcast_to(own[None], (n,) + own.shape)
    first_image, line_copies, row_copies = image(spread(LINES), spread(peers), BF16, True)
    (second_image,) = image(line_copies, row_copies, F32, False)
    return (first_image, second_image)


def solution(mesh):
    rows = mesh.devices.shape[0]
    split = Mesh(mesh.devices.reshape(rows, ZLOS, LINES, CORES), (ROW, ZLO, LINE, CORE))
    col = (ZLO, LINE, CORE)
    whole = (ROW,) + col
    return jax.shard_map(
        per_device,
        mesh=split,
        in_specs=(P(ROW, col, None, None, None), P(ROW, col, None), P(ROW, col, None), P(ROW, col), P(None, whole)),
        out_specs=(P(None, whole), P(None, whole)),
        check_vma=False,
    )
```

time: 153 us -> 167 us (1.092)
  starting transfers between devices: 41.6 us -> 75.4 us
  blocking collectives: 56.7 us -> 43.9 us
  waiting for transfers between devices: 31.8 us -> 23.3 us
    all_to_all x4 -> x2, blocking collectives: 52.7 us -> 25.7 us  [image(): line_recv = lax.all_to_all(line_copies, LINE, 0, 0)]
    all_to_all x0 -> x2, waiting for transfers between devices: none -> 14.6 us  [image(): line_recv = lax.all_to_all(line.reshape((LINES,) + piece), LINE, 0, 0)]
    all_gather x2 -> x4, blocking collectives: 3.99 us -> 18.3 us  [the longest x2 14.3 us: image(): two_lines = lax.all_gather(line_recv.reshape(quad), ZLO, axis=0, tiled=True)]
    all_to_all x2, waiting for transfers between devices: 17 us -> 4.83 us  [image(): row_recv = lax.all_to_all(mirror.reshape((peers,) + piece), ROW, 0, 0)]
    ppermute x2 -> x6, starting transfers between devices: 3.84 us -> 15.2 us  [the longest x2 6.06 us: image(): lax.ppermute(to_z_lo, ZLO, [(0, 1), (1, 0)])]
    all_to_all x2, waiting for transfers between devices: 12.1 us -> 1.54 us  [image(): col_seg = lax.all_to_all(row_copies, ROW, 0, 0).reshape(seg)]
    all_to_all x2, starting transfers between devices: 12.5 us -> 21.9 us  [image(): row_recv = lax.all_to_all(mirror.reshape((peers,) + piece), ROW, 0, 0)]
    all_to_all x0 -> x2, starting transfers between devices: none -> 6.7 us  [image(): line_recv = lax.all_to_all(line.reshape((LINES,) + piece), LINE, 0, 0)]
  transfers between devices with their start and end apart: 6 -> 12, of which waited for: 6 -> 7; matrix products, arithmetic and copies ran while one was open for 0% -> 0% of each run, Pallas kernels for 8% -> 9%
where the time goes in v3:
time: 167 us; the launch traced here: 166 us
  starting transfers between devices  75.4 us (45%)
  blocking collectives  43.9 us (26%)
  waiting for transfers between devices  23.3 us (14%)
  Pallas kernels  16.4 us (10%)
  local copies, waits for them, and re-layouts  5.39 us (3%)
    all_to_all x2, starting transfers between devices, image(): col_seg = lax.all_to_all(row_copies, ROW, 0, 0).reshape(seg)  31.6 us
    all_to_all x2, blocking collectives, image(): line_recv = lax.all_to_all(line_copies, LINE, 0, 0)  25.7 us
    all_to_all x2, starting transfers between devices, image(): row_recv = lax.all_to_all(mirror.reshape((peers,) + piece), ROW, 0, 0)  21.9 us
    pallas_call x10, Pallas kernels, call(): pl.pallas_call(kernel, out_shape=tuple((jax.ShapeDtypeStruct(s, d) for s,...  16.4 us
    all_to_all x2, waiting for transfers between devices, image(): line_recv = lax.all_to_all(line.reshape((LINES,) + piece), LINE, 0, 0)  14.6 us
    all_gather x2, blocking collectives, image(): two_lines = lax.all_gather(line_recv.reshape(quad), ZLO, axis=0, tiled=True)  14.3 us
    all_to_all x2, starting transfers between devices, image(): line_recv = lax.all_to_all(line.reshape((LINES,) + piece), LINE, 0, 0)  6.7 us
    ppermute x2, starting transfers between devices, image(): lax.ppermute(to_z_lo, ZLO, [(0, 1), (1, 0)])  6.06 us
  transfers between devices with their start and end apart: 12, of which 7 were waited for; matrix products, arithmetic and copies ran while one was open for 0% of the time, Pallas kernels for 9%

profile of v3, /device:TPU:16, one launch (start us, length us, event | category | flops | bytes accessed | tf_op | source)
XLA Modules:
  0.0 165.8 jit_solution(3047707218766687093)
XLA Ops:
  1.4 14.9 %all_to_all.40 = bf16[8,2,16,128]{3,2,1,0:T(8,128)(2,1)S(1)} all-to-all(bf16[8,2,16,128]{3,2,1,0:T(8,128)(2,1)S(1)} %broadcast_in_dim.4), channel_id=1, replica_groups=mesh['row'=32,'z_lo'=2,'x'=8,'core'=2] {'x'}, dimensions={0} | all-to-all | bytes 131072 | tf_op jit(solution)/shard_map/all_to_all | solution.py:122
  17.1 22.0 %all-to-all-start.2 = ((bf16[32,2,16,128]{3,2,1,0:T(8,128)(2,1)}), bf16[32,2,16,128]{3,2,1,0:T(8,128)(2,1)S(1)}, u32[]{:S(2)}, u32[]{:S(2)}) async-start(bf16[32,2,16,128]{3,2,1,0:T(8,128)(2,1)} %broadcast_in_dim.5), calls=%async_computation.2 | async-start | bytes 524288 | tf_op jit(solution)/shard_map/all_to_all | solution.py:123
  39.7 7.5 %all_gather.12 = bf16[32,16,128]{2,1,0:T(8,128)(2,1)S(1)} all-gather(bf16[16,16,128]{2,1,0:T(8,128)(2,1)S(1)} %bitcast.33), channel_id=1, replica_groups=mesh['row'=32,'z_lo'=2,'x'=8,'core'=2] {'z_lo'}, dimensions={0}, use_global_device_ids=true | all-gather | bytes 196608 | tf_op jit(solution)/shard_map/all_gather | solution.py:124
  47.2 2.0 %all_gather.13.row_seg_ref = bf16[64,16,128]{2,1,0:T(8,128)(2,1)S(1)} all-gather(bf16[32,16,128]{2,1,0:T(8,128)(2,1)S(1)} %all_gather.12), channel_id=1, replica_groups=mesh['row'=32,'z_lo'=2,'x'=8,'core'=2] {'core'}, dimensions={0}, use_global_device_ids=true | all-gather | bytes 393216 | tf_op jit(solution)/shard_map/all_gather | solution.py:125
  52.4 2.9 %mirror_products.2 = bf16[64,16,128]{2,1,0:T(8,128)(2,1)} custom-call(s32[96]{0:T(128)S(1)} %bitcast.25, s32[96]{0:T(128)S(1)} %bitcast.29, s32[1]{0:T(128)} %bitcast.15.count_ref, bf16[96,128,128]{2,1,0:T(8,128)(2,1)S(1)} %bitcast.19, bf16[64,16,128]{2,1,0:T(8,128)(2,1)S(1)} %all_gather.13.row_seg_ref), custom_call_target="tpu_custom_call" | custom-call | flops 50331648 | bytes 3145728 | tf_op jit(solution)/shard_map/mirror_products/pallas_call | solution.py:95
  55.2 11.8 %all-to-all-start.1 = ((bf16[32,2,16,128]{3,2,1,0:T(8,128)(2,1)}), bf16[32,2,16,128]{3,2,1,0:T(8,128)(2,1)}, u32[]{:S(2)}, u32[]{:S(2)}) async-start(bf16[32,2,16,128]{3,2,1,0:T(8,128)(2,1)} %bitcast.6), calls=%async_computation.1 | async-start | bytes 524288 | tf_op jit(solution)/shard_map/all_to_all | solution.py:129
  67.2 3.0 %direct_products.2 = (f32[16,16,128]{2,1,0:T(8,128)S(1)}, bf16[16,16,128]{2,1,0:T(8,128)(2,1)S(1)}, bf16[16,16,128]{2,1,0:T(8,128)(2,1)S(1)}, bf16[16,16,128]{2,1,0:T(8,128)(2,1)S(1)}) custom-call(s32[96]{0:T(128)S(1)} %bitcast.26, s32[96]{0:T(128)S(1)} %bitcast.30, s32[1]{0:T(128)} %bitcast.16.count_ref, s32[2]{0:T(128)S(1)} %pad_add_fusion.place_ref, ...), custom_call_target="tpu_custom_call" | custom-call | flops 50331648 | bytes 3145728 | tf_op jit(solution)/shard_map/direct_products/pallas_call | solution.py:95
  72.1 3.1 %collective-permute-start.1 = (bf16[16,16,128]{2,1,0:T(8,128)(2,1)S(1)}, bf16[16,16,128]{2,1,0:T(8,128)(2,1)S(1)}, u32[]{:S(2)}, u32[]{:S(2)}) collective-permute-start(bf16[16,16,128]{2,1,0:T(8,128)(2,1)S(1)} %get-tuple-element.15), channel_id=1, source_target_pairs={{0,16},{16,0},{1,17},{17,1},{2,18},{18,2},{3,19},{19,3},{4,20},{20... | collective-permute-start | bytes 196616 | tf_op jit(solution)/shard_map/ppermute | solution.py:135
  75.2 2.5 %collective-permute-start.2 = (bf16[16,16,128]{2,1,0:T(8,128)(2,1)S(1)}, bf16[16,16,128]{2,1,0:T(8,128)(2,1)S(1)}, u32[]{:S(2)}, u32[]{:S(2)}) collective-permute-start(bf16[16,16,128]{2,1,0:T(8,128)(2,1)S(1)} %get-tuple-element.16), channel_id=1, source_target_pairs={{0,1},{1,0},{2,3},{3,2},{4,5},{5,4},{6,7},{7,6},{8,9},{9,8},{10,11... | collective-permute-start | bytes 196616 | tf_op jit(solution)/shard_map/ppermute | solution.py:136
  79.4 2.6 %all-to-all-done.1.recv_ref = bf16[32,2,16,128]{3,2,1,0:T(8,128)(2,1)} async-done(((bf16[32,2,16,128]{3,2,1,0:T(8,128)(2,1)}), bf16[32,2,16,128]{3,2,1,0:T(8,128)(2,1)}, u32[]{:S(2)}, u32[]{:S(2)}) %all-to-all-start.1) | async-done | bytes 262176 | tf_op jit(solution)/shard_map/all_to_all | solution.py:129
  82.0 3.3 %all-to-all-start.3 = ((bf16[8,2,16,128]{3,2,1,0:T(8,128)(2,1)}), bf16[8,2,16,128]{3,2,1,0:T(8,128)(2,1)S(1)}, u32[]{:S(2)}, u32[]{:S(2)}) async-start(bf16[8,2,16,128]{3,2,1,0:T(8,128)(2,1)} %bitcast.10), calls=%async_computation.3 | async-start | bytes 131072 | tf_op jit(solution)/shard_map/all_to_all | solution.py:139
  86.4 7.3 %all-to-all-done.3.line_recv_ref = bf16[8,2,16,128]{3,2,1,0:T(8,128)(2,1)S(1)} async-done(((bf16[8,2,16,128]{3,2,1,0:T(8,128)(2,1)}), bf16[8,2,16,128]{3,2,1,0:T(8,128)(2,1)S(1)}, u32[]{:S(2)}, u32[]{:S(2)}) %all-to-all-start.3) | async-done | bytes 65568 | tf_op jit(solution)/shard_map/all_to_all | solution.py:139
  95.0 10.7 %all_to_all.41 = bf16[8,2,16,128]{3,2,1,0:T(8,128)(2,1)S(1)} all-to-all(bf16[8,2,16,128]{3,2,1,0:T(8,128)(2,1)S(1)} %get-tuple-element.18), channel_id=1, replica_groups=mesh['row'=32,'z_lo'=2,'x'=8,'core'=2] {'x'}, dimensions={0} | all-to-all | bytes 131072 | tf_op jit(solution)/shard_map/all_to_all | solution.py:122
  105.8 9.6 %all-to-all-start.6 = ((bf16[32,2,16,128]{3,2,1,0:T(8,128)(2,1)}), bf16[32,2,16,128]{3,2,1,0:T(8,128)(2,1)S(1)}, u32[]{:S(2)}, u32[]{:S(2)}) async-start(bf16[32,2,16,128]{3,2,1,0:T(8,128)(2,1)} %copy-done.2), calls=%async_computation.6 | async-start | bytes 524288 | tf_op jit(solution)/shard_map/all_to_all | solution.py:123
  115.4 6.8 %all_gather.14 = bf16[32,16,128]{2,1,0:T(8,128)(2,1)S(1)} all-gather(bf16[16,16,128]{2,1,0:T(8,128)(2,1)S(1)} %bitcast.34), channel_id=1, replica_groups=mesh['row'=32,'z_lo'=2,'x'=8,'core'=2] {'z_lo'}, dimensions={0}, use_global_device_ids=true | all-gather | bytes 196608 | tf_op jit(solution)/shard_map/all_gather | solution.py:124
  124.2 2.9 %mirror_products.3 = bf16[64,16,128]{2,1,0:T(8,128)(2,1)} custom-call(s32[96]{0:T(128)S(1)} %bitcast.27, s32[96]{0:T(128)S(1)} %bitcast.31, s32[1]{0:T(128)} %bitcast.17.count_ref, bf16[96,128,128]{2,1,0:T(8,128)(2,1)S(1)} %bitcast.21, bf16[64,16,128]{2,1,0:T(8,128)(2,1)S(1)} %all_gather.15.row_seg_ref), custom_call_target="tpu_custom_call" | custom-call | flops 50331648 | bytes 3145728 | tf_op jit(solution)/shard_map/mirror_products/pallas_call | solution.py:95
  128.6 10.1 %all-to-all-start.5 = ((bf16[32,2,16,128]{3,2,1,0:T(8,128)(2,1)}), bf16[32,2,16,128]{3,2,1,0:T(8,128)(2,1)}, u32[]{:S(2)}, u32[]{:S(2)}) async-start(bf16[32,2,16,128]{3,2,1,0:T(8,128)(2,1)} %bitcast.12), calls=%async_computation.5 | async-start | bytes 524288 | tf_op jit(solution)/shard_map/all_to_all | solution.py:129
  138.7 3.0 %direct_products.3 = (f32[16,16,128]{2,1,0:T(8,128)S(1)}, bf16[16,16,128]{2,1,0:T(8,128)(2,1)S(1)}, bf16[16,16,128]{2,1,0:T(8,128)(2,1)S(1)}, bf16[16,16,128]{2,1,0:T(8,128)(2,1)S(1)}) custom-call(s32[96]{0:T(128)S(1)} %bitcast.28, s32[96]{0:T(128)S(1)} %bitcast.32, s32[1]{0:T(128)} %bitcast.18.count_ref, s32[2]{0:T(128)S(1)} %pad_add_fusion.place_ref, ...), custom_call_target="tpu_custom_call" | custom-call | flops 50331648 | bytes 3145728 | tf_op jit(solution)/shard_map/direct_products/pallas_call | solution.py:95
  141.7 2.1 %collective-permute-start.3 = (bf16[16,16,128]{2,1,0:T(8,128)(2,1)S(1)}, bf16[16,16,128]{2,1,0:T(8,128)(2,1)S(1)}, u32[]{:S(2)}, u32[]{:S(2)}) collective-permute-start(bf16[16,16,128]{2,1,0:T(8,128)(2,1)S(1)} %get-tuple-element.21), channel_id=1, source_target_pairs={{0,17},{1,16},{16,1},{17,0},{2,19},{3,18},{18,3},{19,2},{4,21},{5,... | collective-permute-start | bytes 196616 | tf_op jit(solution)/shard_map/ppermute | solution.py:134
  143.8 2.9 %collective-permute-start.4 = (bf16[16,16,128]{2,1,0:T(8,128)(2,1)S(1)}, bf16[16,16,128]{2,1,0:T(8,128)(2,1)S(1)}, u32[]{:S(2)}, u32[]{:S(2)}) collective-permute-start(bf16[16,16,128]{2,1,0:T(8,128)(2,1)S(1)} %get-tuple-element.22), channel_id=1, source_target_pairs={{0,16},{16,0},{1,17},{17,1},{2,18},{18,2},{3,19},{19,3},{4,20},{20... | collective-permute-start | bytes 196616 | tf_op jit(solution)/shard_map/ppermute | solution.py:135
  146.7 2.5 %collective-permute-start.5 = (bf16[16,16,128]{2,1,0:T(8,128)(2,1)S(1)}, bf16[16,16,128]{2,1,0:T(8,128)(2,1)S(1)}, u32[]{:S(2)}, u32[]{:S(2)}) collective-permute-start(bf16[16,16,128]{2,1,0:T(8,128)(2,1)S(1)} %get-tuple-element.23), channel_id=1, source_target_pairs={{0,1},{1,0},{2,3},{3,2},{4,5},{5,4},{6,7},{7,6},{8,9},{9,8},{10,11... | collective-permute-start | bytes 196616 | tf_op jit(solution)/shard_map/ppermute | solution.py:136
  151.4 2.2 %all-to-all-done.5.recv_ref = bf16[32,2,16,128]{3,2,1,0:T(8,128)(2,1)} async-done(((bf16[32,2,16,128]{3,2,1,0:T(8,128)(2,1)}), bf16[32,2,16,128]{3,2,1,0:T(8,128)(2,1)}, u32[]{:S(2)}, u32[]{:S(2)}) %all-to-all-start.5) | async-done | bytes 262176 | tf_op jit(solution)/shard_map/all_to_all | solution.py:129
  153.6 3.3 %all-to-all-start.7 = ((bf16[8,2,16,128]{3,2,1,0:T(8,128)(2,1)}), bf16[8,2,16,128]{3,2,1,0:T(8,128)(2,1)S(1)}, u32[]{:S(2)}, u32[]{:S(2)}) async-start(bf16[8,2,16,128]{3,2,1,0:T(8,128)(2,1)} %bitcast.14), calls=%async_computation.7 | async-start | bytes 131072 | tf_op jit(solution)/shard_map/all_to_all | solution.py:139
  157.9 7.3 %all-to-all-done.7.line_recv_ref = bf16[8,2,16,128]{3,2,1,0:T(8,128)(2,1)S(1)} async-done(((bf16[8,2,16,128]{3,2,1,0:T(8,128)(2,1)}), bf16[8,2,16,128]{3,2,1,0:T(8,128)(2,1)S(1)}, u32[]{:S(2)}, u32[]{:S(2)}) %all-to-all-start.7) | async-done | bytes 65568 | tf_op jit(solution)/shard_map/all_to_all | solution.py:139
  (35 shorter events, 17.8 us)
Async XLA Ops:
  0.6 66.5 %copy-start.6 = (s32[1,1,96]{2,1,0:T(1,128)S(1)}, s32[1,1,96]{2,1,0:T(1,128)}, u32[]{:S(2)}) copy-start(s32[1,1,96]{2,1,0:T(1,128)} %param.7) | copy-start | bytes 1156
  0.6 66.5 %copy-start.4 = (s32[1,1,96]{2,1,0:T(1,128)S(1)}, s32[1,1,96]{2,1,0:T(1,128)}, u32[]{:S(2)}) copy-start(s32[1,1,96]{2,1,0:T(1,128)} %param.6) | copy-start | bytes 1156
  17.1 38.2 %all-to-all-start.2 = ((bf16[32,2,16,128]{3,2,1,0:T(8,128)(2,1)}), bf16[32,2,16,128]{3,2,1,0:T(8,128)(2,1)S(1)}, u32[]{:S(2)}, u32[]{:S(2)}) async-start(bf16[32,2,16,128]{3,2,1,0:T(8,128)(2,1)} %broadcast_in_dim.5), calls=%async_computation.2 | async-start | bytes 524288 | tf_op jit(solution)/shard_map/all_to_all | solution.py:123
  49.2 1.9 %copy-start = (bf16[1,1,96,128,128]{4,3,2,1,0:T(8,128)(2,1)S(1)}, bf16[1,1,96,128,128]{4,3,2,1,0:T(8,128)(2,1)}, u32[]{:S(2)}) copy-start(bf16[1,1,96,128,128]{4,3,2,1,0:T(8,128)(2,1)} %param.5) | copy-start | bytes 9437188
  51.1 0.7 copy-start.3
  51.7 0.7 copy-start.5
  52.4 14.8 %copy-start.1 = (bf16[1,1,96,128,128]{4,3,2,1,0:T(8,128)(2,1)S(1)}, bf16[1,1,96,128,128]{4,3,2,1,0:T(8,128)(2,1)}, u32[]{:S(2)}) copy-start(bf16[1,1,96,128,128]{4,3,2,1,0:T(8,128)(2,1)} %param.5) | copy-start | bytes 9437188
  55.2 26.8 %all-to-all-start.1 = ((bf16[32,2,16,128]{3,2,1,0:T(8,128)(2,1)}), bf16[32,2,16,128]{3,2,1,0:T(8,128)(2,1)}, u32[]{:S(2)}, u32[]{:S(2)}) async-start(bf16[32,2,16,128]{3,2,1,0:T(8,128)(2,1)} %bitcast.6), calls=%async_computation.1 | async-start | bytes 524288 | tf_op jit(solution)/shard_map/all_to_all | solution.py:129
  70.2 7.6 %collective-permute-start = (bf16[16,16,128]{2,1,0:T(8,128)(2,1)S(1)}, bf16[16,16,128]{2,1,0:T(8,128)(2,1)S(1)}, u32[]{:S(2)}, u32[]{:S(2)}) collective-permute-start(bf16[16,16,128]{2,1,0:T(8,128)(2,1)S(1)} %get-tuple-element.14), channel_id=1, source_target_pairs={{0,17},{1,16},{16,1},{17,0},{2,19},{3,18},{18,3},{19,2},{4,21},{5,... | collective-permute-start | bytes 196616 | tf_op jit(solution)/shard_map/ppermute | solution.py:134
  72.1 6.6 %collective-permute-start.1 = (bf16[16,16,128]{2,1,0:T(8,128)(2,1)S(1)}, bf16[16,16,128]{2,1,0:T(8,128)(2,1)S(1)}, u32[]{:S(2)}, u32[]{:S(2)}) collective-permute-start(bf16[16,16,128]{2,1,0:T(8,128)(2,1)S(1)} %get-tuple-element.15), channel_id=1, source_target_pairs={{0,16},{16,0},{1,17},{17,1},{2,18},{18,2},{3,19},{19,3},{4,20},{20... | collective-permute-start | bytes 196616 | tf_op jit(solution)/shard_map/ppermute | solution.py:135
  75.2 3.5 %collective-permute-start.2 = (bf16[16,16,128]{2,1,0:T(8,128)(2,1)S(1)}, bf16[16,16,128]{2,1,0:T(8,128)(2,1)S(1)}, u32[]{:S(2)}, u32[]{:S(2)}) collective-permute-start(bf16[16,16,128]{2,1,0:T(8,128)(2,1)S(1)} %get-tuple-element.16), channel_id=1, source_target_pairs={{0,1},{1,0},{2,3},{3,2},{4,5},{5,4},{6,7},{7,6},{8,9},{9,8},{10,11... | collective-permute-start | bytes 196616 | tf_op jit(solution)/shard_map/ppermute | solution.py:136
  82.0 11.7 %all-to-all-start.3 = ((bf16[8,2,16,128]{3,2,1,0:T(8,128)(2,1)}), bf16[8,2,16,128]{3,2,1,0:T(8,128)(2,1)S(1)}, u32[]{:S(2)}, u32[]{:S(2)}) async-start(bf16[8,2,16,128]{3,2,1,0:T(8,128)(2,1)} %bitcast.10), calls=%async_computation.3 | async-start | bytes 131072 | tf_op jit(solution)/shard_map/all_to_all | solution.py:139
  94.3 0.7 copy-start.2
  105.8 22.8 %all-to-all-start.6 = ((bf16[32,2,16,128]{3,2,1,0:T(8,128)(2,1)}), bf16[32,2,16,128]{3,2,1,0:T(8,128)(2,1)S(1)}, u32[]{:S(2)}, u32[]{:S(2)}) async-start(bf16[32,2,16,128]{3,2,1,0:T(8,128)(2,1)} %copy-done.2), calls=%async_computation.6 | async-start | bytes 524288 | tf_op jit(solution)/shard_map/all_to_all | solution.py:123
  128.6 25.0 %all-to-all-start.5 = ((bf16[32,2,16,128]{3,2,1,0:T(8,128)(2,1)}), bf16[32,2,16,128]{3,2,1,0:T(8,128)(2,1)}, u32[]{:S(2)}, u32[]{:S(2)}) async-start(bf16[32,2,16,128]{3,2,1,0:T(8,128)(2,1)} %bitcast.12), calls=%async_computation.5 | async-start | bytes 524288 | tf_op jit(solution)/shard_map/all_to_all | solution.py:129
  141.7 7.6 %collective-permute-start.3 = (bf16[16,16,128]{2,1,0:T(8,128)(2,1)S(1)}, bf16[16,16,128]{2,1,0:T(8,128)(2,1)S(1)}, u32[]{:S(2)}, u32[]{:S(2)}) collective-permute-start(bf16[16,16,128]{2,1,0:T(8,128)(2,1)S(1)} %get-tuple-element.21), channel_id=1, source_target_pairs={{0,17},{1,16},{16,1},{17,0},{2,19},{3,18},{18,3},{19,2},{4,21},{5,... | collective-permute-start | bytes 196616 | tf_op jit(solution)/shard_map/ppermute | solution.py:134
  143.8 6.9 %collective-permute-start.4 = (bf16[16,16,128]{2,1,0:T(8,128)(2,1)S(1)}, bf16[16,16,128]{2,1,0:T(8,128)(2,1)S(1)}, u32[]{:S(2)}, u32[]{:S(2)}) collective-permute-start(bf16[16,16,128]{2,1,0:T(8,128)(2,1)S(1)} %get-tuple-element.22), channel_id=1, source_target_pairs={{0,16},{16,0},{1,17},{17,1},{2,18},{18,2},{3,19},{19,3},{4,20},{20... | collective-permute-start | bytes 196616 | tf_op jit(solution)/shard_map/ppermute | solution.py:135
  146.7 3.9 %collective-permute-start.5 = (bf16[16,16,128]{2,1,0:T(8,128)(2,1)S(1)}, bf16[16,16,128]{2,1,0:T(8,128)(2,1)S(1)}, u32[]{:S(2)}, u32[]{:S(2)}) collective-permute-start(bf16[16,16,128]{2,1,0:T(8,128)(2,1)S(1)} %get-tuple-element.23), channel_id=1, source_target_pairs={{0,1},{1,0},{2,3},{3,2},{4,5},{5,4},{6,7},{7,6},{8,9},{9,8},{10,11... | collective-permute-start | bytes 196616 | tf_op jit(solution)/shard_map/ppermute | solution.py:136
  153.6 11.7 %all-to-all-start.7 = ((bf16[8,2,16,128]{3,2,1,0:T(8,128)(2,1)}), bf16[8,2,16,128]{3,2,1,0:T(8,128)(2,1)S(1)}, u32[]{:S(2)}, u32[]{:S(2)}) async-start(bf16[8,2,16,128]{3,2,1,0:T(8,128)(2,1)} %bitcast.14), calls=%async_computation.7 | async-start | bytes 131072 | tf_op jit(solution)/shard_map/all_to_all | solution.py:139

commit v4 on v2

v4 whole, which is shorter than its diff:
```python
import functools

import jax
import jax.numpy as jnp
from jax import lax
from jax.experimental import pallas as pl
from jax.experimental.pallas import tpu as pltpu
from jax.sharding import Mesh
from jax.sharding import PartitionSpec as P

UNROLL = 16
F32 = jnp.float32
BF16 = jnp.bfloat16
Y, ZHI, NEAR, CORE = "y", "z_hi", "near", "core"
ROW = (Y, ZHI)
ZHIS, CORES = 4, 2
VMEM = pl.BlockSpec(memory_space=pltpu.VMEM)
SMEM = pl.BlockSpec(memory_space=pltpu.SMEM)


def by_core(tile_row, parts):
    part, owner = tile_row & (parts - 1), tile_row >> (parts.bit_length() - 1)
    return owner & (CORES - 1), (owner >> (CORES.bit_length() - 1)) * parts + part


def mirror_kernel(parts, rows_ref, cols_ref, count_ref, tiles_ref, row_seg_ref, out_ref, acc):
    slots, col_tiles = tiles_ref.shape[0], out_ref.shape[0]
    half = row_seg_ref.shape[0] // CORES
    acc[...] = jnp.zeros_like(acc)
    count = count_ref[0]

    def block(step, _):
        results = []
        for u in range(UNROLL):
            n = step * UNROLL + u
            core, place = by_core(rows_ref[n], parts)
            product = lax.dot_general(row_seg_ref[core * half + place], tiles_ref[n], (((1,), (0,)), ((), ())), preferred_element_type=F32)
            results.append((jnp.where(n < count, cols_ref[n], col_tiles), product))
        for c, product in results:
            acc[c] += product
        return 0

    lax.fori_loop(0, slots // UNROLL, block, 0)
    out_ref[...] = acc[:col_tiles].astype(BF16)


def direct_kernel(parts, rows_ref, cols_ref, count_ref, at_ref, tiles_ref, col_seg_ref, keep_ref, send_ref, acc):
    slots, half = tiles_ref.shape[0], keep_ref.shape[0]
    acc[...] = jnp.zeros_like(acc)
    count, mine = count_ref[0], at_ref[0]

    def block(step, _):
        results = []
        for u in range(UNROLL):
            n = step * UNROLL + u
            product = lax.dot_general(col_seg_ref[cols_ref[n]], tiles_ref[n], (((1,), (1,)), ((), ())), preferred_element_type=F32)
            core, place = by_core(rows_ref[n], parts)
            results.append((jnp.where(n < count, (core ^ mine) * half + place, CORES * half), product))
        for r, product in results:
            acc[r] += product
        return 0

    lax.fori_loop(0, slots // UNROLL, block, 0)
    keep_ref[...] = acc[:half]
    send_ref[...] = acc[half:2 * half].astype(BF16)


def half_kernel(keep_ref, recv_ref, out_ref):
    out_ref[...] = (keep_ref[...] + recv_ref[...].astype(F32)).astype(BF16)


def total(ref, *index):
    return jnp.sum(ref[(slice(None),) + index].astype(F32), axis=0)


def write_image(image_ref, part, value):
    width = value.shape[-1]
    image_ref[:, part * width:(part + 1) * width] = value


def partial_kernel(at_ref, y_recv_ref, near_recv_ref, out_ref, acc):
    z_his, parts = y_recv_ref.shape[1:3]
    for z in range(z_his):
        for h in range(parts):
            acc[z, h] = total(y_recv_ref, z, h)
    for h in range(parts):
        acc[at_ref[1], h] += total(near_recv_ref, h)
    out_ref[...] = jnp.broadcast_to(acc[...].astype(BF16)[None], out_ref.shape)


def middle_kernel(at_ref, z_recv_ref, image_ref, near_ref, y_ref, acc):
    z_his, parts = z_recv_ref.shape[1:3]
    for z in range(z_his):
        for h in range(parts):
            value = total(z_recv_ref, z, h).astype(BF16)
            acc[z, h] = value
            y_ref[:, z, h] = jnp.broadcast_to(value[None], (y_ref.shape[0],) + value.shape)
    for h in range(parts):
        value = acc[at_ref[1], h]
        write_image(image_ref, h, value)
        near_ref[:, h] = jnp.broadcast_to(value[None], (near_ref.shape[0],) + value.shape)


def last_kernel(row_recv_ref, near_recv_ref, image_ref):
    for h in range(row_recv_ref.shape[1]):
        write_image(image_ref, h, total(row_recv_ref, h) + total(near_recv_ref, h))


def call(kernel, name, in_specs, shapes, scratch, flops, moved, *args):
    return pl.pallas_call(
        kernel,
        out_shape=tuple(jax.ShapeDtypeStruct(s, d) for s, d in shapes),
        in_specs=in_specs,
        out_specs=(VMEM,) * len(shapes),
        scratch_shapes=scratch,
        compiler_params=pltpu.CompilerParams(vmem_limit_bytes=12 * 1024 * 1024),
        cost_estimate=pl.CostEstimate(flops=flops, bytes_accessed=moved, transcendentals=0),
        name=name,
    )(*args)


def per_device(tile_values, tile_rows, tile_cols, tile_count, vectors):
    tiles = tile_values[0, 0]
    rows, cols, count = tile_rows[0, 0], tile_cols[0, 0], tile_count[0]
    slots, tile = tiles.shape[0], tiles.shape[-1]
    vec_count, slice_len = vectors.shape
    parts = slice_len // tile
    ys, z_his, near = lax.axis_size(Y), lax.axis_size(ZHI), lax.axis_size(NEAR)
    at = jnp.stack([lax.axis_index(CORE), lax.axis_index(ZHI)]).astype(jnp.int32)
    piece = (parts, vec_count, tile)
    half = (near * parts, vec_count, tile)
    seg = (ys * z_his * parts, vec_count, tile)
    flops, moved = 2 * slots * vec_count * tile * tile, 2 * tiles.size
    acc = lambda n: [pltpu.VMEM((n + 1, vec_count, tile), F32)]

    def application(near_copies, row_copies, gather_axis, sum_axis, sum_shape):
        near_recv = lax.all_to_all(near_copies, NEAR, 0, 0)
        col_seg = lax.all_to_all(row_copies, gather_axis, 0, 0).reshape(seg)
        row_seg = lax.all_gather(near_recv.reshape(half), CORE, axis=0, tiled=True)
        (mirror,) = call(
            functools.partial(mirror_kernel, parts), "mirror_products", [SMEM] * 3 + [VMEM] * 2,
            [(seg, BF16)], acc(seg[0]), flops, moved, rows, cols, count, tiles, row_seg)
        row_recv = lax.all_to_all(mirror.reshape(sum_shape + piece), sum_axis, 0, 0)
        keep, send = call(
            functools.partial(direct_kernel, parts), "direct_products", [SMEM] * 4 + [VMEM] * 2,
            [(half, F32), (half, BF16)], acc(CORES * half[0]), flops, moved, rows, cols, count, at, tiles, col_seg)
        recv = lax.ppermute(send, CORE, [(0, 1), (1, 0)])
        (chip,) = call(half_kernel, "chip_sum", [VMEM] * 2, [(half, BF16)], [], keep.size, 8 * keep.size, keep, recv)
        return row_recv, lax.all_to_all(chip.reshape((near,) + piece), NEAR, 0, 0)

    own = vectors.reshape(vec_count, parts, tile).swapaxes(0, 1)
    spread = lambda n: jnp.broadcast_to(own[None], (n,) + own.shape)
    plane = (z_his,) + piece
    y_recv, near_recv = application(spread(near), spread(ys * z_his), ROW, Y, (ys, z_his))
    (partials,) = call(
        partial_kernel, "partial_sums", [SMEM] + [VMEM] * 2, [((z_his,) + plane, BF16)], [pltpu.VMEM(plane, F32)],
        2 * y_recv.size, 4 * y_recv.size, at, y_recv, near_recv)
    z_recv = lax.all_to_all(partials, ZHI, 0, 0)
    first_image, near_copies, y_copies = call(
        middle_kernel, "middle_image", [SMEM, VMEM],
        [(vectors.shape, BF16), ((near,) + piece, BF16), ((ys,) + plane, BF16)], [pltpu.VMEM(plane, BF16)],
        2 * y_recv.size, 4 * y_recv.size, at, z_recv)
    row_recv, near_recv = application(near_copies, y_copies, Y, ROW, (ys * z_his,))
    (second_image,) = call(
        last_kernel, "last_image", [VMEM] * 2, [(vectors.shape, F32)], [], 2 * row_recv.size, 4 * row_recv.size, row_recv, near_recv)
    return (first_image, second_image)


def solution(mesh):
    rows, cols = mesh.devices.shape
    split = Mesh(mesh.devices.reshape(rows // ZHIS, ZHIS, cols // CORES, CORES), ROW + (NEAR, CORE))
    col = (NEAR, CORE)
    whole = ROW + col
    return jax.shard_map(
        per_device,
        mesh=split,
        in_specs=(P(ROW, col, None, None, None), P(ROW, col, None), P(ROW, col, None), P(ROW, col), P(None, whole)),
        out_specs=(P(None, whole), P(None, whole)),
        check_vma=False,
    )
```

time: 153 us -> 156 us (1.020)
  blocking collectives: 56.7 us -> 72.1 us
  waiting for transfers between devices: 31.8 us -> 21.5 us
  starting transfers between devices: 41.6 us -> 39.4 us
    all_to_all x4 -> x5, blocking collectives: 52.7 us -> 68.2 us  [the longest x2 29.7 us: application(): near_recv = lax.all_to_all(near_copies, NEAR, 0, 0)]
    all_to_all x4, waiting for transfers between devices: 29.1 us -> 18.9 us  [the longest x2 10.2 us: application(): row_recv = lax.all_to_all(mirror.reshape(sum_shape + piece), sum_axis, 0, 0)]
    all_to_all x4, starting transfers between devices: 37.8 us -> 35.6 us  [the longest x2 25.9 us: application(): col_seg = lax.all_to_all(row_copies, gather_axis, 0, 0).reshape(seg)]
    pallas_call x8 -> x9, Pallas kernels: 15.8 us -> 15.7 us  [call(): pl.pallas_call(kernel, out_shape=tuple((jax.ShapeDtypeStruct(s, d) for s,...]
where the time goes in v4:
time: 156 us; the launch traced here: 155 us
  blocking collectives  72.1 us (46%)
  starting transfers between devices  39.4 us (25%)
  waiting for transfers between devices  21.5 us (14%)
  Pallas kernels  15.7 us (10%)
  local copies, waits for them, and re-layouts  4.69 us (3%)
    all_to_all x2, blocking collectives, application(): near_recv = lax.all_to_all(near_copies, NEAR, 0, 0)  29.7 us
    all_to_all x2, starting transfers between devices, application(): col_seg = lax.all_to_all(row_copies, gather_axis, 0, 0).reshape(seg)  25.9 us
    all_to_all x2, blocking collectives, application(): return (row_recv, lax.all_to_all(chip.reshape((near,) + piece), NEAR, 0, 0))  23.2 us
    pallas_call x9, Pallas kernels, call(): pl.pallas_call(kernel, out_shape=tuple((jax.ShapeDtypeStruct(s, d) for s,...  15.7 us
    all_to_all x1, blocking collectives, per_device(): z_recv = lax.all_to_all(partials, ZHI, 0, 0)  15.2 us
    all_to_all x2, waiting for transfers between devices, application(): row_recv = lax.all_to_all(mirror.reshape(sum_shape + piece), sum_axis, 0, 0)  10.2 us
    all_to_all x2, starting transfers between devices, application(): row_recv = lax.all_to_all(mirror.reshape(sum_shape + piece), sum_axis, 0, 0)  9.64 us
    all_to_all x2, waiting for transfers between devices, application(): col_seg = lax.all_to_all(row_copies, gather_axis, 0, 0).reshape(seg)  8.71 us
  transfers between devices with their start and end apart: 6, of which 6 were waited for; matrix products, arithmetic and copies ran while one was open for 0% of the time, Pallas kernels for 8%

profile of v4, /device:TPU:16, one launch (start us, length us, event | category | flops | bytes accessed | tf_op | source)
XLA Modules:
  0.0 154.9 jit_solution(8671991964023305651)
XLA Ops:
  1.4 18.0 %all_to_all.45 = bf16[16,2,16,128]{3,2,1,0:T(8,128)(2,1)S(1)} all-to-all(bf16[16,2,16,128]{3,2,1,0:T(8,128)(2,1)S(1)} %broadcast_in_dim.4), channel_id=1, replica_groups=mesh['y'=8,'z_hi'=4,'near'=16,'core'=2] {'near'}, dimensions={0} | all-to-all | bytes 262144 | tf_op jit(solution)/shard_map/all_to_all | solution.py:137
  20.1 21.1 %all-to-all-start.2 = ((bf16[32,2,16,128]{3,2,1,0:T(8,128)(2,1)}), bf16[32,2,16,128]{3,2,1,0:T(8,128)(2,1)S(1)}, u32[]{:S(2)}, u32[]{:S(2)}) async-start(bf16[32,2,16,128]{3,2,1,0:T(8,128)(2,1)} %broadcast_in_dim.5), calls=%async_computation.2 | async-start | bytes 524288 | tf_op jit(solution)/shard_map/all_to_all | solution.py:138
  41.8 2.0 %all_gather.6.row_seg_ref = bf16[64,16,128]{2,1,0:T(8,128)(2,1)S(1)} all-gather(bf16[32,16,128]{2,1,0:T(8,128)(2,1)S(1)} %bitcast.35), channel_id=1, replica_groups=mesh['y'=8,'z_hi'=4,'near'=16,'core'=2] {'core'}, dimensions={0}, use_global_device_ids=true | all-gather | bytes 393216 | tf_op jit(solution)/shard_map/all_gather | solution.py:139
  43.8 1.9 %copy-done = bf16[1,1,96,128,128]{4,3,2,1,0:T(8,128)(2,1)S(1)} copy-done((bf16[1,1,96,128,128]{4,3,2,1,0:T(8,128)(2,1)S(1)}, bf16[1,1,96,128,128]{4,3,2,1,0:T(8,128)(2,1)}, u32[]{:S(2)}) %copy-start) | copy-done | bytes 3145752
  47.0 2.9 %mirror_products.2 = bf16[64,16,128]{2,1,0:T(8,128)(2,1)} custom-call(s32[96]{0:T(128)S(1)} %bitcast.27, s32[96]{0:T(128)S(1)} %bitcast.31, s32[1]{0:T(128)} %bitcast.15.count_ref, bf16[96,128,128]{2,1,0:T(8,128)(2,1)S(1)} %bitcast.19, bf16[64,16,128]{2,1,0:T(8,128)(2,1)S(1)} %all_gather.6.row_seg_ref), custom_call_target="tpu_custom_call" | custom-call | flops 50331648 | bytes 3145728 | tf_op jit(solution)/shard_map/mirror_products/pallas_call | solution.py:110
  49.9 4.5 %all-to-all-done.2 = bf16[32,2,16,128]{3,2,1,0:T(8,128)(2,1)S(1)} async-done(((bf16[32,2,16,128]{3,2,1,0:T(8,128)(2,1)}), bf16[32,2,16,128]{3,2,1,0:T(8,128)(2,1)S(1)}, u32[]{:S(2)}, u32[]{:S(2)}) %all-to-all-start.2) | async-done | bytes 262176 | tf_op jit(solution)/shard_map/all_to_all | solution.py:138
  54.4 4.0 %all-to-all-start.1 = ((bf16[8,4,2,16,128]{4,3,2,1,0:T(8,128)(2,1)}), bf16[8,4,2,16,128]{4,3,2,1,0:T(8,128)(2,1)}, u32[]{:S(2)}, u32[]{:S(2)}) async-start(bf16[8,4,2,16,128]{4,3,2,1,0:T(8,128)(2,1)} %bitcast.8), calls=%async_computation.1 | async-start | bytes 524288 | tf_op jit(solution)/shard_map/all_to_all | solution.py:143
  58.5 3.0 %direct_products.2 = (f32[32,16,128]{2,1,0:T(8,128)S(1)}, bf16[32,16,128]{2,1,0:T(8,128)(2,1)S(1)}) custom-call(s32[96]{0:T(128)S(1)} %bitcast.28, s32[96]{0:T(128)S(1)} %bitcast.32, s32[1]{0:T(128)} %bitcast.16.count_ref, s32[2]{0:T(128)S(1)} %pad_add_fusion.at_ref, bf16[96,128,128]{2,1,0:T(8,128)(2,1)S(1)} %bitcast.20, bf16[64,16,128]{2,1,0:T(8,128)(2,1)S(1)} %bitcast.23), custom_call_target="tpu_custom_call" | custom-call | flops 50331648 | bytes 3145728 | tf_op jit(solution)/shard_map/direct_products/pallas_call | solution.py:110
  61.5 1.9 %collective-permute-start = (bf16[32,16,128]{2,1,0:T(8,128)(2,1)S(1)}, bf16[32,16,128]{2,1,0:T(8,128)(2,1)S(1)}, u32[]{:S(2)}, u32[]{:S(2)}) collective-permute-start(bf16[32,16,128]{2,1,0:T(8,128)(2,1)S(1)} %get-tuple-element.10), channel_id=1, source_target_pairs={{0,1},{1,0},{2,3},{3,2},{4,5},{5,4},{6,7},{7,6},{8,9},{9,8},{10,11... | collective-permute-start | bytes 393224 | tf_op jit(solution)/shard_map/ppermute | solution.py:147
  63.4 1.3 collective-permute-done.recv_ref
  64.8 3.2 %all-to-all-done.1.y_recv_ref = bf16[8,4,2,16,128]{4,3,2,1,0:T(8,128)(2,1)} async-done(((bf16[8,4,2,16,128]{4,3,2,1,0:T(8,128)(2,1)}), bf16[8,4,2,16,128]{4,3,2,1,0:T(8,128)(2,1)}, u32[]{:S(2)}, u32[]{:S(2)}) %all-to-all-start.1) | async-done | bytes 262176 | tf_op jit(solution)/shard_map/all_to_all | solution.py:143
  67.9 11.6 %all_to_all.46.near_recv_ref = bf16[16,2,16,128]{3,2,1,0:T(8,128)(2,1)S(1)} all-to-all(bf16[16,2,16,128]{3,2,1,0:T(8,128)(2,1)S(1)} %bitcast.25), channel_id=1, replica_groups=mesh['y'=8,'z_hi'=4,'near'=16,'core'=2] {'near'}, dimensions={0} | all-to-all | bytes 262144 | tf_op jit(solution)/shard_map/all_to_all | solution.py:149
  80.6 15.2 %all_to_all.47.z_recv_ref = bf16[4,4,2,16,128]{4,3,2,1,0:T(8,128)(2,1)S(1)} all-to-all(bf16[4,4,2,16,128]{4,3,2,1,0:T(8,128)(2,1)S(1)} %partial_sums.1), channel_id=1, replica_groups=mesh['y'=8,'z_hi'=4,'near'=16,'core'=2] {'z_hi'}, dimensions={0} | all-to-all | bytes 262144 | tf_op jit(solution)/shard_map/all_to_all | solution.py:158
  96.9 11.8 %all_to_all.48 = bf16[16,2,16,128]{3,2,1,0:T(8,128)(2,1)S(1)} all-to-all(bf16[16,2,16,128]{3,2,1,0:T(8,128)(2,1)S(1)} %get-tuple-element.12), channel_id=1, replica_groups=mesh['y'=8,'z_hi'=4,'near'=16,'core'=2] {'near'}, dimensions={0} | all-to-all | bytes 262144 | tf_op jit(solution)/shard_map/all_to_all | solution.py:137
  108.7 4.9 %all-to-all-start.7 = ((bf16[8,4,2,16,128]{4,3,2,1,0:T(8,128)(2,1)}), bf16[8,4,2,16,128]{4,3,2,1,0:T(8,128)(2,1)S(1)}, u32[]{:S(2)}, u32[]{:S(2)}) async-start(bf16[8,4,2,16,128]{4,3,2,1,0:T(8,128)(2,1)} %copy-done.2), calls=%async_computation.7 | async-start | bytes 524288 | tf_op jit(solution)/shard_map/all_to_all | solution.py:138
  113.6 2.0 %all_gather.7.row_seg_ref = bf16[64,16,128]{2,1,0:T(8,128)(2,1)S(1)} all-gather(bf16[32,16,128]{2,1,0:T(8,128)(2,1)S(1)} %bitcast.36), channel_id=1, replica_groups=mesh['y'=8,'z_hi'=4,'near'=16,'core'=2] {'core'}, dimensions={0}, use_global_device_ids=true | all-gather | bytes 393216 | tf_op jit(solution)/shard_map/all_gather | solution.py:139
  115.6 2.9 %mirror_products.3 = bf16[64,16,128]{2,1,0:T(8,128)(2,1)} custom-call(s32[96]{0:T(128)S(1)} %bitcast.29, s32[96]{0:T(128)S(1)} %bitcast.33, s32[1]{0:T(128)} %bitcast.17.count_ref, bf16[96,128,128]{2,1,0:T(8,128)(2,1)S(1)} %bitcast.21, bf16[64,16,128]{2,1,0:T(8,128)(2,1)S(1)} %all_gather.7.row_seg_ref), custom_call_target="tpu_custom_call" | custom-call | flops 50331648 | bytes 3145728 | tf_op jit(solution)/shard_map/mirror_products/pallas_call | solution.py:110
  118.4 4.2 %all-to-all-done.7 = bf16[8,4,2,16,128]{4,3,2,1,0:T(8,128)(2,1)S(1)} async-done(((bf16[8,4,2,16,128]{4,3,2,1,0:T(8,128)(2,1)}), bf16[8,4,2,16,128]{4,3,2,1,0:T(8,128)(2,1)S(1)}, u32[]{:S(2)}, u32[]{:S(2)}) %all-to-all-start.7) | async-done | bytes 262176 | tf_op jit(solution)/shard_map/all_to_all | solution.py:138
  122.6 5.6 %all-to-all-start.6 = ((bf16[32,2,16,128]{3,2,1,0:T(8,128)(2,1)}), bf16[32,2,16,128]{3,2,1,0:T(8,128)(2,1)}, u32[]{:S(2)}, u32[]{:S(2)}) async-start(bf16[32,2,16,128]{3,2,1,0:T(8,128)(2,1)} %bitcast.12), calls=%async_computation.6 | async-start | bytes 524288 | tf_op jit(solution)/shard_map/all_to_all | solution.py:143
  128.3 3.0 %direct_products.3 = (f32[32,16,128]{2,1,0:T(8,128)S(1)}, bf16[32,16,128]{2,1,0:T(8,128)(2,1)S(1)}) custom-call(s32[96]{0:T(128)S(1)} %bitcast.30, s32[96]{0:T(128)S(1)} %bitcast.34, s32[1]{0:T(128)} %bitcast.18.count_ref, s32[2]{0:T(128)S(1)} %pad_add_fusion.at_ref, bf16[96,128,128]{2,1,0:T(8,128)(2,1)S(1)} %bitcast.22, bf16[64,16,128]{2,1,0:T(8,128)(2,1)S(1)} %bitcast.24), custom_call_target="tpu_custom_call" | custom-call | flops 50331648 | bytes 3145728 | tf_op jit(solution)/shard_map/direct_products/pallas_call | solution.py:110
  131.3 1.9 %collective-permute-start.1 = (bf16[32,16,128]{2,1,0:T(8,128)(2,1)S(1)}, bf16[32,16,128]{2,1,0:T(8,128)(2,1)S(1)}, u32[]{:S(2)}, u32[]{:S(2)}) collective-permute-start(bf16[32,16,128]{2,1,0:T(8,128)(2,1)S(1)} %get-tuple-element.15), channel_id=1, source_target_pairs={{0,1},{1,0},{2,3},{3,2},{4,5},{5,4},{6,7},{7,6},{8,9},{9,8},{10,11... | collective-permute-start | bytes 393224 | tf_op jit(solution)/shard_map/ppermute | solution.py:147
  134.6 7.0 %all-to-all-done.6.row_recv_ref = bf16[32,2,16,128]{3,2,1,0:T(8,128)(2,1)} async-done(((bf16[32,2,16,128]{3,2,1,0:T(8,128)(2,1)}), bf16[32,2,16,128]{3,2,1,0:T(8,128)(2,1)}, u32[]{:S(2)}, u32[]{:S(2)}) %all-to-all-start.6) | async-done | bytes 262176 | tf_op jit(solution)/shard_map/all_to_all | solution.py:143
  141.6 11.6 %all_to_all.49.near_recv_ref = bf16[16,2,16,128]{3,2,1,0:T(8,128)(2,1)S(1)} all-to-all(bf16[16,2,16,128]{3,2,1,0:T(8,128)(2,1)S(1)} %bitcast.26), channel_id=1, replica_groups=mesh['y'=8,'z_hi'=4,'near'=16,'core'=2] {'near'}, dimensions={0} | all-to-all | bytes 262144 | tf_op jit(solution)/shard_map/all_to_all | solution.py:149
  153.2 1.6 %last_image.1 = f32[16,256]{1,0:T(8,128)} custom-call(bf16[32,2,16,128]{3,2,1,0:T(8,128)(2,1)} %all-to-all-done.6.row_recv_ref, bf16[16,2,16,128]{3,2,1,0:T(8,128)(2,1)S(1)} %all_to_all.49.near_recv_ref), custom_call_target="tpu_custom_call" | custom-call | flops 262144 | bytes 524288 | tf_op jit(solution)/shard_map/last_image/pallas_call | solution.py:110
  (23 shorter events, 6.5 us)
Async XLA Ops:
  0.6 57.8 %copy-start.4 = (s32[1,1,96]{2,1,0:T(1,128)S(1)}, s32[1,1,96]{2,1,0:T(1,128)}, u32[]{:S(2)}) copy-start(s32[1,1,96]{2,1,0:T(1,128)} %param.6) | copy-start | bytes 1156
  0.6 57.8 %copy-start.6 = (s32[1,1,96]{2,1,0:T(1,128)S(1)}, s32[1,1,96]{2,1,0:T(1,128)}, u32[]{:S(2)}) copy-start(s32[1,1,96]{2,1,0:T(1,128)} %param.7) | copy-start | bytes 1156
  20.1 34.3 %all-to-all-start.2 = ((bf16[32,2,16,128]{3,2,1,0:T(8,128)(2,1)}), bf16[32,2,16,128]{3,2,1,0:T(8,128)(2,1)S(1)}, u32[]{:S(2)}, u32[]{:S(2)}) async-start(bf16[32,2,16,128]{3,2,1,0:T(8,128)(2,1)} %broadcast_in_dim.5), calls=%async_computation.2 | async-start | bytes 524288 | tf_op jit(solution)/shard_map/all_to_all | solution.py:138
  43.8 1.9 %copy-start = (bf16[1,1,96,128,128]{4,3,2,1,0:T(8,128)(2,1)S(1)}, bf16[1,1,96,128,128]{4,3,2,1,0:T(8,128)(2,1)}, u32[]{:S(2)}) copy-start(bf16[1,1,96,128,128]{4,3,2,1,0:T(8,128)(2,1)} %param.5) | copy-start | bytes 9437188
  45.7 0.7 copy-start.3
  46.4 0.7 copy-start.5
  47.0 11.4 %copy-start.1 = (bf16[1,1,96,128,128]{4,3,2,1,0:T(8,128)(2,1)S(1)}, bf16[1,1,96,128,128]{4,3,2,1,0:T(8,128)(2,1)}, u32[]{:S(2)}) copy-start(bf16[1,1,96,128,128]{4,3,2,1,0:T(8,128)(2,1)} %param.5) | copy-start | bytes 9437188
  54.4 13.6 %all-to-all-start.1 = ((bf16[8,4,2,16,128]{4,3,2,1,0:T(8,128)(2,1)}), bf16[8,4,2,16,128]{4,3,2,1,0:T(8,128)(2,1)}, u32[]{:S(2)}, u32[]{:S(2)}) async-start(bf16[8,4,2,16,128]{4,3,2,1,0:T(8,128)(2,1)} %bitcast.8), calls=%async_computation.1 | async-start | bytes 524288 | tf_op jit(solution)/shard_map/all_to_all | solution.py:143
  61.5 3.2 %collective-permute-start = (bf16[32,16,128]{2,1,0:T(8,128)(2,1)S(1)}, bf16[32,16,128]{2,1,0:T(8,128)(2,1)S(1)}, u32[]{:S(2)}, u32[]{:S(2)}) collective-permute-start(bf16[32,16,128]{2,1,0:T(8,128)(2,1)S(1)} %get-tuple-element.10), channel_id=1, source_target_pairs={{0,1},{1,0},{2,3},{3,2},{4,5},{5,4},{6,7},{7,6},{8,9},{9,8},{10,11... | collective-permute-start | bytes 393224 | tf_op jit(solution)/shard_map/ppermute | solution.py:147
  96.9 11.8 %copy-start.2 = (bf16[8,4,2,16,128]{4,3,2,1,0:T(8,128)(2,1)}, bf16[8,4,2,16,128]{4,3,2,1,0:T(8,128)(2,1)S(1)}, u32[]{:S(2)}) copy-start(bf16[8,4,2,16,128]{4,3,2,1,0:T(8,128)(2,1)S(1)} %get-tuple-element.13) | copy-start | bytes 786436
  108.7 13.9 %all-to-all-start.7 = ((bf16[8,4,2,16,128]{4,3,2,1,0:T(8,128)(2,1)}), bf16[8,4,2,16,128]{4,3,2,1,0:T(8,128)(2,1)S(1)}, u32[]{:S(2)}, u32[]{:S(2)}) async-start(bf16[8,4,2,16,128]{4,3,2,1,0:T(8,128)(2,1)} %copy-done.2), calls=%async_computation.7 | async-start | bytes 524288 | tf_op jit(solution)/shard_map/all_to_all | solution.py:138
  122.6 19.0 %all-to-all-start.6 = ((bf16[32,2,16,128]{3,2,1,0:T(8,128)(2,1)}), bf16[32,2,16,128]{3,2,1,0:T(8,128)(2,1)}, u32[]{:S(2)}, u32[]{:S(2)}) async-start(bf16[32,2,16,128]{3,2,1,0:T(8,128)(2,1)} %bitcast.12), calls=%async_computation.6 | async-start | bytes 524288 | tf_op jit(solution)/shard_map/all_to_all | solution.py:143
  131.3 3.2 %collective-permute-start.1 = (bf16[32,16,128]{2,1,0:T(8,128)(2,1)S(1)}, bf16[32,16,128]{2,1,0:T(8,128)(2,1)S(1)}, u32[]{:S(2)}, u32[]{:S(2)}) collective-permute-start(bf16[32,16,128]{2,1,0:T(8,128)(2,1)S(1)} %get-tuple-element.15), channel_id=1, source_target_pairs={{0,1},{1,0},{2,3},{3,2},{4,5},{5,4},{6,7},{7,6},{8,9},{9,8},{10,11... | collective-permute-start | bytes 393224 | tf_op jit(solution)/shard_map/ppermute | solution.py:147

commit v5 on v2

v5 whole, which is shorter than its diff:
```python
import jax
import jax.numpy as jnp
from jax import lax
from jax.experimental import pallas as pl
from jax.experimental.pallas import tpu as pltpu
from jax.sharding import Mesh
from jax.sharding import PartitionSpec as P

UNROLL = 16
F32 = jnp.float32
BF16 = jnp.bfloat16
ROW, NEAR, CORE = "row", "near", "core"
CORES = 2
VMEM = pl.BlockSpec(memory_space=pltpu.VMEM)
SMEM = pl.BlockSpec(memory_space=pltpu.SMEM)


def by_core(tile_row, parts):
    part, owner = tile_row & (parts - 1), tile_row >> (parts.bit_length() - 1)
    return owner & (CORES - 1), (owner >> (CORES.bit_length() - 1)) * parts + part


def start_kernel(vectors_ref, count_ref, own_ref, copies_ref, counts_ref):
    width = own_ref.shape[-1]
    for h in range(own_ref.shape[0]):
        value = vectors_ref[:, h * width:(h + 1) * width]
        own_ref[h] = value
        copies_ref[:, h] = jnp.broadcast_to(value[None], (copies_ref.shape[0],) + value.shape)
    counts_ref[...] = jnp.broadcast_to(count_ref[...], counts_ref.shape)


def mirror_kernel(rows_ref, cols_ref, count_ref, tiles_ref, row_seg_ref, own_ref, packet_ref, acc):
    slots, parts, peers = tiles_ref.shape[0], own_ref.shape[0], packet_ref.shape[0]
    half = row_seg_ref.shape[0] // CORES
    acc[...] = jnp.zeros_like(acc)
    count = count_ref[...]

    def block(step, _):
        results = []
        for u in range(UNROLL):
            n = step * UNROLL + u
            core, place = by_core(rows_ref[n], parts)
            product = lax.dot_general(row_seg_ref[core * half + place], tiles_ref[n], (((1,), (0,)), ((), ())), preferred_element_type=F32)
            results.append((cols_ref[n], jnp.where(n < count, product, 0.0)))
        for c, product in results:
            acc[c] += product
        return 0

    lax.fori_loop(0, slots // UNROLL, block, 0)
    packet_ref[:, :parts] = jnp.broadcast_to(own_ref[...][None], (peers,) + own_ref.shape)
    packet_ref[:, parts:] = acc[...].astype(BF16).reshape((peers,) + own_ref.shape)


def direct_kernel(rows_ref, cols_ref, count_ref, tiles_ref, packet_ref, keep_ref, send_ref, row_sum_ref, acc):
    slots, half, parts = tiles_ref.shape[0], keep_ref.shape[0], row_sum_ref.shape[0]
    acc[...] = jnp.zeros_like(acc)
    count, mine = count_ref[...], lax.axis_index(CORE)

    def block(step, _):
        results = []
        for u in range(UNROLL):
            n = step * UNROLL + u
            col = cols_ref[n]
            picked = packet_ref[col >> (parts.bit_length() - 1), col & (parts - 1)]
            product = lax.dot_general(picked, tiles_ref[n], (((1,), (1,)), ((), ())), preferred_element_type=F32)
            core, place = by_core(rows_ref[n], parts)
            results.append(((core ^ mine) * half + place, jnp.where(n < count, product, 0.0)))
        for r, product in results:
            acc[r] += product
        return 0

    lax.fori_loop(0, slots // UNROLL, block, 0)
    keep_ref[...] = acc[:half]
    send_ref[...] = acc[half:2 * half].astype(BF16)
    for h in range(parts):
        row_sum_ref[h] = jnp.sum(packet_ref[:, parts + h].astype(F32), axis=0)


def half_kernel(keep_ref, recv_ref, out_ref):
    out_ref[...] = (keep_ref[...] + recv_ref[...].astype(F32)).astype(BF16)


def image_kernel(row_sum_ref, near_recv_ref, image_ref, *next_refs):
    parts, width = row_sum_ref.shape[0], row_sum_ref.shape[-1]
    for h in range(parts):
        value = (row_sum_ref[h] + jnp.sum(near_recv_ref[:, h].astype(F32), axis=0)).astype(image_ref.dtype)
        image_ref[:, h * width:(h + 1) * width] = value
        if next_refs:
            own_ref, copies_ref = next_refs
            own_ref[h] = value
            copies_ref[:, h] = jnp.broadcast_to(value[None], (copies_ref.shape[0],) + value.shape)


def call(kernel, name, in_specs, shapes, scratch, flops, moved, *args):
    return pl.pallas_call(
        kernel,
        out_shape=tuple(jax.ShapeDtypeStruct(s, d) for s, d in shapes),
        in_specs=in_specs,
        out_specs=(VMEM,) * len(shapes),
        scratch_shapes=scratch,
        compiler_params=pltpu.CompilerParams(vmem_limit_bytes=12 * 1024 * 1024),
        cost_estimate=pl.CostEstimate(flops=flops, bytes_accessed=moved, transcendentals=0),
        name=name,
    )(*args)


def per_device(tile_values, tile_rows, tile_cols, tile_count, vectors):
    tiles = tile_values[0, 0]
    rows, cols = tile_rows[0, 0], tile_cols[0, 0]
    slots, tile = tiles.shape[0], tiles.shape[-1]
    vec_count, slice_len = vectors.shape
    parts = slice_len // tile
    peers, near = lax.axis_size(ROW), lax.axis_size(NEAR)
    piece = (parts, vec_count, tile)
    half = (near * parts, vec_count, tile)
    packets = (peers, 2 * parts, vec_count, tile)
    flops, moved = 2 * slots * vec_count * tile * tile, 2 * tiles.size
    acc = lambda n: [pltpu.VMEM((n, vec_count, tile), F32)]

    def image(own, near_copies, dtype, again):
        near_recv = lax.all_to_all(near_copies, NEAR, 0, 0)
        row_seg = lax.all_gather(near_recv.reshape(half), CORE, axis=0, tiled=True)
        (packet,) = call(
            mirror_kernel, "mirror_products", [SMEM] * 2 + [VMEM] * 4,
            [(packets, BF16)], acc(peers * parts), flops, moved, rows, cols, count, tiles, row_seg, own)
        packet = lax.all_to_all(packet, ROW, 0, 0)
        keep, send, row_sum = call(
            direct_kernel, "direct_products", [SMEM] * 2 + [VMEM] * 3,
            [(half, F32), (half, BF16), (piece, F32)], acc(CORES * half[0]), flops, moved, rows, cols, count, tiles, packet)
        recv = lax.ppermute(send, CORE, [(0, 1), (1, 0)])
        (chip,) = call(half_kernel, "chip_sum", [VMEM] * 2, [(half, BF16)], [], keep.size, 8 * keep.size, keep, recv)
        near_recv = lax.all_to_all(chip.reshape((near,) + piece), NEAR, 0, 0)
        shapes = [((vec_count, slice_len), dtype)]
        if again:
            shapes += [(piece, dtype), ((near,) + piece, dtype)]
        return call(image_kernel, "image", [VMEM] * 2, shapes, [], near_recv.size, 4 * near_recv.size, row_sum, near_recv)

    own, copies, count = call(
        start_kernel, "start", [VMEM] * 2, [(piece, BF16), ((near,) + piece, BF16), ((vec_count, tile), jnp.int32)],
        [], vectors.size, 40 * vectors.size, vectors, tile_count)
    first_image, own, copies = image(own, copies, BF16, True)
    (second_image,) = image(own, copies, F32, False)
    return (first_image, second_image)


def solution(mesh):
    rows, cols = mesh.devices.shape
    split = Mesh(mesh.devices.reshape(rows, cols // CORES, CORES), (ROW, NEAR, CORE))
    col = (NEAR, CORE)
    whole = (ROW,) + col
    return jax.shard_map(
        per_device,
        mesh=split,
        in_specs=(P(ROW, col, None, None, None), P(ROW, col, None), P(ROW, col, None), P(ROW, col), P(None, whole)),
        out_specs=(P(None, whole), P(None, whole)),
        check_vma=False,
    )
```

time: 153 us -> 146 us (0.954)
  blocking collectives: 56.7 us -> 122 us
  starting transfers between devices: 41.6 us -> 3.84 us
  waiting for transfers between devices: 31.8 us -> 2.63 us
  Pallas kernels: 15.8 us -> 11.7 us
    all_to_all x0 -> x2, blocking collectives: none -> 65.2 us  [image(): packet = lax.all_to_all(packet, ROW, 0, 0)]
    all_to_all x4 -> x0, starting transfers between devices: 37.8 us -> none  [the longest x2 25.3 us: image(): col_seg = lax.all_to_all(row_copies, ROW, 0, 0).reshape(seg)]
    all_to_all x4 -> x0, waiting for transfers between devices: 29.1 us -> none  [the longest x2 17 us: image(): row_recv = lax.all_to_all(mirror.reshape((peers,) + piece), ROW, 0, 0)]
    pallas_call x8 -> x9, Pallas kernels: 15.8 us -> 11.7 us  [call(): pl.pallas_call(kernel, out_shape=tuple((jax.ShapeDtypeStruct(s, d) for s,...]
  transfers between devices with their start and end apart: 6 -> 2, of which waited for: 6 -> 2; matrix products, arithmetic and copies ran while one was open for 0% -> 0% of each run, Pallas kernels for 8% -> 0%
where the time goes in v5:
time: 146 us
  blocking collectives  122 us (84%)
  Pallas kernels  11.7 us (8%)
  local copies, waits for them, and re-layouts  3.91 us (3%)
  starting transfers between devices  3.84 us (3%)
  waiting for transfers between devices  2.63 us (2%)
    all_to_all x2, blocking collectives, image(): packet = lax.all_to_all(packet, ROW, 0, 0)  65.2 us
    all_to_all x2, blocking collectives, image(): near_recv = lax.all_to_all(near_copies, NEAR, 0, 0)  29.7 us
    all_to_all x2, blocking collectives, image(): near_recv = lax.all_to_all(chip.reshape((near,) + piece), NEAR, 0, 0)  23.5 us
    pallas_call x9, Pallas kernels, call(): pl.pallas_call(kernel, out_shape=tuple((jax.ShapeDtypeStruct(s, d) for s,...  11.7 us
    all_gather x2, blocking collectives, image(): row_seg = lax.all_gather(near_recv.reshape(half), CORE, axis=0, tiled=True)  3.96 us
    unnamed x14, local copies, waits for them, and re-layouts  3.91 us
    ppermute x2, starting transfers between devices, image(): recv = lax.ppermute(send, CORE, [(0, 1), (1, 0)])  3.84 us
  transfers between devices with their start and end apart: 2, of which 2 were waited for; matrix products, arithmetic and copies ran while one was open for 0% of the time, Pallas kernels for 0%

profile of v5, /device:TPU:16, one launch (start us, length us, event | category | flops | bytes accessed | tf_op | source)
XLA Modules:
  0.0 145.9 jit_solution(4458190936411406046)
XLA Ops:
  0.6 0.0 copy-start.5
  1.3 0.7 copy-done.6
  2.0 0.1 start.1
  2.1 17.9 %all_to_all.30 = bf16[16,2,16,128]{3,2,1,0:T(8,128)(2,1)S(1)} all-to-all(bf16[16,2,16,128]{3,2,1,0:T(8,128)(2,1)S(1)} %get-tuple-element.15), channel_id=1, replica_groups=mesh['row'=32,'near'=16,'core'=2] {'near'}, dimensions={0} | all-to-all | bytes 262144 | tf_op jit(solution)/shard_map/all_to_all | solution.py:121
  20.0 2.0 %all_gather.6.row_seg_ref = bf16[64,16,128]{2,1,0:T(8,128)(2,1)S(1)} all-gather(bf16[32,16,128]{2,1,0:T(8,128)(2,1)S(1)} %bitcast.21), channel_id=1, replica_groups=mesh['row'=32,'near'=16,'core'=2] {'core'}, dimensions={0}, use_global_device_ids=true | all-gather | bytes 393216 | tf_op jit(solution)/shard_map/all_gather | solution.py:122
  22.0 1.9 %copy-done = bf16[1,1,96,128,128]{4,3,2,1,0:T(8,128)(2,1)S(1)} copy-done((bf16[1,1,96,128,128]{4,3,2,1,0:T(8,128)(2,1)S(1)}, bf16[1,1,96,128,128]{4,3,2,1,0:T(8,128)(2,1)}, u32[]{:S(2)}) %copy-start) | copy-done | bytes 3145752
  23.9 0.7 copy-done.2
  24.6 0.7 copy-done.4
  25.2 2.2 %mirror_products.2 = bf16[32,4,16,128]{3,2,1,0:T(8,128)(2,1)S(1)} custom-call(s32[96]{0:T(128)S(1)} %bitcast.13, s32[96]{0:T(128)S(1)} %bitcast.17, s32[16,128]{1,0:T(8,128)S(1)} %get-tuple-element.14.count_ref, bf16[96,128,128]{2,1,0:T(8,128)(2,1)S(1)} %bitcast.7, bf16[64,16,128]{2,1,0:T(8,128)(2,1)S(1)} %all_gather.6.row_seg_ref, ...), custom_call_target="tpu_custom_call" | custom-call | flops 50331648 | bytes 3145728 | tf_op jit(solution)/shard_map/mirror_products/pallas_call | solution.py:95
  27.4 40.6 %all_to_all.31.packet_ref = bf16[32,4,16,128]{3,2,1,0:T(8,128)(2,1)S(1)} all-to-all(bf16[32,4,16,128]{3,2,1,0:T(8,128)(2,1)S(1)} %mirror_products.2), channel_id=1, replica_groups=mesh['row'=32,'near'=16,'core'=2] {'row'}, dimensions={0} | all-to-all | bytes 1048576 | tf_op jit(solution)/shard_map/all_to_all | solution.py:126
  68.0 3.0 %direct_products.2 = (f32[32,16,128]{2,1,0:T(8,128)S(1)}, bf16[32,16,128]{2,1,0:T(8,128)(2,1)S(1)}, f32[2,16,128]{2,1,0:T(8,128)S(1)}) custom-call(s32[96]{0:T(128)S(1)} %bitcast.14, s32[96]{0:T(128)S(1)} %bitcast.18, s32[16,128]{1,0:T(8,128)S(1)} %get-tuple-element.14.count_ref, bf16[96,128,128]{2,1,0:T(8,128)(2,1)S(1)} %bitcast.8, ...), custom_call_target="tpu_custom_call" | custom-call | flops 50331648 | bytes 3145728 | tf_op jit(solution)/shard_map/direct_products/pallas_call | solution.py:95
  71.0 1.9 %collective-permute-start = (bf16[32,16,128]{2,1,0:T(8,128)(2,1)S(1)}, bf16[32,16,128]{2,1,0:T(8,128)(2,1)S(1)}, u32[]{:S(2)}, u32[]{:S(2)}) collective-permute-start(bf16[32,16,128]{2,1,0:T(8,128)(2,1)S(1)} %get-tuple-element.19), channel_id=1, source_target_pairs={{0,1},{1,0},{2,3},{3,2},{4,5},{5,4},{6,7},{7,6},{8,9},{9,8},{10,11... | collective-permute-start | bytes 393224 | tf_op jit(solution)/shard_map/ppermute | solution.py:130
  72.9 1.3 collective-permute-done.recv_ref
  74.3 11.8 %all_to_all.32.near_recv_ref = bf16[16,2,16,128]{3,2,1,0:T(8,128)(2,1)S(1)} all-to-all(bf16[16,2,16,128]{3,2,1,0:T(8,128)(2,1)S(1)} %bitcast.11), channel_id=1, replica_groups=mesh['row'=32,'near'=16,'core'=2] {'near'}, dimensions={0} | all-to-all | bytes 262144 | tf_op jit(solution)/shard_map/all_to_all | solution.py:132
  86.0 0.6 image.2
  86.7 11.8 %all_to_all.33 = bf16[16,2,16,128]{3,2,1,0:T(8,128)(2,1)S(1)} all-to-all(bf16[16,2,16,128]{3,2,1,0:T(8,128)(2,1)S(1)} %get-tuple-element.21), channel_id=1, replica_groups=mesh['row'=32,'near'=16,'core'=2] {'near'}, dimensions={0} | all-to-all | bytes 262144 | tf_op jit(solution)/shard_map/all_to_all | solution.py:121
  98.4 2.0 %all_gather.7.row_seg_ref = bf16[64,16,128]{2,1,0:T(8,128)(2,1)S(1)} all-gather(bf16[32,16,128]{2,1,0:T(8,128)(2,1)S(1)} %bitcast.22), channel_id=1, replica_groups=mesh['row'=32,'near'=16,'core'=2] {'core'}, dimensions={0}, use_global_device_ids=true | all-gather | bytes 393216 | tf_op jit(solution)/shard_map/all_gather | solution.py:122
  100.4 2.2 %mirror_products.3 = bf16[32,4,16,128]{3,2,1,0:T(8,128)(2,1)S(1)} custom-call(s32[96]{0:T(128)S(1)} %bitcast.15, s32[96]{0:T(128)S(1)} %bitcast.19, s32[16,128]{1,0:T(8,128)S(1)} %get-tuple-element.14.count_ref, bf16[96,128,128]{2,1,0:T(8,128)(2,1)S(1)} %bitcast.9, bf16[64,16,128]{2,1,0:T(8,128)(2,1)S(1)} %all_gather.7.row_seg_ref, ...), custom_call_target="tpu_custom_call" | custom-call | flops 50331648 | bytes 3145728 | tf_op jit(solution)/shard_map/mirror_products/pallas_call | solution.py:95
  102.6 24.6 %all_to_all.34.packet_ref = bf16[32,4,16,128]{3,2,1,0:T(8,128)(2,1)S(1)} all-to-all(bf16[32,4,16,128]{3,2,1,0:T(8,128)(2,1)S(1)} %mirror_products.3), channel_id=1, replica_groups=mesh['row'=32,'near'=16,'core'=2] {'row'}, dimensions={0} | all-to-all | bytes 1048576 | tf_op jit(solution)/shard_map/all_to_all | solution.py:126
  127.2 3.0 %direct_products.3 = (f32[32,16,128]{2,1,0:T(8,128)S(1)}, bf16[32,16,128]{2,1,0:T(8,128)(2,1)S(1)}, f32[2,16,128]{2,1,0:T(8,128)S(1)}) custom-call(s32[96]{0:T(128)S(1)} %bitcast.16, s32[96]{0:T(128)S(1)} %bitcast.20, s32[16,128]{1,0:T(8,128)S(1)} %get-tuple-element.14.count_ref, bf16[96,128,128]{2,1,0:T(8,128)(2,1)S(1)} %bitcast.10, ...), custom_call_target="tpu_custom_call" | custom-call | flops 50331648 | bytes 3145728 | tf_op jit(solution)/shard_map/direct_products/pallas_call | solution.py:95
  130.2 1.9 %collective-permute-start.1 = (bf16[32,16,128]{2,1,0:T(8,128)(2,1)S(1)}, bf16[32,16,128]{2,1,0:T(8,128)(2,1)S(1)}, u32[]{:S(2)}, u32[]{:S(2)}) collective-permute-start(bf16[32,16,128]{2,1,0:T(8,128)(2,1)S(1)} %get-tuple-element.25), channel_id=1, source_target_pairs={{0,1},{1,0},{2,3},{3,2},{4,5},{5,4},{6,7},{7,6},{8,9},{9,8},{10,11... | collective-permute-start | bytes 393224 | tf_op jit(solution)/shard_map/ppermute | solution.py:130
  132.1 1.3 collective-permute-done.1.recv_ref
  133.5 11.8 %all_to_all.35.near_recv_ref = bf16[16,2,16,128]{3,2,1,0:T(8,128)(2,1)S(1)} all-to-all(bf16[16,2,16,128]{3,2,1,0:T(8,128)(2,1)S(1)} %bitcast.12), channel_id=1, replica_groups=mesh['row'=32,'near'=16,'core'=2] {'near'}, dimensions={0} | all-to-all | bytes 262144 | tf_op jit(solution)/shard_map/all_to_all | solution.py:132
  145.3 0.6 image.3
  (11 shorter events, 0.1 us)
Async XLA Ops:
  0.6 67.3 %copy-start.5 = (s32[1,1,96]{2,1,0:T(1,128)S(1)}, s32[1,1,96]{2,1,0:T(1,128)}, u32[]{:S(2)}) copy-start(s32[1,1,96]{2,1,0:T(1,128)} %param.7) | copy-start | bytes 1156
  0.6 67.3 %copy-start.3 = (s32[1,1,96]{2,1,0:T(1,128)S(1)}, s32[1,1,96]{2,1,0:T(1,128)}, u32[]{:S(2)}) copy-start(s32[1,1,96]{2,1,0:T(1,128)} %param.6) | copy-start | bytes 1156
  1.3 0.7 copy-start.6
  22.0 1.9 %copy-start = (bf16[1,1,96,128,128]{4,3,2,1,0:T(8,128)(2,1)S(1)}, bf16[1,1,96,128,128]{4,3,2,1,0:T(8,128)(2,1)}, u32[]{:S(2)}) copy-start(bf16[1,1,96,128,128]{4,3,2,1,0:T(8,128)(2,1)} %param.5) | copy-start | bytes 9437188
  23.9 0.7 copy-start.2
  24.6 0.7 copy-start.4
  25.2 42.8 %copy-start.1 = (bf16[1,1,96,128,128]{4,3,2,1,0:T(8,128)(2,1)S(1)}, bf16[1,1,96,128,128]{4,3,2,1,0:T(8,128)(2,1)}, u32[]{:S(2)}) copy-start(bf16[1,1,96,128,128]{4,3,2,1,0:T(8,128)(2,1)} %param.5) | copy-start | bytes 9437188
  71.0 3.2 %collective-permute-start = (bf16[32,16,128]{2,1,0:T(8,128)(2,1)S(1)}, bf16[32,16,128]{2,1,0:T(8,128)(2,1)S(1)}, u32[]{:S(2)}, u32[]{:S(2)}) collective-permute-start(bf16[32,16,128]{2,1,0:T(8,128)(2,1)S(1)} %get-tuple-element.19), channel_id=1, source_target_pairs={{0,1},{1,0},{2,3},{3,2},{4,5},{5,4},{6,7},{7,6},{8,9},{9,8},{10,11... | collective-permute-start | bytes 393224 | tf_op jit(solution)/shard_map/ppermute | solution.py:130
  130.2 3.2 %collective-permute-start.1 = (bf16[32,16,128]{2,1,0:T(8,128)(2,1)S(1)}, bf16[32,16,128]{2,1,0:T(8,128)(2,1)S(1)}, u32[]{:S(2)}, u32[]{:S(2)}) collective-permute-start(bf16[32,16,128]{2,1,0:T(8,128)(2,1)S(1)} %get-tuple-element.25), channel_id=1, source_target_pairs={{0,1},{1,0},{2,3},{3,2},{4,5},{5,4},{6,7},{7,6},{8,9},{9,8},{10,11... | collective-permute-start | bytes 393224 | tf_op jit(solution)/shard_map/ppermute | solution.py:130

commit v6 on v5

--- a/solution.py
+++ b/solution.py
@@ -6,13 +6,15 @@
 from jax.sharding import Mesh
 from jax.sharding import PartitionSpec as P
 
-UNROLL = 16
+UNROLL = 32
+TILE_COPIES = 4
 F32 = jnp.float32
 BF16 = jnp.bfloat16
 ROW, NEAR, CORE = "row", "near", "core"
 CORES = 2
 VMEM = pl.BlockSpec(memory_space=pltpu.VMEM)
 SMEM = pl.BlockSpec(memory_space=pltpu.SMEM)
+ANY = pl.BlockSpec(memory_space=pl.ANY)
 
 
 def by_core(tile_row, parts):
@@ -20,13 +22,22 @@
     return owner & (CORES - 1), (owner >> (CORES.bit_length() - 1)) * parts + part
 
 
-def start_kernel(vectors_ref, count_ref, own_ref, copies_ref, counts_ref):
+def start_kernel(vectors_in, rows_in, cols_in, tiles_in, count_ref, own_ref, copies_ref, counts_ref, rows_ref, cols_ref, tiles_ref, vectors_ref, arrived):
+    chunk = tiles_ref.shape[0] // TILE_COPIES
+    spans = [pl.ds(i * chunk, chunk) for i in range(TILE_COPIES)]
+    moves = [(vectors_in, vectors_ref), (rows_in, rows_ref), (cols_in, cols_ref)] + [(tiles_in.at[s], tiles_ref.at[s]) for s in spans]
+    copies = [pltpu.make_async_copy(source, target, arrived.at[i]) for i, (source, target) in enumerate(moves)]
+    for copy in copies:
+        copy.start()
+    counts_ref[...] = jnp.broadcast_to(count_ref[...], counts_ref.shape)
+    copies[0].wait()
     width = own_ref.shape[-1]
     for h in range(own_ref.shape[0]):
         value = vectors_ref[:, h * width:(h + 1) * width]
         own_ref[h] = value
         copies_ref[:, h] = jnp.broadcast_to(value[None], (copies_ref.shape[0],) + value.shape)
-    counts_ref[...] = jnp.broadcast_to(count_ref[...], counts_ref.shape)
+    for copy in copies[1:]:
+        copy.wait()
 
 
 def mirror_kernel(rows_ref, cols_ref, count_ref, tiles_ref, row_seg_ref, own_ref, packet_ref, acc):
@@ -77,7 +88,8 @@
 
 
 def half_kernel(keep_ref, recv_ref, out_ref):
-    out_ref[...] = (keep_ref[...] + recv_ref[...].astype(F32)).astype(BF16)
+    other = CORES - 1 - lax.axis_index(CORE)
+    out_ref[...] = (keep_ref[...] + recv_ref[other].astype(F32)).astype(BF16)
 
 
 def image_kernel(row_sum_ref, near_recv_ref, image_ref, *next_refs):
@@ -91,14 +103,14 @@
             copies_ref[:, h] = jnp.broadcast_to(value[None], (copies_ref.shape[0],) + value.shape)
 
 
-def call(kernel, name, in_specs, shapes, scratch, flops, moved, *args):
+def call(kernel, name, in_specs, shapes, scratch, flops, moved, *args, vmem=12 * 1024):
     return pl.pallas_call(
         kernel,
         out_shape=tuple(jax.ShapeDtypeStruct(s, d) for s, d in shapes),
         in_specs=in_specs,
         out_specs=(VMEM,) * len(shapes),
         scratch_shapes=scratch,
-        compiler_params=pltpu.CompilerParams(vmem_limit_bytes=12 * 1024 * 1024),
+        compiler_params=pltpu.CompilerParams(vmem_limit_bytes=vmem * 1024),
         cost_estimate=pl.CostEstimate(flops=flops, bytes_accessed=moved, transcendentals=0),
         name=name,
     )(*args)
@@ -106,7 +118,6 @@
 
 def per_device(tile_values, tile_rows, tile_cols, tile_count, vectors):
     tiles = tile_values[0, 0]
-    rows, cols = tile_rows[0, 0], tile_cols[0, 0]
     slots, tile = tiles.shape[0], tiles.shape[-1]
     vec_count, slice_len = vectors.shape
     parts = slice_len // tile
@@ -127,7 +138,7 @@
         keep, send, row_sum = call(
             direct_kernel, "direct_products", [SMEM] * 2 + [VMEM] * 3,
             [(half, F32), (half, BF16), (piece, F32)], acc(CORES * half[0]), flops, moved, rows, cols, count, tiles, packet)
-        recv = lax.ppermute(send, CORE, [(0, 1), (1, 0)])
+        recv = lax.all_gather(send, CORE, axis=0)
         (chip,) = call(half_kernel, "chip_sum", [VMEM] * 2, [(half, BF16)], [], keep.size, 8 * keep.size, keep, recv)
         near_recv = lax.all_to_all(chip.reshape((near,) + piece), NEAR, 0, 0)
         shapes = [((vec_count, slice_len), dtype)]
@@ -135,9 +146,13 @@
             shapes += [(piece, dtype), ((near,) + piece, dtype)]
         return call(image_kernel, "image", [VMEM] * 2, shapes, [], near_recv.size, 4 * near_recv.size, row_sum, near_recv)
 
-    own, copies, count = call(
-        start_kernel, "start", [VMEM] * 2, [(piece, BF16), ((near,) + piece, BF16), ((vec_count, tile), jnp.int32)],
-        [], vectors.size, 40 * vectors.size, vectors, tile_count)
+    places = [(tile_rows.shape, jnp.int32), (tile_cols.shape, jnp.int32)]
+    own, copies, count, rows, cols, tiles = call(
+        start_kernel, "start", [ANY] * 4 + [VMEM],
+        [(piece, BF16), ((near,) + piece, BF16), ((vec_count, tile), jnp.int32)] + places + [(tiles.shape, BF16)],
+        [pltpu.VMEM(vectors.shape, BF16), pltpu.SemaphoreType.DMA((3 + TILE_COPIES,))], vectors.size, moved,
+        vectors, tile_rows, tile_cols, tiles, tile_count, vmem=50500)
+    rows, cols = rows[0, 0], cols[0, 0]
     first_image, own, copies = image(own, copies, BF16, True)
     (second_image,) = image(own, copies, F32, False)
     return (first_image, second_image)

time: 146 us -> 142 us (0.973)
  blocking collectives: 122 us -> 126 us
  starting transfers between devices: 3.84 us -> 0 us
  waiting for transfers between devices: 2.63 us -> 0 us
  local copies, waits for them, and re-layouts: 3.91 us -> 2 us
    all_gather x0 -> x2, blocking collectives: none -> 3.99 us  [image(): recv = lax.all_gather(send, CORE, axis=0)]
    ppermute x2 -> x0, starting transfers between devices: 3.84 us -> none  [image(): recv = lax.ppermute(send, CORE, [(0, 1), (1, 0)])]
    ppermute x2 -> x0, waiting for transfers between devices: 2.63 us -> none  [image(): recv = lax.ppermute(send, CORE, [(0, 1), (1, 0)])]
    unnamed x14 -> x6, local copies, waits for them, and re-layouts: 3.91 us -> 2 us
  transfers between devices with their start and end apart: 2 -> 0, of which waited for: 2 -> 0; matrix products, arithmetic and copies ran while one was open for 0% -> 0% of each run, Pallas kernels for 0% -> 0%
where the time goes in v6:
time: 142 us
  blocking collectives  126 us (89%)
  Pallas kernels  12.2 us (9%)
  local copies, waits for them, and re-layouts  2 us (1%)
    all_to_all x2, blocking collectives, image(): packet = lax.all_to_all(packet, ROW, 0, 0)  65.2 us
    all_to_all x2, blocking collectives, image(): near_recv = lax.all_to_all(near_copies, NEAR, 0, 0)  29.7 us
    all_to_all x2, blocking collectives, image(): near_recv = lax.all_to_all(chip.reshape((near,) + piece), NEAR, 0, 0)  23.5 us
    pallas_call x9, Pallas kernels, call(): pl.pallas_call(kernel, out_shape=tuple((jax.ShapeDtypeStruct(s, d) for s,...  12.2 us
    all_gather x2, blocking collectives, image(): recv = lax.all_gather(send, CORE, axis=0)  3.99 us
    all_gather x2, blocking collectives, image(): row_seg = lax.all_gather(near_recv.reshape(half), CORE, axis=0, tiled=True)  3.96 us

profile of v6, /device:TPU:16, one launch (start us, length us, event | category | flops | bytes accessed | tf_op | source)
XLA Modules:
  0.0 141.9 jit_solution(8027951013863538269)
XLA Ops:
  1.3 0.0 copy-start
  1.3 0.7 copy-done
  2.0 0.0 copy-start.1
  2.0 0.7 copy-done.1
  2.6 0.0 copy-start.2
  2.6 0.7 copy-done.2
  3.3 1.9 %start.1 = (bf16[2,16,128]{2,1,0:T(8,128)(2,1)S(1)}, bf16[16,2,16,128]{3,2,1,0:T(8,128)(2,1)S(1)}, s32[16,128]{1,0:T(8,128)S(1)}, s32[1,1,96]{2,1,0:T(1,128)S(1)...) custom-call(bf16[16,256]{1,0:T(8,128)(2,1)S(1)} %copy-done, s32[1,1,96]{2,1,0:T(1,128)S(1)} %copy-done.1, ...), custom_call_target="tpu_custom_call" | custom-call | flops 4096 | bytes 3145728 | tf_op jit(solution)/shard_map/start/pallas_call | solution.py:107
  5.2 18.0 %all_to_all.30 = bf16[16,2,16,128]{3,2,1,0:T(8,128)(2,1)S(1)} all-to-all(bf16[16,2,16,128]{3,2,1,0:T(8,128)(2,1)S(1)} %get-tuple-element.21), channel_id=1, replica_groups=mesh['row'=32,'near'=16,'core'=2] {'near'}, dimensions={0} | all-to-all | bytes 262144 | tf_op jit(solution)/shard_map/all_to_all | solution.py:132
  23.2 2.0 %all_gather.18.row_seg_ref = bf16[64,16,128]{2,1,0:T(8,128)(2,1)S(1)} all-gather(bf16[32,16,128]{2,1,0:T(8,128)(2,1)S(1)} %bitcast.22), channel_id=1, replica_groups=mesh['row'=32,'near'=16,'core'=2] {'core'}, dimensions={0}, use_global_device_ids=true | all-gather | bytes 393216 | tf_op jit(solution)/shard_map/all_gather | solution.py:133
  25.1 1.8 %mirror_products.2 = bf16[32,4,16,128]{3,2,1,0:T(8,128)(2,1)S(1)} custom-call(s32[96]{0:T(128)S(1)} %bitcast.13, s32[96]{0:T(128)S(1)} %bitcast.17, s32[16,128]{1,0:T(8,128)S(1)} %get-tuple-element.19.count_ref, bf16[96,128,128]{2,1,0:T(8,128)(2,1)S(1)} %get-tuple-element.20.tiles_ref, bf16[64,16,128]{2,1,0:T(8,128)(2,1)S(1)} %all_gather.18.row_seg_ref, ...), custom_call_target="tpu_custom_call" | custom-call | flops 50331648 | bytes 3145728 | tf_op jit(solution)/shard_map/mirror_products/pallas_call | solution.py:107
  27.0 40.6 %all_to_all.31.packet_ref = bf16[32,4,16,128]{3,2,1,0:T(8,128)(2,1)S(1)} all-to-all(bf16[32,4,16,128]{3,2,1,0:T(8,128)(2,1)S(1)} %mirror_products.2), channel_id=1, replica_groups=mesh['row'=32,'near'=16,'core'=2] {'row'}, dimensions={0} | all-to-all | bytes 1048576 | tf_op jit(solution)/shard_map/all_to_all | solution.py:137
  67.6 2.6 %direct_products.2 = (f32[32,16,128]{2,1,0:T(8,128)S(1)}, bf16[32,16,128]{2,1,0:T(8,128)(2,1)S(1)}, f32[2,16,128]{2,1,0:T(8,128)S(1)}) custom-call(s32[96]{0:T(128)S(1)} %bitcast.14, s32[96]{0:T(128)S(1)} %bitcast.18, s32[16,128]{1,0:T(8,128)S(1)} %get-tuple-element.19.count_ref, bf16[96,128,128]{2,1,0:T(8,128)(2,1)S(1)} %get-tuple-element.20.tiles_ref, ...), custom_call_target="tpu_custom_call" | custom-call | flops 50331648 | bytes 3145728 | tf_op jit(solution)/shard_map/direct_products/pallas_call | solution.py:107
  70.2 2.0 %all-gather = bf16[64,16,128]{2,1,0:T(8,128)(2,1)S(1)} all-gather(bf16[32,16,128]{2,1,0:T(8,128)(2,1)S(1)} %get-tuple-element.25), channel_id=2, replica_groups=mesh['row'=32,'near'=16,'core'=2] {'core'}, dimensions={0}, use_global_device_ids=true | all-gather | bytes 393216 | tf_op jit(solution)/shard_map/all_gather | solution.py:141
  72.2 11.8 %all_to_all.32.near_recv_ref = bf16[16,2,16,128]{3,2,1,0:T(8,128)(2,1)S(1)} all-to-all(bf16[16,2,16,128]{3,2,1,0:T(8,128)(2,1)S(1)} %bitcast.11), channel_id=1, replica_groups=mesh['row'=32,'near'=16,'core'=2] {'near'}, dimensions={0} | all-to-all | bytes 262144 | tf_op jit(solution)/shard_map/all_to_all | solution.py:143
  84.0 0.6 image.2
  84.6 11.8 %all_to_all.33 = bf16[16,2,16,128]{3,2,1,0:T(8,128)(2,1)S(1)} all-to-all(bf16[16,2,16,128]{3,2,1,0:T(8,128)(2,1)S(1)} %get-tuple-element.27), channel_id=1, replica_groups=mesh['row'=32,'near'=16,'core'=2] {'near'}, dimensions={0} | all-to-all | bytes 262144 | tf_op jit(solution)/shard_map/all_to_all | solution.py:132
  96.4 2.0 %all_gather.21.row_seg_ref = bf16[64,16,128]{2,1,0:T(8,128)(2,1)S(1)} all-gather(bf16[32,16,128]{2,1,0:T(8,128)(2,1)S(1)} %bitcast.23), channel_id=1, replica_groups=mesh['row'=32,'near'=16,'core'=2] {'core'}, dimensions={0}, use_global_device_ids=true | all-gather | bytes 393216 | tf_op jit(solution)/shard_map/all_gather | solution.py:133
  98.4 1.8 %mirror_products.3 = bf16[32,4,16,128]{3,2,1,0:T(8,128)(2,1)S(1)} custom-call(s32[96]{0:T(128)S(1)} %bitcast.15, s32[96]{0:T(128)S(1)} %bitcast.19, s32[16,128]{1,0:T(8,128)S(1)} %get-tuple-element.19.count_ref, bf16[96,128,128]{2,1,0:T(8,128)(2,1)S(1)} %get-tuple-element.20.tiles_ref, bf16[64,16,128]{2,1,0:T(8,128)(2,1)S(1)} %all_gather.21.row_seg_ref, ...), custom_call_target="tpu_custom_call" | custom-call | flops 50331648 | bytes 3145728 | tf_op jit(solution)/shard_map/mirror_products/pallas_call | solution.py:107
  100.2 24.6 %all_to_all.34.packet_ref = bf16[32,4,16,128]{3,2,1,0:T(8,128)(2,1)S(1)} all-to-all(bf16[32,4,16,128]{3,2,1,0:T(8,128)(2,1)S(1)} %mirror_products.3), channel_id=1, replica_groups=mesh['row'=32,'near'=16,'core'=2] {'row'}, dimensions={0} | all-to-all | bytes 1048576 | tf_op jit(solution)/shard_map/all_to_all | solution.py:137
  124.8 2.7 %direct_products.3 = (f32[32,16,128]{2,1,0:T(8,128)S(1)}, bf16[32,16,128]{2,1,0:T(8,128)(2,1)S(1)}, f32[2,16,128]{2,1,0:T(8,128)S(1)}) custom-call(s32[96]{0:T(128)S(1)} %bitcast.16, s32[96]{0:T(128)S(1)} %bitcast.20, s32[16,128]{1,0:T(8,128)S(1)} %get-tuple-element.19.count_ref, bf16[96,128,128]{2,1,0:T(8,128)(2,1)S(1)} %get-tuple-element.20.tiles_ref, ...), custom_call_target="tpu_custom_call" | custom-call | flops 50331648 | bytes 3145728 | tf_op jit(solution)/shard_map/direct_products/pallas_call | solution.py:107
  127.5 2.0 %all-gather.1 = bf16[64,16,128]{2,1,0:T(8,128)(2,1)S(1)} all-gather(bf16[32,16,128]{2,1,0:T(8,128)(2,1)S(1)} %get-tuple-element.31), channel_id=3, replica_groups=mesh['row'=32,'near'=16,'core'=2] {'core'}, dimensions={0}, use_global_device_ids=true | all-gather | bytes 393216 | tf_op jit(solution)/shard_map/all_gather | solution.py:141
  129.5 11.8 %all_to_all.35.near_recv_ref = bf16[16,2,16,128]{3,2,1,0:T(8,128)(2,1)S(1)} all-to-all(bf16[16,2,16,128]{3,2,1,0:T(8,128)(2,1)S(1)} %bitcast.12), channel_id=1, replica_groups=mesh['row'=32,'near'=16,'core'=2] {'near'}, dimensions={0} | all-to-all | bytes 262144 | tf_op jit(solution)/shard_map/all_to_all | solution.py:143
  141.3 0.6 image.3
  (2 shorter events, 0.1 us)
Async XLA Ops:
  1.3 0.7 copy-start
  2.0 0.7 copy-start.1
  2.6 0.7 copy-start.2

commit v7 on v6

--- a/solution.py
+++ b/solution.py
@@ -6,7 +6,7 @@
 from jax.sharding import Mesh
 from jax.sharding import PartitionSpec as P
 
-UNROLL = 32
+UNROLL = 48
 TILE_COPIES = 4
 F32 = jnp.float32
 BF16 = jnp.bfloat16
@@ -22,14 +22,14 @@
     return owner & (CORES - 1), (owner >> (CORES.bit_length() - 1)) * parts + part
 
 
-def start_kernel(vectors_in, rows_in, cols_in, tiles_in, count_ref, own_ref, copies_ref, counts_ref, rows_ref, cols_ref, tiles_ref, vectors_ref, arrived):
+def start_kernel(vectors_in, tiles_in, places_ref, own_ref, copies_ref, places_out, tiles_ref, vectors_ref, arrived):
     chunk = tiles_ref.shape[0] // TILE_COPIES
     spans = [pl.ds(i * chunk, chunk) for i in range(TILE_COPIES)]
-    moves = [(vectors_in, vectors_ref), (rows_in, rows_ref), (cols_in, cols_ref)] + [(tiles_in.at[s], tiles_ref.at[s]) for s in spans]
+    moves = [(vectors_in, vectors_ref)] + [(tiles_in.at[s], tiles_ref.at[s]) for s in spans]
     copies = [pltpu.make_async_copy(source, target, arrived.at[i]) for i, (source, target) in enumerate(moves)]
     for copy in copies:
         copy.start()
-    counts_ref[...] = jnp.broadcast_to(count_ref[...], counts_ref.shape)
+    places_out[...] = places_ref[...]
     copies[0].wait()
     width = own_ref.shape[-1]
     for h in range(own_ref.shape[0]):
@@ -40,42 +40,42 @@
         copy.wait()
 
 
-def mirror_kernel(rows_ref, cols_ref, count_ref, tiles_ref, row_seg_ref, own_ref, packet_ref, acc):
+def mirror_kernel(places_ref, tiles_ref, row_seg_ref, own_ref, packet_ref, acc):
     slots, parts, peers = tiles_ref.shape[0], own_ref.shape[0], packet_ref.shape[0]
     half = row_seg_ref.shape[0] // CORES
     acc[...] = jnp.zeros_like(acc)
-    count = count_ref[...]
+    count, spare = places_ref[2 * slots], acc.shape[0] - 1
 
     def block(step, _):
         results = []
         for u in range(UNROLL):
             n = step * UNROLL + u
-            core, place = by_core(rows_ref[n], parts)
+            core, place = by_core(places_ref[n] & (CORES * half - 1), parts)
             product = lax.dot_general(row_seg_ref[core * half + place], tiles_ref[n], (((1,), (0,)), ((), ())), preferred_element_type=F32)
-            results.append((cols_ref[n], jnp.where(n < count, product, 0.0)))
+            results.append((jnp.where(n < count, places_ref[slots + n], spare), product))
         for c, product in results:
             acc[c] += product
         return 0
 
     lax.fori_loop(0, slots // UNROLL, block, 0)
     packet_ref[:, :parts] = jnp.broadcast_to(own_ref[...][None], (peers,) + own_ref.shape)
-    packet_ref[:, parts:] = acc[...].astype(BF16).reshape((peers,) + own_ref.shape)
+    packet_ref[:, parts:] = acc[:peers * parts].astype(BF16).reshape((peers,) + own_ref.shape)
 
 
-def direct_kernel(rows_ref, cols_ref, count_ref, tiles_ref, packet_ref, keep_ref, send_ref, row_sum_ref, acc):
+def direct_kernel(places_ref, tiles_ref, packet_ref, keep_ref, send_ref, row_sum_ref, acc):
     slots, half, parts = tiles_ref.shape[0], keep_ref.shape[0], row_sum_ref.shape[0]
     acc[...] = jnp.zeros_like(acc)
-    count, mine = count_ref[...], lax.axis_index(CORE)
+    count, mine, spare = places_ref[2 * slots], lax.axis_index(CORE), acc.shape[0] - 1
 
     def block(step, _):
         results = []
         for u in range(UNROLL):
             n = step * UNROLL + u
-            col = cols_ref[n]
+            col = places_ref[slots + n] & (packet_ref.shape[0] * parts - 1)
             picked = packet_ref[col >> (parts.bit_length() - 1), col & (parts - 1)]
             product = lax.dot_general(picked, tiles_ref[n], (((1,), (1,)), ((), ())), preferred_element_type=F32)
-            core, place = by_core(rows_ref[n], parts)
-            results.append(((core ^ mine) * half + place, jnp.where(n < count, product, 0.0)))
+            core, place = by_core(places_ref[n], parts)
+            results.append((jnp.where(n < count, (core ^ mine) * half + place, spare), product))
         for r, product in results:
             acc[r] += product
         return 0
@@ -126,18 +126,18 @@
     half = (near * parts, vec_count, tile)
     packets = (peers, 2 * parts, vec_count, tile)
     flops, moved = 2 * slots * vec_count * tile * tile, 2 * tiles.size
-    acc = lambda n: [pltpu.VMEM((n, vec_count, tile), F32)]
+    acc = lambda n: [pltpu.VMEM((n + 1, vec_count, tile), F32)]
 
     def image(own, near_copies, dtype, again):
         near_recv = lax.all_to_all(near_copies, NEAR, 0, 0)
         row_seg = lax.all_gather(near_recv.reshape(half), CORE, axis=0, tiled=True)
         (packet,) = call(
-            mirror_kernel, "mirror_products", [SMEM] * 2 + [VMEM] * 4,
-            [(packets, BF16)], acc(peers * parts), flops, moved, rows, cols, count, tiles, row_seg, own)
+            mirror_kernel, "mirror_products", [SMEM] + [VMEM] * 3,
+            [(packets, BF16)], acc(peers * parts), flops, moved, places, tiles, row_seg, own)
         packet = lax.all_to_all(packet, ROW, 0, 0)
         keep, send, row_sum = call(
-            direct_kernel, "direct_products", [SMEM] * 2 + [VMEM] * 3,
-            [(half, F32), (half, BF16), (piece, F32)], acc(CORES * half[0]), flops, moved, rows, cols, count, tiles, packet)
+            direct_kernel, "direct_products", [SMEM] + [VMEM] * 2,
+            [(half, F32), (half, BF16), (piece, F32)], acc(CORES * half[0]), flops, moved, places, tiles, packet)
         recv = lax.all_gather(send, CORE, axis=0)
         (chip,) = call(half_kernel, "chip_sum", [VMEM] * 2, [(half, BF16)], [], keep.size, 8 * keep.size, keep, recv)
         near_recv = lax.all_to_all(chip.reshape((near,) + piece), NEAR, 0, 0)
@@ -146,13 +146,12 @@
             shapes += [(piece, dtype), ((near,) + piece, dtype)]
         return call(image_kernel, "image", [VMEM] * 2, shapes, [], near_recv.size, 4 * near_recv.size, row_sum, near_recv)
 
-    places = [(tile_rows.shape, jnp.int32), (tile_cols.shape, jnp.int32)]
-    own, copies, count, rows, cols, tiles = call(
-        start_kernel, "start", [ANY] * 4 + [VMEM],
-        [(piece, BF16), ((near,) + piece, BF16), ((vec_count, tile), jnp.int32)] + places + [(tiles.shape, BF16)],
-        [pltpu.VMEM(vectors.shape, BF16), pltpu.SemaphoreType.DMA((3 + TILE_COPIES,))], vectors.size, moved,
-        vectors, tile_rows, tile_cols, tiles, tile_count, vmem=50500)
-    rows, cols = rows[0, 0], cols[0, 0]
+    places = jnp.concatenate([tile_rows[0, 0], tile_cols[0, 0], tile_count[0]])
+    own, copies, places, tiles = call(
+        start_kernel, "start", [ANY] * 2 + [VMEM],
+        [(piece, BF16), ((near,) + piece, BF16), (places.shape, jnp.int32), (tiles.shape, BF16)],
+        [pltpu.VMEM(vectors.shape, BF16), pltpu.SemaphoreType.DMA((1 + TILE_COPIES,))], vectors.size, moved,
+        vectors, tiles, places, vmem=50500)
     first_image, own, copies = image(own, copies, BF16, True)
     (second_image,) = image(own, copies, F32, False)
     return (first_image, second_image)

time: 142 us -> 142 us (level)
  no operation moved by 1% of the time
where the time goes in v7:
time: 142 us; the launch traced here: 141 us
  blocking collectives  126 us (89%)
  Pallas kernels  11.9 us (8%)
    all_to_all x2, blocking collectives, image(): packet = lax.all_to_all(packet, ROW, 0, 0)  65.2 us
    all_to_all x2, blocking collectives, image(): near_recv = lax.all_to_all(near_copies, NEAR, 0, 0)  29.7 us
    all_to_all x2, blocking collectives, image(): near_recv = lax.all_to_all(chip.reshape((near,) + piece), NEAR, 0, 0)  23.5 us
    pallas_call x9, Pallas kernels, call(): pl.pallas_call(kernel, out_shape=tuple((jax.ShapeDtypeStruct(s, d) for s,...  11.9 us
    all_gather x2, blocking collectives, image(): recv = lax.all_gather(send, CORE, axis=0)  3.99 us
    all_gather x2, blocking collectives, image(): row_seg = lax.all_gather(near_recv.reshape(half), CORE, axis=0, tiled=True)  3.96 us

profile of v7, /device:TPU:16, one launch (start us, length us, event | category | flops | bytes accessed | tf_op | source)
XLA Modules:
  0.0 141.1 jit_solution(7127109412008159726)
XLA Ops:
  1.3 0.7 pad_add_fusion.places_ref
  2.0 0.0 copy-start
  2.0 0.7 copy-done
  2.7 1.9 %start.1 = (bf16[2,16,128]{2,1,0:T(8,128)(2,1)S(1)}, bf16[16,2,16,128]{3,2,1,0:T(8,128)(2,1)S(1)}, s32[193]{0:T(256)S(1)}, bf16[96,128,128]{2,1,0:T(8,128)(2,1)S(1)}) custom-call(bf16[16,256]{1,0:T(8,128)(2,1)S(1)} %copy-done, bf16[96,128,128]{2,1,0:T(8,128)(2,1)} %bitcast.15, s32[193]{0:T(256)S(1)} %pad_add_fusion.places_ref), custom_call_target="tpu_custom_call" | custom-call | flops 4096 | bytes 3145728 | tf_op jit(solution)/shard_map/start/pallas_call | solution.py:107
  4.6 18.0 %all_to_all.30 = bf16[16,2,16,128]{3,2,1,0:T(8,128)(2,1)S(1)} all-to-all(bf16[16,2,16,128]{3,2,1,0:T(8,128)(2,1)S(1)} %get-tuple-element.17), channel_id=1, replica_groups=mesh['row'=32,'near'=16,'core'=2] {'near'}, dimensions={0} | all-to-all | bytes 262144 | tf_op jit(solution)/shard_map/all_to_all | solution.py:132
  22.6 2.0 %all_gather.18.row_seg_ref = bf16[64,16,128]{2,1,0:T(8,128)(2,1)S(1)} all-gather(bf16[32,16,128]{2,1,0:T(8,128)(2,1)S(1)} %bitcast.16), channel_id=1, replica_groups=mesh['row'=32,'near'=16,'core'=2] {'core'}, dimensions={0}, use_global_device_ids=true | all-gather | bytes 393216 | tf_op jit(solution)/shard_map/all_gather | solution.py:133
  24.6 1.7 %mirror_products.2 = bf16[32,4,16,128]{3,2,1,0:T(8,128)(2,1)S(1)} custom-call(s32[193]{0:T(256)S(1)} %get-tuple-element.15.places_ref, bf16[96,128,128]{2,1,0:T(8,128)(2,1)S(1)} %get-tuple-element.16.tiles_ref, bf16[64,16,128]{2,1,0:T(8,128)(2,1)S(1)} %all_gather.18.row_seg_ref, bf16[2,16,128]{2,1,0:T(8,128)(2,1)S(1)} %get-tuple-element.18.own_ref), custom_call_target="tpu_custom_call" | custom-call | flops 50331648 | bytes 3145728 | tf_op jit(solution)/shard_map/mirror_products/pallas_call | solution.py:107
  26.3 40.6 %all_to_all.31.packet_ref = bf16[32,4,16,128]{3,2,1,0:T(8,128)(2,1)S(1)} all-to-all(bf16[32,4,16,128]{3,2,1,0:T(8,128)(2,1)S(1)} %mirror_products.2), channel_id=1, replica_groups=mesh['row'=32,'near'=16,'core'=2] {'row'}, dimensions={0} | all-to-all | bytes 1048576 | tf_op jit(solution)/shard_map/all_to_all | solution.py:137
  66.9 2.6 %direct_products.2 = (f32[32,16,128]{2,1,0:T(8,128)S(1)}, bf16[32,16,128]{2,1,0:T(8,128)(2,1)S(1)}, f32[2,16,128]{2,1,0:T(8,128)S(1)}) custom-call(s32[193]{0:T(256)S(1)} %get-tuple-element.15.places_ref, bf16[96,128,128]{2,1,0:T(8,128)(2,1)S(1)} %get-tuple-element.16.tiles_ref, bf16[32,4,16,128]{3,2,1,0:T(8,128)(2,1)S(1)} %all_to_all.31.packet_ref), custom_call_target="tpu_custom_call" | custom-call | flops 50331648 | bytes 3145728 | tf_op jit(solution)/shard_map/direct_products/pallas_call | solution.py:107
  69.5 2.0 %all-gather = bf16[64,16,128]{2,1,0:T(8,128)(2,1)S(1)} all-gather(bf16[32,16,128]{2,1,0:T(8,128)(2,1)S(1)} %get-tuple-element.21), channel_id=2, replica_groups=mesh['row'=32,'near'=16,'core'=2] {'core'}, dimensions={0}, use_global_device_ids=true | all-gather | bytes 393216 | tf_op jit(solution)/shard_map/all_gather | solution.py:141
  71.5 11.8 %all_to_all.32.near_recv_ref = bf16[16,2,16,128]{3,2,1,0:T(8,128)(2,1)S(1)} all-to-all(bf16[16,2,16,128]{3,2,1,0:T(8,128)(2,1)S(1)} %bitcast.13), channel_id=1, replica_groups=mesh['row'=32,'near'=16,'core'=2] {'near'}, dimensions={0} | all-to-all | bytes 262144 | tf_op jit(solution)/shard_map/all_to_all | solution.py:143
  83.3 0.6 image.2
  83.9 11.8 %all_to_all.33 = bf16[16,2,16,128]{3,2,1,0:T(8,128)(2,1)S(1)} all-to-all(bf16[16,2,16,128]{3,2,1,0:T(8,128)(2,1)S(1)} %get-tuple-element.23), channel_id=1, replica_groups=mesh['row'=32,'near'=16,'core'=2] {'near'}, dimensions={0} | all-to-all | bytes 262144 | tf_op jit(solution)/shard_map/all_to_all | solution.py:132
  95.7 2.0 %all_gather.21.row_seg_ref = bf16[64,16,128]{2,1,0:T(8,128)(2,1)S(1)} all-gather(bf16[32,16,128]{2,1,0:T(8,128)(2,1)S(1)} %bitcast.17), channel_id=1, replica_groups=mesh['row'=32,'near'=16,'core'=2] {'core'}, dimensions={0}, use_global_device_ids=true | all-gather | bytes 393216 | tf_op jit(solution)/shard_map/all_gather | solution.py:133
  97.7 1.7 %mirror_products.3 = bf16[32,4,16,128]{3,2,1,0:T(8,128)(2,1)S(1)} custom-call(s32[193]{0:T(256)S(1)} %get-tuple-element.15.places_ref, bf16[96,128,128]{2,1,0:T(8,128)(2,1)S(1)} %get-tuple-element.16.tiles_ref, bf16[64,16,128]{2,1,0:T(8,128)(2,1)S(1)} %all_gather.21.row_seg_ref, bf16[2,16,128]{2,1,0:T(8,128)(2,1)S(1)} %get-tuple-element.24.own_ref), custom_call_target="tpu_custom_call" | custom-call | flops 50331648 | bytes 3145728 | tf_op jit(solution)/shard_map/mirror_products/pallas_call | solution.py:107
  99.4 24.6 %all_to_all.34.packet_ref = bf16[32,4,16,128]{3,2,1,0:T(8,128)(2,1)S(1)} all-to-all(bf16[32,4,16,128]{3,2,1,0:T(8,128)(2,1)S(1)} %mirror_products.3), channel_id=1, replica_groups=mesh['row'=32,'near'=16,'core'=2] {'row'}, dimensions={0} | all-to-all | bytes 1048576 | tf_op jit(solution)/shard_map/all_to_all | solution.py:137
  124.1 2.6 %direct_products.3 = (f32[32,16,128]{2,1,0:T(8,128)S(1)}, bf16[32,16,128]{2,1,0:T(8,128)(2,1)S(1)}, f32[2,16,128]{2,1,0:T(8,128)S(1)}) custom-call(s32[193]{0:T(256)S(1)} %get-tuple-element.15.places_ref, bf16[96,128,128]{2,1,0:T(8,128)(2,1)S(1)} %get-tuple-element.16.tiles_ref, bf16[32,4,16,128]{3,2,1,0:T(8,128)(2,1)S(1)} %all_to_all.34.packet_ref), custom_call_target="tpu_custom_call" | custom-call | flops 50331648 | bytes 3145728 | tf_op jit(solution)/shard_map/direct_products/pallas_call | solution.py:107
  126.7 2.0 %all-gather.1 = bf16[64,16,128]{2,1,0:T(8,128)(2,1)S(1)} all-gather(bf16[32,16,128]{2,1,0:T(8,128)(2,1)S(1)} %get-tuple-element.27), channel_id=3, replica_groups=mesh['row'=32,'near'=16,'core'=2] {'core'}, dimensions={0}, use_global_device_ids=true | all-gather | bytes 393216 | tf_op jit(solution)/shard_map/all_gather | solution.py:141
  128.7 11.7 %all_to_all.35.near_recv_ref = bf16[16,2,16,128]{3,2,1,0:T(8,128)(2,1)S(1)} all-to-all(bf16[16,2,16,128]{3,2,1,0:T(8,128)(2,1)S(1)} %bitcast.14), channel_id=1, replica_groups=mesh['row'=32,'near'=16,'core'=2] {'near'}, dimensions={0} | all-to-all | bytes 262144 | tf_op jit(solution)/shard_map/all_to_all | solution.py:143
  140.4 0.6 image.3
  (2 shorter events, 0.1 us)
Async XLA Ops:
  2.0 0.7 copy-start

commit v8 on v7

--- a/solution.py
+++ b/solution.py
@@ -22,21 +22,22 @@
     return owner & (CORES - 1), (owner >> (CORES.bit_length() - 1)) * parts + part
 
 
-def start_kernel(vectors_in, tiles_in, places_ref, own_ref, copies_ref, places_out, tiles_ref, vectors_ref, arrived):
-    chunk = tiles_ref.shape[0] // TILE_COPIES
-    spans = [pl.ds(i * chunk, chunk) for i in range(TILE_COPIES)]
-    moves = [(vectors_in, vectors_ref)] + [(tiles_in.at[s], tiles_ref.at[s]) for s in spans]
-    copies = [pltpu.make_async_copy(source, target, arrived.at[i]) for i, (source, target) in enumerate(moves)]
-    for copy in copies:
-        copy.start()
-    places_out[...] = places_ref[...]
-    copies[0].wait()
+def start_kernel(vectors_ref, own_ref, copies_ref):
     width = own_ref.shape[-1]
     for h in range(own_ref.shape[0]):
         value = vectors_ref[:, h * width:(h + 1) * width]
         own_ref[h] = value
         copies_ref[:, h] = jnp.broadcast_to(value[None], (copies_ref.shape[0],) + value.shape)
-    for copy in copies[1:]:
+
+
+def load_kernel(tiles_in, places_ref, places_out, tiles_ref, arrived):
+    chunk = tiles_ref.shape[0] // TILE_COPIES
+    spans = [pl.ds(i * chunk, chunk) for i in range(TILE_COPIES)]
+    copies = [pltpu.make_async_copy(tiles_in.at[s], tiles_ref.at[s], arrived.at[i]) for i, s in enumerate(spans)]
+    for copy in copies:
+        copy.start()
+    places_out[...] = places_ref[...]
+    for copy in copies:
         copy.wait()
 
 
@@ -147,11 +148,11 @@
         return call(image_kernel, "image", [VMEM] * 2, shapes, [], near_recv.size, 4 * near_recv.size, row_sum, near_recv)
 
     places = jnp.concatenate([tile_rows[0, 0], tile_cols[0, 0], tile_count[0]])
-    own, copies, places, tiles = call(
-        start_kernel, "start", [ANY] * 2 + [VMEM],
-        [(piece, BF16), ((near,) + piece, BF16), (places.shape, jnp.int32), (tiles.shape, BF16)],
-        [pltpu.VMEM(vectors.shape, BF16), pltpu.SemaphoreType.DMA((1 + TILE_COPIES,))], vectors.size, moved,
-        vectors, tiles, places, vmem=50500)
+    places, tiles = call(
+        load_kernel, "load", [ANY, VMEM], [(places.shape, jnp.int32), (tiles.shape, BF16)],
+        [pltpu.SemaphoreType.DMA((TILE_COPIES,))], vectors.size, 2 * moved, tiles, places, vmem=50500)
+    own, copies = call(
+        start_kernel, "start", [VMEM], [(piece, BF16), ((near,) + piece, BF16)], [], vectors.size, 40 * vectors.size, vectors)
     first_image, own, copies = image(own, copies, BF16, True)
     (second_image,) = image(own, copies, F32, False)
     return (first_image, second_image)

time: 142 us -> 139 us (0.979)
  blocking collectives: 126 us -> 108 us
  starting transfers between devices: 0 us -> 9.58 us
  waiting for transfers between devices: 0 us -> 5.29 us
    all_to_all x2 -> x1, blocking collectives: 29.7 us -> 11.8 us  [image(): near_recv = lax.all_to_all(near_copies, NEAR, 0, 0)]
    all_to_all x0 -> x1, starting transfers between devices: none -> 9.58 us  [image(): near_recv = lax.all_to_all(near_copies, NEAR, 0, 0)]
    all_to_all x0 -> x1, waiting for transfers between devices: none -> 5.29 us  [image(): near_recv = lax.all_to_all(near_copies, NEAR, 0, 0)]
    pallas_call x9 -> x10, Pallas kernels: 11.9 us -> 12.6 us  [call(): pl.pallas_call(kernel, out_shape=tuple((jax.ShapeDtypeStruct(s, d) for s,...]
  transfers between devices with their start and end apart: 0 -> 1, of which waited for: 0 -> 1; matrix products, arithmetic and copies ran while one was open for 0% -> 1% of each run, Pallas kernels for 0% -> 1%
where the time goes in v8:
time: 139 us
  blocking collectives  108 us (78%)
  Pallas kernels  12.6 us (9%)
  starting transfers between devices  9.58 us (7%)
  waiting for transfers between devices  5.29 us (4%)
    all_to_all x2, blocking collectives, image(): packet = lax.all_to_all(packet, ROW, 0, 0)  65.1 us
    all_to_all x2, blocking collectives, image(): near_recv = lax.all_to_all(chip.reshape((near,) + piece), NEAR, 0, 0)  23.5 us
    pallas_call x10, Pallas kernels, call(): pl.pallas_call(kernel, out_shape=tuple((jax.ShapeDtypeStruct(s, d) for s,...  12.6 us
    all_to_all x1, blocking collectives, image(): near_recv = lax.all_to_all(near_copies, NEAR, 0, 0)  11.8 us
    all_to_all x1, starting transfers between devices, image(): near_recv = lax.all_to_all(near_copies, NEAR, 0, 0)  9.58 us
    all_to_all x1, waiting for transfers between devices, image(): near_recv = lax.all_to_all(near_copies, NEAR, 0, 0)  5.29 us
    all_gather x2, blocking collectives, image(): recv = lax.all_gather(send, CORE, axis=0)  3.99 us
    all_gather x2, blocking collectives, image(): row_seg = lax.all_gather(near_recv.reshape(half), CORE, axis=0, tiled=True)  3.96 us
  transfers between devices with their start and end apart: 1, of which 1 were waited for; matrix products, arithmetic and copies ran while one was open for 1% of the time, Pallas kernels for 1%

profile of v8, /device:TPU:16, one launch (start us, length us, event | category | flops | bytes accessed | tf_op | source)
XLA Modules:
  0.0 138.7 jit_solution(2272034648285381641)
XLA Ops:
  0.6 0.0 copy-start
  0.6 0.7 copy-done
  1.3 0.7 start.1
  2.0 9.6 %all-to-all-start = ((bf16[16,2,16,128]{3,2,1,0:T(8,128)(2,1)}), bf16[16,2,16,128]{3,2,1,0:T(8,128)(2,1)S(1)}, u32[]{:S(2)}, u32[]{:S(2)}) async-start(bf16[16,2,16,128]{3,2,1,0:T(8,128)(2,1)} %get-tuple-element.17), calls=%async_computation | async-start | bytes 262144 | tf_op jit(solution)/shard_map/all_to_all | solution.py:133
  12.2 0.7 pad_add_fusion.places_ref
  13.0 1.9 %load.1 = (s32[193]{0:T(256)S(1)}, bf16[96,128,128]{2,1,0:T(8,128)(2,1)S(1)}) custom-call(bf16[96,128,128]{2,1,0:T(8,128)(2,1)} %bitcast.15, s32[193]{0:T(256)S(1)} %pad_add_fusion.places_ref), custom_call_target="tpu_custom_call" | custom-call | flops 4096 | bytes 6291456 | tf_op jit(solution)/shard_map/load/pallas_call | solution.py:108
  14.9 5.3 %all-to-all-done = bf16[16,2,16,128]{3,2,1,0:T(8,128)(2,1)S(1)} async-done(((bf16[16,2,16,128]{3,2,1,0:T(8,128)(2,1)}), bf16[16,2,16,128]{3,2,1,0:T(8,128)(2,1)S(1)}, u32[]{:S(2)}, u32[]{:S(2)}) %all-to-all-start) | async-done | bytes 131104 | tf_op jit(solution)/shard_map/all_to_all | solution.py:133
  20.2 2.0 %all_gather.18.row_seg_ref = bf16[64,16,128]{2,1,0:T(8,128)(2,1)S(1)} all-gather(bf16[32,16,128]{2,1,0:T(8,128)(2,1)S(1)} %bitcast.16), channel_id=1, replica_groups=mesh['row'=32,'near'=16,'core'=2] {'core'}, dimensions={0}, use_global_device_ids=true | all-gather | bytes 393216 | tf_op jit(solution)/shard_map/all_gather | solution.py:134
  22.1 1.8 %mirror_products.2 = bf16[32,4,16,128]{3,2,1,0:T(8,128)(2,1)S(1)} custom-call(s32[193]{0:T(256)S(1)} %get-tuple-element.15.places_ref, bf16[96,128,128]{2,1,0:T(8,128)(2,1)S(1)} %get-tuple-element.16.tiles_ref, bf16[64,16,128]{2,1,0:T(8,128)(2,1)S(1)} %all_gather.18.row_seg_ref, bf16[2,16,128]{2,1,0:T(8,128)(2,1)S(1)} %get-tuple-element.18.own_ref), custom_call_target="tpu_custom_call" | custom-call | flops 50331648 | bytes 3145728 | tf_op jit(solution)/shard_map/mirror_products/pallas_call | solution.py:108
  23.9 40.6 %all_to_all.30.packet_ref = bf16[32,4,16,128]{3,2,1,0:T(8,128)(2,1)S(1)} all-to-all(bf16[32,4,16,128]{3,2,1,0:T(8,128)(2,1)S(1)} %mirror_products.2), channel_id=1, replica_groups=mesh['row'=32,'near'=16,'core'=2] {'row'}, dimensions={0} | all-to-all | bytes 1048576 | tf_op jit(solution)/shard_map/all_to_all | solution.py:138
  64.5 2.6 %direct_products.2 = (f32[32,16,128]{2,1,0:T(8,128)S(1)}, bf16[32,16,128]{2,1,0:T(8,128)(2,1)S(1)}, f32[2,16,128]{2,1,0:T(8,128)S(1)}) custom-call(s32[193]{0:T(256)S(1)} %get-tuple-element.15.places_ref, bf16[96,128,128]{2,1,0:T(8,128)(2,1)S(1)} %get-tuple-element.16.tiles_ref, bf16[32,4,16,128]{3,2,1,0:T(8,128)(2,1)S(1)} %all_to_all.30.packet_ref), custom_call_target="tpu_custom_call" | custom-call | flops 50331648 | bytes 3145728 | tf_op jit(solution)/shard_map/direct_products/pallas_call | solution.py:108
  67.1 2.0 %all-gather = bf16[64,16,128]{2,1,0:T(8,128)(2,1)S(1)} all-gather(bf16[32,16,128]{2,1,0:T(8,128)(2,1)S(1)} %get-tuple-element.21), channel_id=2, replica_groups=mesh['row'=32,'near'=16,'core'=2] {'core'}, dimensions={0}, use_global_device_ids=true | all-gather | bytes 393216 | tf_op jit(solution)/shard_map/all_gather | solution.py:142
  69.1 11.8 %all_to_all.31.near_recv_ref = bf16[16,2,16,128]{3,2,1,0:T(8,128)(2,1)S(1)} all-to-all(bf16[16,2,16,128]{3,2,1,0:T(8,128)(2,1)S(1)} %bitcast.13), channel_id=1, replica_groups=mesh['row'=32,'near'=16,'core'=2] {'near'}, dimensions={0} | all-to-all | bytes 262144 | tf_op jit(solution)/shard_map/all_to_all | solution.py:144
  80.9 0.6 image.2
  81.5 11.8 %all_to_all.32 = bf16[16,2,16,128]{3,2,1,0:T(8,128)(2,1)S(1)} all-to-all(bf16[16,2,16,128]{3,2,1,0:T(8,128)(2,1)S(1)} %get-tuple-element.23), channel_id=1, replica_groups=mesh['row'=32,'near'=16,'core'=2] {'near'}, dimensions={0} | all-to-all | bytes 262144 | tf_op jit(solution)/shard_map/all_to_all | solution.py:133
  93.3 2.0 %all_gather.21.row_seg_ref = bf16[64,16,128]{2,1,0:T(8,128)(2,1)S(1)} all-gather(bf16[32,16,128]{2,1,0:T(8,128)(2,1)S(1)} %bitcast.17), channel_id=1, replica_groups=mesh['row'=32,'near'=16,'core'=2] {'core'}, dimensions={0}, use_global_device_ids=true | all-gather | bytes 393216 | tf_op jit(solution)/shard_map/all_gather | solution.py:134
  95.3 1.8 %mirror_products.3 = bf16[32,4,16,128]{3,2,1,0:T(8,128)(2,1)S(1)} custom-call(s32[193]{0:T(256)S(1)} %get-tuple-element.15.places_ref, bf16[96,128,128]{2,1,0:T(8,128)(2,1)S(1)} %get-tuple-element.16.tiles_ref, bf16[64,16,128]{2,1,0:T(8,128)(2,1)S(1)} %all_gather.21.row_seg_ref, bf16[2,16,128]{2,1,0:T(8,128)(2,1)S(1)} %get-tuple-element.24.own_ref), custom_call_target="tpu_custom_call" | custom-call | flops 50331648 | bytes 3145728 | tf_op jit(solution)/shard_map/mirror_products/pallas_call | solution.py:108
  97.0 24.6 %all_to_all.33.packet_ref = bf16[32,4,16,128]{3,2,1,0:T(8,128)(2,1)S(1)} all-to-all(bf16[32,4,16,128]{3,2,1,0:T(8,128)(2,1)S(1)} %mirror_products.3), channel_id=1, replica_groups=mesh['row'=32,'near'=16,'core'=2] {'row'}, dimensions={0} | all-to-all | bytes 1048576 | tf_op jit(solution)/shard_map/all_to_all | solution.py:138
  121.6 2.6 %direct_products.3 = (f32[32,16,128]{2,1,0:T(8,128)S(1)}, bf16[32,16,128]{2,1,0:T(8,128)(2,1)S(1)}, f32[2,16,128]{2,1,0:T(8,128)S(1)}) custom-call(s32[193]{0:T(256)S(1)} %get-tuple-element.15.places_ref, bf16[96,128,128]{2,1,0:T(8,128)(2,1)S(1)} %get-tuple-element.16.tiles_ref, bf16[32,4,16,128]{3,2,1,0:T(8,128)(2,1)S(1)} %all_to_all.33.packet_ref), custom_call_target="tpu_custom_call" | custom-call | flops 50331648 | bytes 3145728 | tf_op jit(solution)/shard_map/direct_products/pallas_call | solution.py:108
  124.2 2.0 %all-gather.1 = bf16[64,16,128]{2,1,0:T(8,128)(2,1)S(1)} all-gather(bf16[32,16,128]{2,1,0:T(8,128)(2,1)S(1)} %get-tuple-element.27), channel_id=3, replica_groups=mesh['row'=32,'near'=16,'core'=2] {'core'}, dimensions={0}, use_global_device_ids=true | all-gather | bytes 393216 | tf_op jit(solution)/shard_map/all_gather | solution.py:142
  126.3 11.8 %all_to_all.34.near_recv_ref = bf16[16,2,16,128]{3,2,1,0:T(8,128)(2,1)S(1)} all-to-all(bf16[16,2,16,128]{3,2,1,0:T(8,128)(2,1)S(1)} %bitcast.14), channel_id=1, replica_groups=mesh['row'=32,'near'=16,'core'=2] {'near'}, dimensions={0} | all-to-all | bytes 262144 | tf_op jit(solution)/shard_map/all_to_all | solution.py:144
  138.0 0.6 image.3
  (2 shorter events, 0.1 us)
Async XLA Ops:
  0.6 0.7 copy-start
  2.0 18.2 %all-to-all-start = ((bf16[16,2,16,128]{3,2,1,0:T(8,128)(2,1)}), bf16[16,2,16,128]{3,2,1,0:T(8,128)(2,1)S(1)}, u32[]{:S(2)}, u32[]{:S(2)}) async-start(bf16[16,2,16,128]{3,2,1,0:T(8,128)(2,1)} %get-tuple-element.17), calls=%async_computation | async-start | bytes 262144 | tf_op jit(solution)/shard_map/all_to_all | solution.py:133

commit v9 on v8

--- a/solution.py
+++ b/solution.py
@@ -6,7 +6,7 @@
 from jax.sharding import Mesh
 from jax.sharding import PartitionSpec as P
 
-UNROLL = 48
+UNROLL = 96
 TILE_COPIES = 4
 F32 = jnp.float32
 BF16 = jnp.bfloat16
@@ -152,7 +152,7 @@
         load_kernel, "load", [ANY, VMEM], [(places.shape, jnp.int32), (tiles.shape, BF16)],
         [pltpu.SemaphoreType.DMA((TILE_COPIES,))], vectors.size, 2 * moved, tiles, places, vmem=50500)
     own, copies = call(
-        start_kernel, "start", [VMEM], [(piece, BF16), ((near,) + piece, BF16)], [], vectors.size, 40 * vectors.size, vectors)
+        start_kernel, "start", [VMEM], [(piece, BF16), ((near,) + piece, BF16)], [], vectors.size, 40 * vectors.size, vectors, vmem=57000)
     first_image, own, copies = image(own, copies, BF16, True)
     (second_image,) = image(own, copies, F32, False)
     return (first_image, second_image)

time: 139 us -> 139 us (level)
  no operation moved by 1% of the time
where the time goes in v9:
time: 139 us; the launch traced here: 138 us
  blocking collectives  108 us (78%)
  Pallas kernels  12.5 us (9%)
  starting transfers between devices  9.71 us (7%)
  waiting for transfers between devices  5.29 us (4%)
    all_to_all x2, blocking collectives, image(): packet = lax.all_to_all(packet, ROW, 0, 0)  65.1 us
    all_to_all x2, blocking collectives, image(): near_recv = lax.all_to_all(chip.reshape((near,) + piece), NEAR, 0, 0)  23.6 us
    pallas_call x10, Pallas kernels, call(): pl.pallas_call(kernel, out_shape=tuple((jax.ShapeDtypeStruct(s, d) for s,...  12.5 us
    all_to_all x1, blocking collectives, image(): near_recv = lax.all_to_all(near_copies, NEAR, 0, 0)  11.8 us
    all_to_all x1, starting transfers between devices, image(): near_recv = lax.all_to_all(near_copies, NEAR, 0, 0)  9.71 us
    all_to_all x1, waiting for transfers between devices, image(): near_recv = lax.all_to_all(near_copies, NEAR, 0, 0)  5.29 us
    all_gather x2, blocking collectives, image(): recv = lax.all_gather(send, CORE, axis=0)  3.99 us
    all_gather x2, blocking collectives, image(): row_seg = lax.all_gather(near_recv.reshape(half), CORE, axis=0, tiled=True)  3.96 us
  transfers between devices with their start and end apart: 1, of which 1 were waited for; matrix products, arithmetic and copies ran while one was open for 1% of the time, Pallas kernels for 1%

profile of v9, /device:TPU:16, one launch (start us, length us, event | category | flops | bytes accessed | tf_op | source)
XLA Modules:
  0.0 138.1 jit_solution(13568956266421913882)
XLA Ops:
  0.6 1.4 start.1
  2.0 0.0 copy-start
  2.0 9.7 %all-to-all-start = ((bf16[16,2,16,128]{3,2,1,0:T(8,128)(2,1)}), bf16[16,2,16,128]{3,2,1,0:T(8,128)(2,1)S(1)}, u32[]{:S(2)}, u32[]{:S(2)}) async-start(bf16[16,2,16,128]{3,2,1,0:T(8,128)(2,1)} %get-tuple-element.17), calls=%async_computation | async-start | bytes 262144 | tf_op jit(solution)/shard_map/all_to_all | solution.py:133
  12.4 0.7 pad_add_fusion.places_ref
  13.1 1.9 %load.1 = (s32[193]{0:T(256)S(1)}, bf16[96,128,128]{2,1,0:T(8,128)(2,1)S(1)}) custom-call(bf16[96,128,128]{2,1,0:T(8,128)(2,1)} %bitcast.15, s32[193]{0:T(256)S(1)} %pad_add_fusion.places_ref), custom_call_target="tpu_custom_call" | custom-call | flops 4096 | bytes 6291456 | tf_op jit(solution)/shard_map/load/pallas_call | solution.py:108
  15.0 5.3 %all-to-all-done = bf16[16,2,16,128]{3,2,1,0:T(8,128)(2,1)S(1)} async-done(((bf16[16,2,16,128]{3,2,1,0:T(8,128)(2,1)}), bf16[16,2,16,128]{3,2,1,0:T(8,128)(2,1)S(1)}, u32[]{:S(2)}, u32[]{:S(2)}) %all-to-all-start) | async-done | bytes 131104 | tf_op jit(solution)/shard_map/all_to_all | solution.py:133
  20.3 2.0 %all_gather.18.row_seg_ref = bf16[64,16,128]{2,1,0:T(8,128)(2,1)S(1)} all-gather(bf16[32,16,128]{2,1,0:T(8,128)(2,1)S(1)} %bitcast.16), channel_id=1, replica_groups=mesh['row'=32,'near'=16,'core'=2] {'core'}, dimensions={0}, use_global_device_ids=true | all-gather | bytes 393216 | tf_op jit(solution)/shard_map/all_gather | solution.py:134
  22.3 0.0 copy-done
  22.3 1.6 %mirror_products.2 = bf16[32,4,16,128]{3,2,1,0:T(8,128)(2,1)S(1)} custom-call(s32[193]{0:T(256)S(1)} %get-tuple-element.15.places_ref, bf16[96,128,128]{2,1,0:T(8,128)(2,1)S(1)} %get-tuple-element.16.tiles_ref, bf16[64,16,128]{2,1,0:T(8,128)(2,1)S(1)} %all_gather.18.row_seg_ref, bf16[2,16,128]{2,1,0:T(8,128)(2,1)S(1)} %copy-done), custom_call_target="tpu_custom_call" | custom-call | flops 50331648 | bytes 3145728 | tf_op jit(solution)/shard_map/mirror_products/pallas_call | solution.py:108
  23.9 40.5 %all_to_all.30.packet_ref = bf16[32,4,16,128]{3,2,1,0:T(8,128)(2,1)S(1)} all-to-all(bf16[32,4,16,128]{3,2,1,0:T(8,128)(2,1)S(1)} %mirror_products.2), channel_id=1, replica_groups=mesh['row'=32,'near'=16,'core'=2] {'row'}, dimensions={0} | all-to-all | bytes 1048576 | tf_op jit(solution)/shard_map/all_to_all | solution.py:138
  64.4 2.4 %direct_products.2 = (f32[32,16,128]{2,1,0:T(8,128)S(1)}, bf16[32,16,128]{2,1,0:T(8,128)(2,1)S(1)}, f32[2,16,128]{2,1,0:T(8,128)S(1)}) custom-call(s32[193]{0:T(256)S(1)} %get-tuple-element.15.places_ref, bf16[96,128,128]{2,1,0:T(8,128)(2,1)S(1)} %get-tuple-element.16.tiles_ref, bf16[32,4,16,128]{3,2,1,0:T(8,128)(2,1)S(1)} %all_to_all.30.packet_ref), custom_call_target="tpu_custom_call" | custom-call | flops 50331648 | bytes 3145728 | tf_op jit(solution)/shard_map/direct_products/pallas_call | solution.py:108
  66.8 2.0 %all-gather = bf16[64,16,128]{2,1,0:T(8,128)(2,1)S(1)} all-gather(bf16[32,16,128]{2,1,0:T(8,128)(2,1)S(1)} %get-tuple-element.21), channel_id=2, replica_groups=mesh['row'=32,'near'=16,'core'=2] {'core'}, dimensions={0}, use_global_device_ids=true | all-gather | bytes 393216 | tf_op jit(solution)/shard_map/all_gather | solution.py:142
  68.8 11.9 %all_to_all.31.near_recv_ref = bf16[16,2,16,128]{3,2,1,0:T(8,128)(2,1)S(1)} all-to-all(bf16[16,2,16,128]{3,2,1,0:T(8,128)(2,1)S(1)} %bitcast.13), channel_id=1, replica_groups=mesh['row'=32,'near'=16,'core'=2] {'near'}, dimensions={0} | all-to-all | bytes 262144 | tf_op jit(solution)/shard_map/all_to_all | solution.py:144
  80.7 0.6 image.2
  81.3 11.8 %all_to_all.32 = bf16[16,2,16,128]{3,2,1,0:T(8,128)(2,1)S(1)} all-to-all(bf16[16,2,16,128]{3,2,1,0:T(8,128)(2,1)S(1)} %get-tuple-element.23), channel_id=1, replica_groups=mesh['row'=32,'near'=16,'core'=2] {'near'}, dimensions={0} | all-to-all | bytes 262144 | tf_op jit(solution)/shard_map/all_to_all | solution.py:133
  93.0 2.0 %all_gather.21.row_seg_ref = bf16[64,16,128]{2,1,0:T(8,128)(2,1)S(1)} all-gather(bf16[32,16,128]{2,1,0:T(8,128)(2,1)S(1)} %bitcast.17), channel_id=1, replica_groups=mesh['row'=32,'near'=16,'core'=2] {'core'}, dimensions={0}, use_global_device_ids=true | all-gather | bytes 393216 | tf_op jit(solution)/shard_map/all_gather | solution.py:134
  95.0 1.6 %mirror_products.3 = bf16[32,4,16,128]{3,2,1,0:T(8,128)(2,1)S(1)} custom-call(s32[193]{0:T(256)S(1)} %get-tuple-element.15.places_ref, bf16[96,128,128]{2,1,0:T(8,128)(2,1)S(1)} %get-tuple-element.16.tiles_ref, bf16[64,16,128]{2,1,0:T(8,128)(2,1)S(1)} %all_gather.21.row_seg_ref, bf16[2,16,128]{2,1,0:T(8,128)(2,1)S(1)} %get-tuple-element.24.own_ref), custom_call_target="tpu_custom_call" | custom-call | flops 50331648 | bytes 3145728 | tf_op jit(solution)/shard_map/mirror_products/pallas_call | solution.py:108
  96.6 24.6 %all_to_all.33.packet_ref = bf16[32,4,16,128]{3,2,1,0:T(8,128)(2,1)S(1)} all-to-all(bf16[32,4,16,128]{3,2,1,0:T(8,128)(2,1)S(1)} %mirror_products.3), channel_id=1, replica_groups=mesh['row'=32,'near'=16,'core'=2] {'row'}, dimensions={0} | all-to-all | bytes 1048576 | tf_op jit(solution)/shard_map/all_to_all | solution.py:138
  121.3 2.4 %direct_products.3 = (f32[32,16,128]{2,1,0:T(8,128)S(1)}, bf16[32,16,128]{2,1,0:T(8,128)(2,1)S(1)}, f32[2,16,128]{2,1,0:T(8,128)S(1)}) custom-call(s32[193]{0:T(256)S(1)} %get-tuple-element.15.places_ref, bf16[96,128,128]{2,1,0:T(8,128)(2,1)S(1)} %get-tuple-element.16.tiles_ref, bf16[32,4,16,128]{3,2,1,0:T(8,128)(2,1)S(1)} %all_to_all.33.packet_ref), custom_call_target="tpu_custom_call" | custom-call | flops 50331648 | bytes 3145728 | tf_op jit(solution)/shard_map/direct_products/pallas_call | solution.py:108
  123.6 2.0 %all-gather.1 = bf16[64,16,128]{2,1,0:T(8,128)(2,1)S(1)} all-gather(bf16[32,16,128]{2,1,0:T(8,128)(2,1)S(1)} %get-tuple-element.27), channel_id=3, replica_groups=mesh['row'=32,'near'=16,'core'=2] {'core'}, dimensions={0}, use_global_device_ids=true | all-gather | bytes 393216 | tf_op jit(solution)/shard_map/all_gather | solution.py:142
  125.7 11.8 %all_to_all.34.near_recv_ref = bf16[16,2,16,128]{3,2,1,0:T(8,128)(2,1)S(1)} all-to-all(bf16[16,2,16,128]{3,2,1,0:T(8,128)(2,1)S(1)} %bitcast.14), channel_id=1, replica_groups=mesh['row'=32,'near'=16,'core'=2] {'near'}, dimensions={0} | all-to-all | bytes 262144 | tf_op jit(solution)/shard_map/all_to_all | solution.py:144
  137.4 0.6 image.3
  (2 shorter events, 0.1 us)
Async XLA Ops:
  2.0 20.3 %copy-start = (bf16[2,16,128]{2,1,0:T(8,128)(2,1)S(1)}, bf16[2,16,128]{2,1,0:T(8,128)(2,1)}, u32[]{:S(2)}) copy-start(bf16[2,16,128]{2,1,0:T(8,128)(2,1)} %get-tuple-element.18.own_ref) | copy-start | bytes 24580
  2.0 18.3 %all-to-all-start = ((bf16[16,2,16,128]{3,2,1,0:T(8,128)(2,1)}), bf16[16,2,16,128]{3,2,1,0:T(8,128)(2,1)S(1)}, u32[]{:S(2)}, u32[]{:S(2)}) async-start(bf16[16,2,16,128]{3,2,1,0:T(8,128)(2,1)} %get-tuple-element.17), calls=%async_computation | async-start | bytes 262144 | tf_op jit(solution)/shard_map/all_to_all | solution.py:133

commit v10 on v9

--- a/solution.py
+++ b/solution.py
@@ -7,6 +7,7 @@
 from jax.sharding import PartitionSpec as P
 
 UNROLL = 96
+LAG = 16
 TILE_COPIES = 4
 F32 = jnp.float32
 BF16 = jnp.bfloat16
@@ -41,6 +42,11 @@
         copy.wait()
 
 
+def add(acc, result):
+    where, product = result
+    acc[where] += product
+
+
 def mirror_kernel(places_ref, tiles_ref, row_seg_ref, own_ref, packet_ref, acc):
     slots, parts, peers = tiles_ref.shape[0], own_ref.shape[0], packet_ref.shape[0]
     half = row_seg_ref.shape[0] // CORES
@@ -54,8 +60,10 @@
             core, place = by_core(places_ref[n] & (CORES * half - 1), parts)
             product = lax.dot_general(row_seg_ref[core * half + place], tiles_ref[n], (((1,), (0,)), ((), ())), preferred_element_type=F32)
             results.append((jnp.where(n < count, places_ref[slots + n], spare), product))
-        for c, product in results:
-            acc[c] += product
+            if u >= LAG:
+                add(acc, results.pop(0))
+        for result in results:
+            add(acc, result)
         return 0
 
     lax.fori_loop(0, slots // UNROLL, block, 0)
@@ -77,8 +85,10 @@
             product = lax.dot_general(picked, tiles_ref[n], (((1,), (1,)), ((), ())), preferred_element_type=F32)
             core, place = by_core(places_ref[n], parts)
             results.append((jnp.where(n < count, (core ^ mine) * half + place, spare), product))
-        for r, product in results:
-            acc[r] += product
+            if u >= LAG:
+                add(acc, results.pop(0))
+        for result in results:
+            add(acc, result)
         return 0
 
     lax.fori_loop(0, slots // UNROLL, block, 0)

time: 139 us -> 139 us (level)
  no operation moved by 1% of the time
where the time goes in v10:
time: 139 us; the launch traced here: 138 us
  blocking collectives  109 us (78%)
  Pallas kernels  12.4 us (9%)
  starting transfers between devices  9.71 us (7%)
  waiting for transfers between devices  5.29 us (4%)
    all_to_all x2, blocking collectives, image(): packet = lax.all_to_all(packet, ROW, 0, 0)  65.3 us
    all_to_all x2, blocking collectives, image(): near_recv = lax.all_to_all(chip.reshape((near,) + piece), NEAR, 0, 0)  23.5 us
    pallas_call x10, Pallas kernels, call(): pl.pallas_call(kernel, out_shape=tuple((jax.ShapeDtypeStruct(s, d) for s,...  12.4 us
    all_to_all x1, blocking collectives, image(): near_recv = lax.all_to_all(near_copies, NEAR, 0, 0)  11.8 us
    all_to_all x1, starting transfers between devices, image(): near_recv = lax.all_to_all(near_copies, NEAR, 0, 0)  9.71 us
    all_to_all x1, waiting for transfers between devices, image(): near_recv = lax.all_to_all(near_copies, NEAR, 0, 0)  5.29 us
    all_gather x2, blocking collectives, image(): recv = lax.all_gather(send, CORE, axis=0)  3.99 us
    all_gather x2, blocking collectives, image(): row_seg = lax.all_gather(near_recv.reshape(half), CORE, axis=0, tiled=True)  3.96 us
  transfers between devices with their start and end apart: 1, of which 1 were waited for; matrix products, arithmetic and copies ran while one was open for 1% of the time, Pallas kernels for 1%

profile of v10, /device:TPU:16, one launch (start us, length us, event | category | flops | bytes accessed | tf_op | source)
XLA Modules:
  0.0 138.0 jit_solution(13568956266421913882)
XLA Ops:
  0.6 1.4 start.1
  2.0 0.0 copy-start
  2.0 9.7 %all-to-all-start = ((bf16[16,2,16,128]{3,2,1,0:T(8,128)(2,1)}), bf16[16,2,16,128]{3,2,1,0:T(8,128)(2,1)S(1)}, u32[]{:S(2)}, u32[]{:S(2)}) async-start(bf16[16,2,16,128]{3,2,1,0:T(8,128)(2,1)} %get-tuple-element.17), calls=%async_computation | async-start | bytes 262144 | tf_op jit(solution)/shard_map/all_to_all | solution.py:143
  12.4 0.7 pad_add_fusion.places_ref
  13.1 1.9 %load.1 = (s32[193]{0:T(256)S(1)}, bf16[96,128,128]{2,1,0:T(8,128)(2,1)S(1)}) custom-call(bf16[96,128,128]{2,1,0:T(8,128)(2,1)} %bitcast.15, s32[193]{0:T(256)S(1)} %pad_add_fusion.places_ref), custom_call_target="tpu_custom_call" | custom-call | flops 4096 | bytes 6291456 | tf_op jit(solution)/shard_map/load/pallas_call | solution.py:118
  15.0 5.3 %all-to-all-done = bf16[16,2,16,128]{3,2,1,0:T(8,128)(2,1)S(1)} async-done(((bf16[16,2,16,128]{3,2,1,0:T(8,128)(2,1)}), bf16[16,2,16,128]{3,2,1,0:T(8,128)(2,1)S(1)}, u32[]{:S(2)}, u32[]{:S(2)}) %all-to-all-start) | async-done | bytes 131104 | tf_op jit(solution)/shard_map/all_to_all | solution.py:143
  20.3 2.0 %all_gather.18.row_seg_ref = bf16[64,16,128]{2,1,0:T(8,128)(2,1)S(1)} all-gather(bf16[32,16,128]{2,1,0:T(8,128)(2,1)S(1)} %bitcast.16), channel_id=1, replica_groups=mesh['row'=32,'near'=16,'core'=2] {'core'}, dimensions={0}, use_global_device_ids=true | all-gather | bytes 393216 | tf_op jit(solution)/shard_map/all_gather | solution.py:144
  22.3 0.0 copy-done
  22.3 1.6 %mirror_products.2 = bf16[32,4,16,128]{3,2,1,0:T(8,128)(2,1)S(1)} custom-call(s32[193]{0:T(256)S(1)} %get-tuple-element.15.places_ref, bf16[96,128,128]{2,1,0:T(8,128)(2,1)S(1)} %get-tuple-element.16.tiles_ref, bf16[64,16,128]{2,1,0:T(8,128)(2,1)S(1)} %all_gather.18.row_seg_ref, bf16[2,16,128]{2,1,0:T(8,128)(2,1)S(1)} %copy-done), custom_call_target="tpu_custom_call" | custom-call | flops 50331648 | bytes 3145728 | tf_op jit(solution)/shard_map/mirror_products/pallas_call | solution.py:118
  23.9 40.6 %all_to_all.30.packet_ref = bf16[32,4,16,128]{3,2,1,0:T(8,128)(2,1)S(1)} all-to-all(bf16[32,4,16,128]{3,2,1,0:T(8,128)(2,1)S(1)} %mirror_products.2), channel_id=1, replica_groups=mesh['row'=32,'near'=16,'core'=2] {'row'}, dimensions={0} | all-to-all | bytes 1048576 | tf_op jit(solution)/shard_map/all_to_all | solution.py:148
  64.5 2.4 %direct_products.2 = (f32[32,16,128]{2,1,0:T(8,128)S(1)}, bf16[32,16,128]{2,1,0:T(8,128)(2,1)S(1)}, f32[2,16,128]{2,1,0:T(8,128)S(1)}) custom-call(s32[193]{0:T(256)S(1)} %get-tuple-element.15.places_ref, bf16[96,128,128]{2,1,0:T(8,128)(2,1)S(1)} %get-tuple-element.16.tiles_ref, bf16[32,4,16,128]{3,2,1,0:T(8,128)(2,1)S(1)} %all_to_all.30.packet_ref), custom_call_target="tpu_custom_call" | custom-call | flops 50331648 | bytes 3145728 | tf_op jit(solution)/shard_map/direct_products/pallas_call | solution.py:118
  66.8 2.0 %all-gather = bf16[64,16,128]{2,1,0:T(8,128)(2,1)S(1)} all-gather(bf16[32,16,128]{2,1,0:T(8,128)(2,1)S(1)} %get-tuple-element.21), channel_id=2, replica_groups=mesh['row'=32,'near'=16,'core'=2] {'core'}, dimensions={0}, use_global_device_ids=true | all-gather | bytes 393216 | tf_op jit(solution)/shard_map/all_gather | solution.py:152
  68.9 11.8 %all_to_all.31.near_recv_ref = bf16[16,2,16,128]{3,2,1,0:T(8,128)(2,1)S(1)} all-to-all(bf16[16,2,16,128]{3,2,1,0:T(8,128)(2,1)S(1)} %bitcast.13), channel_id=1, replica_groups=mesh['row'=32,'near'=16,'core'=2] {'near'}, dimensions={0} | all-to-all | bytes 262144 | tf_op jit(solution)/shard_map/all_to_all | solution.py:154
  80.6 0.6 image.2
  81.3 11.8 %all_to_all.32 = bf16[16,2,16,128]{3,2,1,0:T(8,128)(2,1)S(1)} all-to-all(bf16[16,2,16,128]{3,2,1,0:T(8,128)(2,1)S(1)} %get-tuple-element.23), channel_id=1, replica_groups=mesh['row'=32,'near'=16,'core'=2] {'near'}, dimensions={0} | all-to-all | bytes 262144 | tf_op jit(solution)/shard_map/all_to_all | solution.py:143
  93.0 2.0 %all_gather.21.row_seg_ref = bf16[64,16,128]{2,1,0:T(8,128)(2,1)S(1)} all-gather(bf16[32,16,128]{2,1,0:T(8,128)(2,1)S(1)} %bitcast.17), channel_id=1, replica_groups=mesh['row'=32,'near'=16,'core'=2] {'core'}, dimensions={0}, use_global_device_ids=true | all-gather | bytes 393216 | tf_op jit(solution)/shard_map/all_gather | solution.py:144
  95.0 1.6 %mirror_products.3 = bf16[32,4,16,128]{3,2,1,0:T(8,128)(2,1)S(1)} custom-call(s32[193]{0:T(256)S(1)} %get-tuple-element.15.places_ref, bf16[96,128,128]{2,1,0:T(8,128)(2,1)S(1)} %get-tuple-element.16.tiles_ref, bf16[64,16,128]{2,1,0:T(8,128)(2,1)S(1)} %all_gather.21.row_seg_ref, bf16[2,16,128]{2,1,0:T(8,128)(2,1)S(1)} %get-tuple-element.24.own_ref), custom_call_target="tpu_custom_call" | custom-call | flops 50331648 | bytes 3145728 | tf_op jit(solution)/shard_map/mirror_products/pallas_call | solution.py:118
  96.6 24.7 %all_to_all.33.packet_ref = bf16[32,4,16,128]{3,2,1,0:T(8,128)(2,1)S(1)} all-to-all(bf16[32,4,16,128]{3,2,1,0:T(8,128)(2,1)S(1)} %mirror_products.3), channel_id=1, replica_groups=mesh['row'=32,'near'=16,'core'=2] {'row'}, dimensions={0} | all-to-all | bytes 1048576 | tf_op jit(solution)/shard_map/all_to_all | solution.py:148
  121.2 2.4 %direct_products.3 = (f32[32,16,128]{2,1,0:T(8,128)S(1)}, bf16[32,16,128]{2,1,0:T(8,128)(2,1)S(1)}, f32[2,16,128]{2,1,0:T(8,128)S(1)}) custom-call(s32[193]{0:T(256)S(1)} %get-tuple-element.15.places_ref, bf16[96,128,128]{2,1,0:T(8,128)(2,1)S(1)} %get-tuple-element.16.tiles_ref, bf16[32,4,16,128]{3,2,1,0:T(8,128)(2,1)S(1)} %all_to_all.33.packet_ref), custom_call_target="tpu_custom_call" | custom-call | flops 50331648 | bytes 3145728 | tf_op jit(solution)/shard_map/direct_products/pallas_call | solution.py:118
  123.6 2.0 %all-gather.1 = bf16[64,16,128]{2,1,0:T(8,128)(2,1)S(1)} all-gather(bf16[32,16,128]{2,1,0:T(8,128)(2,1)S(1)} %get-tuple-element.27), channel_id=3, replica_groups=mesh['row'=32,'near'=16,'core'=2] {'core'}, dimensions={0}, use_global_device_ids=true | all-gather | bytes 393216 | tf_op jit(solution)/shard_map/all_gather | solution.py:152
  125.6 11.8 %all_to_all.34.near_recv_ref = bf16[16,2,16,128]{3,2,1,0:T(8,128)(2,1)S(1)} all-to-all(bf16[16,2,16,128]{3,2,1,0:T(8,128)(2,1)S(1)} %bitcast.14), channel_id=1, replica_groups=mesh['row'=32,'near'=16,'core'=2] {'near'}, dimensions={0} | all-to-all | bytes 262144 | tf_op jit(solution)/shard_map/all_to_all | solution.py:154
  137.4 0.6 image.3
  (2 shorter events, 0.1 us)
Async XLA Ops:
  2.0 20.3 %copy-start = (bf16[2,16,128]{2,1,0:T(8,128)(2,1)S(1)}, bf16[2,16,128]{2,1,0:T(8,128)(2,1)}, u32[]{:S(2)}) copy-start(bf16[2,16,128]{2,1,0:T(8,128)(2,1)} %get-tuple-element.18.own_ref) | copy-start | bytes 24580
  2.0 18.3 %all-to-all-start = ((bf16[16,2,16,128]{3,2,1,0:T(8,128)(2,1)}), bf16[16,2,16,128]{3,2,1,0:T(8,128)(2,1)S(1)}, u32[]{:S(2)}, u32[]{:S(2)}) async-start(bf16[16,2,16,128]{3,2,1,0:T(8,128)(2,1)} %get-tuple-element.17), calls=%async_computation | async-start | bytes 262144 | tf_op jit(solution)/shard_map/all_to_all | solution.py:143
